TPU v7x, 256 devices: a whole 4x4x8 slice. The times are simulated.
256 devices in a mesh: dp: 64 (over y, z, core), tensor: 4 (over x).
Axes of the slice: x: 4, y: 4, z: 8, core: 2. Of those that a mesh axis runs over, the one named last changes fastest.
Arguments:
- queries: bfloat16 [2, 512, 8192], P(None, 'dp', 'tensor'), may hold values from -60 to 60
- key_cache: bfloat16 [512, 8, 512, 128], P('dp', 'tensor'), may hold values from -6 to 6
- value_cache: bfloat16 [512, 8, 512, 128], P('dp', 'tensor'), may hold values from -6 to 6
- new_keys: bfloat16 [2, 512, 1024], P(None, 'dp', 'tensor'), may hold values from -8 to 8
- new_values: bfloat16 [2, 512, 1024], P(None, 'dp', 'tensor'), may hold values from -6 to 6
- lengths: int32 [512], P('dp'), may hold values from 64 to 512, as said below
- ancestors: int32 [2, 512], replicated, may hold values from 0 to 511, as said below
- out_weight: bfloat16 [8192, 8192], P('tensor', 'dp'), may hold values from -0.25 to 0.25
Outputs:
- mixed: bfloat16 [2, 512, 8192], P(None, 'tensor', 'dp')
Inputs may be any that keep to these rules, and one draw needn't show every extreme that they name: `lengths`: every particle has at least 64 filled slots, and some particle has exactly 512. Each ancestor is a particle of the same prompt: ancestors[r, p] // 32 == p // 32.
All inputs are finite; a program needn't handle non-finite values.
Results may differ from a plain program's by a relative error of at most 0.008.
Values may be sent and summed in bfloat16 or wider, within the bound.
No kernel may reach another device: no remote copies, remote signals or barrier semaphores. Data moves between devices by JAX's collectives and lax.ppermute only.
A program may use at most 64 MiB of HBM per device.

v0:
```python
import math

import jax
import jax.numpy as jnp
from jax import lax
from jax.sharding import PartitionSpec as P

FAMILY = 32


NEGATIVE = -1e30


def from_behind(value, axis, steps):
    count = lax.axis_size(axis)
    first, last = (max(0, -steps), min(count, count - steps))
    return lax.ppermute(value, axis, [(source, source + steps) for source in range(first, last)])


def combine_parts(first, second):
    first_top, first_sum, first_mix = first
    second_top, second_sum, second_mix = second
    summit = jnp.maximum(first_top, second_top)
    first_factor = jnp.exp(first_top - summit)
    second_factor = jnp.exp(second_top - summit)
    totals = first_sum * first_factor + second_sum * second_factor
    mixture = first_mix * first_factor[..., None] + second_mix * second_factor[..., None]
    return (summit, totals, mixture)


def select_parts(marked, chosen, kept):
    summit = jnp.where(marked, chosen[0], kept[0])
    totals = jnp.where(marked, chosen[1], kept[1])
    mixture = jnp.where(jnp.expand_dims(marked, -1), chosen[2], kept[2])
    return (summit, totals, mixture)


def attend_local(queries_block, item_ids, round_batch, allowed, tables):
    key_cache, value_cache, new_keys, new_values, lengths, roots, ancestors, own_index = tables
    count_rounds, item_count, feature_width = queries_block.shape
    holders, kv_local, cache_len, head_dim = key_cache.shape
    per_group = feature_width // head_dim // kv_local
    factor = 1.0 / math.sqrt(head_dim)
    grouped = queries_block.reshape(count_rounds, item_count, kv_local, per_group, head_dim)
    safe_ids = jnp.clip(item_ids, 0, roots.shape[1] - 1)
    item_roots = jnp.stack([jnp.take(roots[round_index], safe_ids) for round_index in round_batch])
    offsets = item_roots - own_index * holders
    places = jnp.arange(cache_len)
    part_shape = (count_rounds, item_count, kv_local, per_group)
    carried = (
        jnp.full(part_shape, NEGATIVE, jnp.float32),
        jnp.zeros(part_shape, jnp.float32),
        jnp.zeros(part_shape + (head_dim,), jnp.float32),
    )
    for holder in range(holders):
        scores = (
            jnp.einsum(
                "rngqd,gtd->rngqt", grouped, key_cache[holder], preferred_element_type=jnp.float32
            )
            * factor
        )
        inside = places < lengths[holder]
        summit = jnp.max(jnp.where(inside, scores, -jnp.inf), axis=-1)
        weights = jnp.where(inside, jnp.exp(scores - summit[..., None]), 0.0).astype(jnp.bfloat16)
        totals = jnp.sum(weights, axis=-1, dtype=jnp.float32)
        mixture = jnp.einsum(
            "rngqt,gtd->rngqd", weights, value_cache[holder], preferred_element_type=jnp.float32
        )
        marked = jnp.logical_and(offsets == holder, allowed)[:, :, None, None]
        carried = select_parts(marked, (summit, totals, mixture), carried)
    result_rows = []
    for position, round_index in enumerate(round_batch):
        current = tuple((member[position] for member in carried))
        if round_index >= 1:
            parents = jnp.take(ancestors[round_index], safe_ids) - own_index * holders
            present = jnp.logical_and(jnp.logical_and(parents >= 0, parents < holders), allowed)
            picked = jnp.clip(parents, 0, holders - 1)
            parent_keys = jnp.take(new_keys[round_index - 1], picked, axis=0).reshape(
                item_count, kv_local, head_dim
            )
            parent_values = (
                jnp.take(new_values[round_index - 1], picked, axis=0)
                .reshape(item_count, kv_local, 1, head_dim)
                .astype(jnp.float32)
            )
            parent_scores = (
                jnp.einsum(
                    "ngqd,ngd->ngq",
                    grouped[position],
                    parent_keys,
                    preferred_element_type=jnp.float32,
                )
                * factor
            )
            single_token = (
                parent_scores,
                jnp.ones_like(parent_scores),
                jnp.broadcast_to(parent_values, parent_scores.shape + (head_dim,)),
            )
            current = select_parts(
                present[:, None, None], combine_parts(current, single_token), current
            )
        result_rows.append(current)
    return tuple((jnp.stack([entry[member] for entry in result_rows]) for member in range(3)))


def per_device(
    queries, key_cache, value_cache, new_keys, new_values, lengths, ancestors, out_weight
):
    count_rounds, holders, feature_width = queries.shape
    kv_local = key_cache.shape[1]
    head_dim = key_cache.shape[3]
    per_group = feature_width // head_dim // kv_local
    factor = 1.0 / math.sqrt(head_dim)
    group_size = FAMILY // holders
    own_index = lax.axis_index("dp")
    lineage = []
    for round_index in range(count_rounds):
        stepped = ancestors[round_index]
        lineage.append(stepped if round_index == 0 else jnp.take(lineage[-1], stepped))
    roots = jnp.stack(lineage)
    tables = (key_cache, value_cache, new_keys, new_values, lengths, roots, ancestors, own_index)
    own_ids = own_index * holders + jnp.arange(holders)
    batches = [[round_index] for round_index in range(count_rounds)]
    outputs = []
    for round_batch in batches:
        batch_rounds = len(round_batch)
        queries_block = queries[round_batch[0] : round_batch[-1] + 1]
        carried = attend_local(queries_block, own_ids, round_batch, True, tables)
        distances = list(range(1 - group_size, 0)) + list(range(1, group_size))
        for distance in distances:
            source = own_index - distance
            arrived = from_behind(queries_block, "dp", distance)
            same_group = source // group_size == own_index // group_size
            answered = attend_local(
                arrived, source * holders + jnp.arange(holders), round_batch, same_group, tables
            )
            returned = from_behind(answered, "dp", -distance)
            usable = (own_index + distance) // group_size == own_index // group_size
            carried = select_parts(usable, combine_parts(carried, returned), carried)
        grouped = queries_block.reshape(batch_rounds, holders, kv_local, per_group, head_dim)
        own_keys = new_keys[round_batch[0] : round_batch[-1] + 1].reshape(
            batch_rounds, holders, kv_local, head_dim
        )
        own_values = (
            new_values[round_batch[0] : round_batch[-1] + 1]
            .reshape(batch_rounds, holders, kv_local, 1, head_dim)
            .astype(jnp.float32)
        )
        own_scores = (
            jnp.einsum("rngqd,rngd->rngq", grouped, own_keys, preferred_element_type=jnp.float32)
            * factor
        )
        single_token = (
            own_scores,
            jnp.ones_like(own_scores),
            jnp.broadcast_to(own_values, own_scores.shape + (head_dim,)),
        )
        summit, totals, mixture = combine_parts(carried, single_token)
        attention = (
            (mixture / totals[..., None])
            .astype(jnp.bfloat16)
            .reshape(batch_rounds, holders, feature_width)
        )
        outputs.append(attention)
    attention = jnp.concatenate(outputs, 0)
    terms = jnp.einsum(
        "rpk,kc->rpc",
        lax.all_gather(attention, "dp", axis=1, tiled=True),
        out_weight,
        preferred_element_type=jnp.float32,
    )
    return lax.psum_scatter(terms, "tensor", scatter_dimension=1, tiled=True).astype(jnp.bfloat16)


def solution(mesh):
    in_specs = (
        P(None, "dp", "tensor"),
        P("dp", "tensor", None, None),
        P("dp", "tensor", None, None),
        P(None, "dp", "tensor"),
        P(None, "dp", "tensor"),
        P("dp"),
        P(),
        P("tensor", "dp"),
    )
    out_specs = P(None, "tensor", "dp")
    return jax.shard_map(
        per_device, mesh=mesh, in_specs=in_specs, out_specs=out_specs, check_vma=False
    )
```

profile of v0, /device:TPU:6, one launch (start us, length us, event | category | flops | bytes accessed | tf_op | source)
XLA Modules:
  0.0 428.9 jit_solution(9129714572119240775)
XLA Ops:
  7.4 3.8 collective-permute-start.36
  15.3 7.2 %collective-permute-start.15 = (bf16[1,8,2048]{2,1,0:T(8,128)(2,1)S(1)}, bf16[1,8,2048]{2,1,0:T(8,128)(2,1)S(1)}, u32[]{:S(2)}, u32[]{:S(2)}) collective-permute-start(bf16[1,8,2048]{2,1,0:T(8,128)(2,1)S(1)} %get-tuple-element.334), channel_id=1, source_target_pairs={{0,12},{4,16},{8,20},{12,24},{16,28},{20,32},{24,36},{28,40},{32,4... | collective-permute-start | bytes 98312 | tf_op jit(solution)/shard_map/ppermute | solution.py:17
  24.0 3.5 gather_fusion
  61.5 3.9 collective-permute-done.3
  68.7 4.5 %collective-permute-start.9 = (bf16[1,8,2048]{2,1,0:T(8,128)(2,1)S(1)}, bf16[1,8,2048]{2,1,0:T(8,128)(2,1)S(1)}, u32[]{:S(2)}, u32[]{:S(2)}) collective-permute-start(bf16[1,8,2048]{2,1,0:T(8,128)(2,1)S(1)} %get-tuple-element.334), channel_id=1, source_target_pairs={{0,4},{4,8},{8,12},{12,16},{16,20},{20,24},{24,28},{28,32},{32,36}... | collective-permute-start | bytes 98312 | tf_op jit(solution)/shard_map/ppermute | solution.py:17
  75.0 5.1 %collective-permute-start.12 = (bf16[1,8,2048]{2,1,0:T(8,128)(2,1)S(1)}, bf16[1,8,2048]{2,1,0:T(8,128)(2,1)S(1)}, u32[]{:S(2)}, u32[]{:S(2)}) collective-permute-start(bf16[1,8,2048]{2,1,0:T(8,128)(2,1)S(1)} %get-tuple-element.334), channel_id=1, source_target_pairs={{0,8},{4,12},{8,16},{12,20},{16,24},{20,28},{24,32},{28,36},{32,40... | collective-permute-start | bytes 98312 | tf_op jit(solution)/shard_map/ppermute | solution.py:17
  81.9 3.1 collective-permute-start.39
  89.8 6.4 %collective-permute-done.24 = bf16[1,8,2048]{2,1,0:T(8,128)(2,1)S(1)} collective-permute-done((bf16[1,8,2048]{2,1,0:T(8,128)(2,1)S(1)}, bf16[1,8,2048]{2,1,0:T(8,128)(2,1)S(1)}, u32[]{:S(2)}, u32[]{:S(2)}) %collective-permute-start.24) | collective-permute-done | bytes 32800 | tf_op jit(solution)/shard_map/ppermute | solution.py:17
  121.1 12.9 %fusion.150 = f32[2,128,1,8,8]{1,4,3,0,2:T(8,128)S(1)} fusion(f32[2,128,1,8,8]{1,4,3,0,2:T(8,128)S(1)} %fusion.151, pred[8]{0:T(512)(128)(4,1)S(1)} %get-tuple-element.387, f32[1,8,2,8,512]{4,3,1,2,0:T(8,128)S(1)} %fusion.78, f32[8,2,8]{2,0,1:T(8,128)S(1)} %get-tuple-element.192, pred[512]{0:T(512)(128)(4,1)S(1)} %iota_compare_fusion.6, ...), kind=kOutput, calls=%fused_computation.410 | convolution fusion | flops 16990208 | bytes 664576 | tf_op jit(solution)/shard_map/rngqt,gtd->rngqd/dot_general | solution.py:66
  147.8 6.1 %collective-permute-start.19 = (f32[1,8,2,8]{3,1,2,0:T(8,128)S(1)}, f32[1,8,2,8]{3,1,2,0:T(8,128)S(1)}, u32[]{:S(2)}, u32[]{:S(2)}) collective-permute-start(f32[1,8,2,8]{3,1,2,0:T(8,128)S(1)} %fusion.692), channel_id=1, source_target_pairs={{0,8},{4,12},{8,16},{12,20},{16,24},{20,28},{24,32},{28,36},{32,40... | collective-permute-start | bytes 1544 | tf_op jit(solution)/shard_map/ppermute | solution.py:17
  153.9 7.1 %collective-permute-start.1 = (f32[1,8,2,8]{3,1,2,0:T(8,128)S(1)}, f32[1,8,2,8]{3,1,2,0:T(8,128)S(1)}, u32[]{:S(2)}, u32[]{:S(2)}) collective-permute-start(f32[1,8,2,8]{3,1,2,0:T(8,128)S(1)} %fusion.748), channel_id=1, source_target_pairs={{0,12},{4,16},{8,20},{12,24},{16,28},{20,32},{24,36},{28,40},{32,4... | collective-permute-start | bytes 1544 | tf_op jit(solution)/shard_map/ppermute | solution.py:17
  180.8 5.1 %collective-permute-start.4 = (f32[1,8,2,8]{3,1,2,0:T(8,128)S(1)}, f32[1,8,2,8]{3,1,2,0:T(8,128)S(1)}, u32[]{:S(2)}, u32[]{:S(2)}) collective-permute-start(f32[1,8,2,8]{3,1,2,0:T(8,128)S(1)} %fusion.741), channel_id=1, source_target_pairs={{0,8},{4,12},{8,16},{12,20},{16,24},{20,28},{24,32},{28,36},{32,40... | collective-permute-start | bytes 1544 | tf_op jit(solution)/shard_map/ppermute | solution.py:17
  190.7 4.2 collective-permute-done.10
  196.5 5.1 %collective-permute-done.13 = f32[1,8,2,8]{3,1,2,0:T(8,128)S(1)} collective-permute-done((f32[1,8,2,8]{3,1,2,0:T(8,128)S(1)}, f32[1,8,2,8]{3,1,2,0:T(8,128)S(1)}, u32[]{:S(2)}, u32[]{:S(2)}) %collective-permute-start.13) | collective-permute-done | bytes 544 | tf_op jit(solution)/shard_map/ppermute | solution.py:17
  202.9 3.9 collective-permute-done.16
  206.8 6.6 %collective-permute-start.18 = (f32[1,8,2,8]{3,1,2,0:T(8,128)S(1)}, f32[1,8,2,8]{3,1,2,0:T(8,128)S(1)}, u32[]{:S(2)}, u32[]{:S(2)}) collective-permute-start(f32[1,8,2,8]{3,1,2,0:T(8,128)S(1)} %fusion.699), channel_id=1, source_target_pairs={{0,12},{4,16},{8,20},{12,24},{16,28},{20,32},{24,36},{28,40},{32,4... | collective-permute-start | bytes 1544 | tf_op jit(solution)/shard_map/ppermute | solution.py:17
  220.0 8.0 %collective-permute-start.25 = (f32[1,8,2,8]{3,1,2,0:T(8,128)S(1)}, f32[1,8,2,8]{3,1,2,0:T(8,128)S(1)}, u32[]{:S(2)}, u32[]{:S(2)}) collective-permute-start(f32[1,8,2,8]{3,1,2,0:T(8,128)S(1)} %get-tuple-element.281), channel_id=1, source_target_pairs={{0,12},{4,16},{8,20},{12,24},{16,28},{20,32},{24,36},{28,40},{32,4... | collective-permute-start | bytes 1544 | tf_op jit(solution)/shard_map/ppermute | solution.py:17
  229.3 4.2 collective-permute-start.28
  234.9 3.2 collective-permute-start.31
  240.2 3.8 collective-permute-done.34
  245.4 5.5 %collective-permute-start.44 = (f32[1,8,2,8]{3,1,2,0:T(8,128)S(1)}, f32[1,8,2,8]{3,1,2,0:T(8,128)S(1)}, u32[]{:S(2)}, u32[]{:S(2)}) collective-permute-start(f32[1,8,2,8]{3,1,2,0:T(8,128)S(1)} %get-tuple-element.295), channel_id=1, source_target_pairs={{0,4},{4,8},{8,12},{12,16},{16,20},{20,24},{24,28},{28,32},{32,36}... | collective-permute-start | bytes 1544 | tf_op jit(solution)/shard_map/ppermute | solution.py:17
  250.9 4.2 collective-permute-start.43
  255.1 7.1 %collective-permute-start.42 = (f32[1,8,2,8]{3,1,2,0:T(8,128)S(1)}, f32[1,8,2,8]{3,1,2,0:T(8,128)S(1)}, u32[]{:S(2)}, u32[]{:S(2)}) collective-permute-start(f32[1,8,2,8]{3,1,2,0:T(8,128)S(1)} %get-tuple-element.289), channel_id=1, source_target_pairs={{0,12},{4,16},{8,20},{12,24},{16,28},{20,32},{24,36},{28,40},{32,4... | collective-permute-start | bytes 1544 | tf_op jit(solution)/shard_map/ppermute | solution.py:17
  266.2 5.7 %collective-permute-start.32 = (f32[1,8,2,8,128]{4,3,1,2,0:T(8,128)S(1)}, f32[1,8,2,8,128]{4,3,1,2,0:T(8,128)S(1)}, u32[]{:S(2)}, u32[]{:S(2)}) collective-permute-start(f32[1,8,2,8,128]{4,3,1,2,0:T(8,128)S(1)} %add_select_fusion.3), channel_id=1, source_target_pairs={{0,4},{4,8},{8,12},{12,16},{16,20},{20,24},{24,28},{28,32},{32,36}... | collective-permute-start | bytes 196616 | tf_op jit(solution)/shard_map/ppermute | solution.py:17
  271.9 6.0 %collective-permute-start.29 = (f32[1,8,2,8,128]{4,3,1,2,0:T(8,128)S(1)}, f32[1,8,2,8,128]{4,3,1,2,0:T(8,128)S(1)}, u32[]{:S(2)}, u32[]{:S(2)}) collective-permute-start(f32[1,8,2,8,128]{4,3,1,2,0:T(8,128)S(1)} %add_select_fusion.4), channel_id=1, source_target_pairs={{0,8},{4,12},{8,16},{12,20},{16,24},{20,28},{24,32},{28,36},{32,40... | collective-permute-start | bytes 196616 | tf_op jit(solution)/shard_map/ppermute | solution.py:17
  278.1 5.0 %collective-permute-start.26 = (f32[1,8,2,8,128]{4,3,1,2,0:T(8,128)S(1)}, f32[1,8,2,8,128]{4,3,1,2,0:T(8,128)S(1)}, u32[]{:S(2)}, u32[]{:S(2)}) collective-permute-start(f32[1,8,2,8,128]{4,3,1,2,0:T(8,128)S(1)} %add_select_fusion.5), channel_id=1, source_target_pairs={{0,12},{4,16},{8,20},{12,24},{16,28},{20,32},{24,36},{28,40},{32,4... | collective-permute-start | bytes 196616 | tf_op jit(solution)/shard_map/ppermute | solution.py:17
  285.8 5.5 %collective-permute-start.5 = (f32[1,8,2,8,128]{4,3,1,2,0:T(8,128)S(1)}, f32[1,8,2,8,128]{4,3,1,2,0:T(8,128)S(1)}, u32[]{:S(2)}, u32[]{:S(2)}) collective-permute-start(f32[1,8,2,8,128]{4,3,1,2,0:T(8,128)S(1)} %fusion.131), channel_id=1, source_target_pairs={{0,8},{4,12},{8,16},{12,20},{16,24},{20,28},{24,32},{28,36},{32,40... | collective-permute-start | bytes 196616 | tf_op jit(solution)/shard_map/ppermute | solution.py:17
  291.3 5.9 %collective-permute-start.8 = (f32[1,8,2,8,128]{4,3,1,2,0:T(8,128)S(1)}, f32[1,8,2,8,128]{4,3,1,2,0:T(8,128)S(1)}, u32[]{:S(2)}, u32[]{:S(2)}) collective-permute-start(f32[1,8,2,8,128]{4,3,1,2,0:T(8,128)S(1)} %fusion.140), channel_id=1, source_target_pairs={{0,4},{4,8},{8,12},{12,16},{16,20},{20,24},{24,28},{28,32},{32,36}... | collective-permute-start | bytes 196616 | tf_op jit(solution)/shard_map/ppermute | solution.py:17
  298.5 8.3 %collective-permute-start.2 = (f32[1,8,2,8,128]{4,3,1,2,0:T(8,128)S(1)}, f32[1,8,2,8,128]{4,3,1,2,0:T(8,128)S(1)}, u32[]{:S(2)}, u32[]{:S(2)}) collective-permute-start(f32[1,8,2,8,128]{4,3,1,2,0:T(8,128)S(1)} %fusion.122), channel_id=1, source_target_pairs={{0,12},{4,16},{8,20},{12,24},{16,28},{20,32},{24,36},{28,40},{32,4... | collective-permute-start | bytes 196616 | tf_op jit(solution)/shard_map/ppermute | solution.py:17
  310.8 86.0 %all-gather.2.cloned.1.call-done = bf16[2,512,2048]{2,1,0:T(8,128)(2,1)} async-done(((bf16[2,8,2048]{2,1,0:T(8,128)(2,1)}), bf16[2,512,2048]{2,1,0:T(8,128)(2,1)}) %all-gather.2.cloned.1.call-update) | async-done | bytes 4194320 | tf_op jit(solution)/shard_map/all_gather | solution.py:169
  396.8 4.2 fusion.238
  401.0 19.3 %reduce-scatter.2.cloned.1.call-done = f32[2,128,128]{2,1,0:T(8,128)} async-done(((f32[2,512,128]{2,1,0:T(8,128)}), f32[2,128,128]{2,1,0:T(8,128)}) %reduce-scatter.2.cloned.1.call-update) | async-done | bytes 131088 | tf_op jit(solution)/shard_map/reduce_scatter | solution.py:173
  (475 shorter events, 141.5 us)
Async XLA Ops:
  6.5 390.2 %all-gather.2.cloned.1.call-start = ((), (), s32[]{:S(2)}) async-start(), calls=%async_computation.1 | async-start | bytes 4259840 | tf_op jit(solution)/shard_map/all_gather | solution.py:169
  7.4 97.2 %collective-permute-start.36 = (bf16[1,8,2048]{2,1,0:T(8,128)(2,1)S(1)}, bf16[1,8,2048]{2,1,0:T(8,128)(2,1)S(1)}, u32[]{:S(2)}, u32[]{:S(2)}) collective-permute-start(bf16[1,8,2048]{2,1,0:T(8,128)(2,1)S(1)} %get-tuple-element.333), channel_id=1, source_target_pairs={{0,8},{4,12},{8,16},{12,20},{16,24},{20,28},{24,32},{28,36},{32,40... | collective-permute-start | bytes 98312 | tf_op jit(solution)/shard_map/ppermute | solution.py:17
  11.2 91.7 %collective-permute-start.33 = (bf16[1,8,2048]{2,1,0:T(8,128)(2,1)S(1)}, bf16[1,8,2048]{2,1,0:T(8,128)(2,1)S(1)}, u32[]{:S(2)}, u32[]{:S(2)}) collective-permute-start(bf16[1,8,2048]{2,1,0:T(8,128)(2,1)S(1)} %get-tuple-element.333), channel_id=1, source_target_pairs={{0,4},{4,8},{8,12},{12,16},{16,20},{20,24},{24,28},{28,32},{32,36}... | collective-permute-start | bytes 98312 | tf_op jit(solution)/shard_map/ppermute | solution.py:17
  12.7 88.5 %collective-permute-start.30 = (bf16[1,8,2048]{2,1,0:T(8,128)(2,1)S(1)}, bf16[1,8,2048]{2,1,0:T(8,128)(2,1)S(1)}, u32[]{:S(2)}, u32[]{:S(2)}) collective-permute-start(bf16[1,8,2048]{2,1,0:T(8,128)(2,1)S(1)} %get-tuple-element.333), channel_id=1, source_target_pairs={{4,0},{8,4},{12,8},{16,12},{20,16},{24,20},{28,24},{32,28},{36,32}... | collective-permute-start | bytes 98312 | tf_op jit(solution)/shard_map/ppermute | solution.py:17
  14.0 85.5 %collective-permute-start.27 = (bf16[1,8,2048]{2,1,0:T(8,128)(2,1)S(1)}, bf16[1,8,2048]{2,1,0:T(8,128)(2,1)S(1)}, u32[]{:S(2)}, u32[]{:S(2)}) collective-permute-start(bf16[1,8,2048]{2,1,0:T(8,128)(2,1)S(1)} %get-tuple-element.333), channel_id=1, source_target_pairs={{8,0},{12,4},{16,8},{20,12},{24,16},{28,20},{32,24},{36,28},{40,32... | collective-permute-start | bytes 98312 | tf_op jit(solution)/shard_map/ppermute | solution.py:17
  15.3 43.2 %collective-permute-start.15 = (bf16[1,8,2048]{2,1,0:T(8,128)(2,1)S(1)}, bf16[1,8,2048]{2,1,0:T(8,128)(2,1)S(1)}, u32[]{:S(2)}, u32[]{:S(2)}) collective-permute-start(bf16[1,8,2048]{2,1,0:T(8,128)(2,1)S(1)} %get-tuple-element.334), channel_id=1, source_target_pairs={{0,12},{4,16},{8,20},{12,24},{16,28},{20,32},{24,36},{28,40},{32,4... | collective-permute-start | bytes 98312 | tf_op jit(solution)/shard_map/ppermute | solution.py:17
  96.2 11.0 %collective-permute-start = (bf16[1,8,2048]{2,1,0:T(8,128)(2,1)S(1)}, bf16[1,8,2048]{2,1,0:T(8,128)(2,1)S(1)}, u32[]{:S(2)}, u32[]{:S(2)}) collective-permute-start(bf16[1,8,2048]{2,1,0:T(8,128)(2,1)S(1)} %get-tuple-element.334), channel_id=1, source_target_pairs={{12,0},{16,4},{20,8},{24,12},{28,16},{32,20},{36,24},{40,28},{44,3... | collective-permute-start | bytes 98312 | tf_op jit(solution)/shard_map/ppermute | solution.py:17
  142.0 71.4 %collective-permute-start.21 = (f32[1,8,2,8]{3,1,2,0:T(8,128)S(1)}, f32[1,8,2,8]{3,1,2,0:T(8,128)S(1)}, u32[]{:S(2)}, u32[]{:S(2)}) collective-permute-start(f32[1,8,2,8]{3,1,2,0:T(8,128)S(1)} %fusion.678), channel_id=1, source_target_pairs={{4,0},{8,4},{12,8},{16,12},{20,16},{24,20},{28,24},{32,28},{36,32}... | collective-permute-start | bytes 1544 | tf_op jit(solution)/shard_map/ppermute | solution.py:17
  143.4 71.4 %collective-permute-start.22 = (f32[1,8,2,8]{3,1,2,0:T(8,128)S(1)}, f32[1,8,2,8]{3,1,2,0:T(8,128)S(1)}, u32[]{:S(2)}, u32[]{:S(2)}) collective-permute-start(f32[1,8,2,8]{3,1,2,0:T(8,128)S(1)} %fusion.671), channel_id=1, source_target_pairs={{8,0},{12,4},{16,8},{20,12},{24,16},{28,20},{32,24},{36,28},{40,32... | collective-permute-start | bytes 1544 | tf_op jit(solution)/shard_map/ppermute | solution.py:17
  144.7 71.3 %collective-permute-start.20 = (f32[1,8,2,8]{3,1,2,0:T(8,128)S(1)}, f32[1,8,2,8]{3,1,2,0:T(8,128)S(1)}, u32[]{:S(2)}, u32[]{:S(2)}) collective-permute-start(f32[1,8,2,8]{3,1,2,0:T(8,128)S(1)} %fusion.685), channel_id=1, source_target_pairs={{0,4},{4,8},{8,12},{12,16},{16,20},{20,24},{24,28},{28,32},{32,36}... | collective-permute-start | bytes 1544 | tf_op jit(solution)/shard_map/ppermute | solution.py:17
  147.8 69.5 %collective-permute-start.19 = (f32[1,8,2,8]{3,1,2,0:T(8,128)S(1)}, f32[1,8,2,8]{3,1,2,0:T(8,128)S(1)}, u32[]{:S(2)}, u32[]{:S(2)}) collective-permute-start(f32[1,8,2,8]{3,1,2,0:T(8,128)S(1)} %fusion.692), channel_id=1, source_target_pairs={{0,8},{4,12},{8,16},{12,20},{16,24},{20,28},{24,32},{28,36},{32,40... | collective-permute-start | bytes 1544 | tf_op jit(solution)/shard_map/ppermute | solution.py:17
  153.9 26.9 %collective-permute-start.1 = (f32[1,8,2,8]{3,1,2,0:T(8,128)S(1)}, f32[1,8,2,8]{3,1,2,0:T(8,128)S(1)}, u32[]{:S(2)}, u32[]{:S(2)}) collective-permute-start(f32[1,8,2,8]{3,1,2,0:T(8,128)S(1)} %fusion.748), channel_id=1, source_target_pairs={{0,12},{4,16},{8,20},{12,24},{16,28},{20,32},{24,36},{28,40},{32,4... | collective-permute-start | bytes 1544 | tf_op jit(solution)/shard_map/ppermute | solution.py:17
  206.8 11.9 %collective-permute-start.18 = (f32[1,8,2,8]{3,1,2,0:T(8,128)S(1)}, f32[1,8,2,8]{3,1,2,0:T(8,128)S(1)}, u32[]{:S(2)}, u32[]{:S(2)}) collective-permute-start(f32[1,8,2,8]{3,1,2,0:T(8,128)S(1)} %fusion.699), channel_id=1, source_target_pairs={{0,12},{4,16},{8,20},{12,24},{16,28},{20,32},{24,36},{28,40},{32,4... | collective-permute-start | bytes 1544 | tf_op jit(solution)/shard_map/ppermute | solution.py:17
  214.7 36.1 %collective-permute-start.47 = (f32[1,8,2,8]{3,1,2,0:T(8,128)S(1)}, f32[1,8,2,8]{3,1,2,0:T(8,128)S(1)}, u32[]{:S(2)}, u32[]{:S(2)}) collective-permute-start(f32[1,8,2,8]{3,1,2,0:T(8,128)S(1)} %get-tuple-element.304), channel_id=1, source_target_pairs={{12,0},{16,4},{20,8},{24,12},{28,16},{32,20},{36,24},{40,28},{44,3... | collective-permute-start | bytes 1544 | tf_op jit(solution)/shard_map/ppermute | solution.py:17
  216.0 39.0 %collective-permute-start.40 = (f32[1,8,2,8]{3,1,2,0:T(8,128)S(1)}, f32[1,8,2,8]{3,1,2,0:T(8,128)S(1)}, u32[]{:S(2)}, u32[]{:S(2)}) collective-permute-start(f32[1,8,2,8]{3,1,2,0:T(8,128)S(1)} %get-tuple-element.283), channel_id=1, source_target_pairs={{12,0},{16,4},{20,8},{24,12},{28,16},{32,20},{36,24},{40,28},{44,3... | collective-permute-start | bytes 1544 | tf_op jit(solution)/shard_map/ppermute | solution.py:17
  217.4 44.9 %collective-permute-start.46 = (f32[1,8,2,8]{3,1,2,0:T(8,128)S(1)}, f32[1,8,2,8]{3,1,2,0:T(8,128)S(1)}, u32[]{:S(2)}, u32[]{:S(2)}) collective-permute-start(f32[1,8,2,8]{3,1,2,0:T(8,128)S(1)} %get-tuple-element.301), channel_id=1, source_target_pairs={{8,0},{12,4},{16,8},{20,12},{24,16},{28,20},{32,24},{36,28},{40,32... | collective-permute-start | bytes 1544 | tf_op jit(solution)/shard_map/ppermute | solution.py:17
  218.7 26.7 %collective-permute-start.37 = (f32[1,8,2,8]{3,1,2,0:T(8,128)S(1)}, f32[1,8,2,8]{3,1,2,0:T(8,128)S(1)}, u32[]{:S(2)}, u32[]{:S(2)}) collective-permute-start(f32[1,8,2,8]{3,1,2,0:T(8,128)S(1)} %get-tuple-element.273), channel_id=1, source_target_pairs={{8,0},{12,4},{16,8},{20,12},{24,16},{28,20},{32,24},{36,28},{40,32... | collective-permute-start | bytes 1544 | tf_op jit(solution)/shard_map/ppermute | solution.py:17
  244.0 19.5 %collective-permute-start.45 = (f32[1,8,2,8]{3,1,2,0:T(8,128)S(1)}, f32[1,8,2,8]{3,1,2,0:T(8,128)S(1)}, u32[]{:S(2)}, u32[]{:S(2)}) collective-permute-start(f32[1,8,2,8]{3,1,2,0:T(8,128)S(1)} %get-tuple-element.298), channel_id=1, source_target_pairs={{4,0},{8,4},{12,8},{16,12},{20,16},{24,20},{28,24},{32,28},{36,32}... | collective-permute-start | bytes 1544 | tf_op jit(solution)/shard_map/ppermute | solution.py:17
  245.4 19.5 %collective-permute-start.44 = (f32[1,8,2,8]{3,1,2,0:T(8,128)S(1)}, f32[1,8,2,8]{3,1,2,0:T(8,128)S(1)}, u32[]{:S(2)}, u32[]{:S(2)}) collective-permute-start(f32[1,8,2,8]{3,1,2,0:T(8,128)S(1)} %get-tuple-element.295), channel_id=1, source_target_pairs={{0,4},{4,8},{8,12},{12,16},{16,20},{20,24},{24,28},{28,32},{32,36}... | collective-permute-start | bytes 1544 | tf_op jit(solution)/shard_map/ppermute | solution.py:17
  250.9 15.3 %collective-permute-start.43 = (f32[1,8,2,8]{3,1,2,0:T(8,128)S(1)}, f32[1,8,2,8]{3,1,2,0:T(8,128)S(1)}, u32[]{:S(2)}, u32[]{:S(2)}) collective-permute-start(f32[1,8,2,8]{3,1,2,0:T(8,128)S(1)} %get-tuple-element.292), channel_id=1, source_target_pairs={{0,8},{4,12},{8,16},{12,20},{16,24},{20,28},{24,32},{28,36},{32,40... | collective-permute-start | bytes 1544 | tf_op jit(solution)/shard_map/ppermute | solution.py:17
  255.1 16.8 %collective-permute-start.42 = (f32[1,8,2,8]{3,1,2,0:T(8,128)S(1)}, f32[1,8,2,8]{3,1,2,0:T(8,128)S(1)}, u32[]{:S(2)}, u32[]{:S(2)}) collective-permute-start(f32[1,8,2,8]{3,1,2,0:T(8,128)S(1)} %get-tuple-element.289), channel_id=1, source_target_pairs={{0,12},{4,16},{8,20},{12,24},{16,28},{20,32},{24,36},{28,40},{32,4... | collective-permute-start | bytes 1544 | tf_op jit(solution)/shard_map/ppermute | solution.py:17
  262.3 15.9 %collective-permute-start.41 = (f32[1,8,2,8,128]{4,3,1,2,0:T(8,128)S(1)}, f32[1,8,2,8,128]{4,3,1,2,0:T(8,128)S(1)}, u32[]{:S(2)}, u32[]{:S(2)}) collective-permute-start(f32[1,8,2,8,128]{4,3,1,2,0:T(8,128)S(1)} %add_select_fusion), channel_id=1, source_target_pairs={{12,0},{16,4},{20,8},{24,12},{28,16},{32,20},{36,24},{40,28},{44,3... | collective-permute-start | bytes 196616 | tf_op jit(solution)/shard_map/ppermute | solution.py:17
  263.6 19.5 %collective-permute-start.38 = (f32[1,8,2,8,128]{4,3,1,2,0:T(8,128)S(1)}, f32[1,8,2,8,128]{4,3,1,2,0:T(8,128)S(1)}, u32[]{:S(2)}, u32[]{:S(2)}) collective-permute-start(f32[1,8,2,8,128]{4,3,1,2,0:T(8,128)S(1)} %add_select_fusion.1), channel_id=1, source_target_pairs={{8,0},{12,4},{16,8},{20,12},{24,16},{28,20},{32,24},{36,28},{40,32... | collective-permute-start | bytes 196616 | tf_op jit(solution)/shard_map/ppermute | solution.py:17
  264.9 19.6 %collective-permute-start.35 = (f32[1,8,2,8,128]{4,3,1,2,0:T(8,128)S(1)}, f32[1,8,2,8,128]{4,3,1,2,0:T(8,128)S(1)}, u32[]{:S(2)}, u32[]{:S(2)}) collective-permute-start(f32[1,8,2,8,128]{4,3,1,2,0:T(8,128)S(1)} %add_select_fusion.2), channel_id=1, source_target_pairs={{4,0},{8,4},{12,8},{16,12},{20,16},{24,20},{28,24},{32,28},{36,32}... | collective-permute-start | bytes 196616 | tf_op jit(solution)/shard_map/ppermute | solution.py:17
  266.2 19.6 %collective-permute-start.32 = (f32[1,8,2,8,128]{4,3,1,2,0:T(8,128)S(1)}, f32[1,8,2,8,128]{4,3,1,2,0:T(8,128)S(1)}, u32[]{:S(2)}, u32[]{:S(2)}) collective-permute-start(f32[1,8,2,8,128]{4,3,1,2,0:T(8,128)S(1)} %add_select_fusion.3), channel_id=1, source_target_pairs={{0,4},{4,8},{8,12},{12,16},{16,20},{20,24},{24,28},{28,32},{32,36}... | collective-permute-start | bytes 196616 | tf_op jit(solution)/shard_map/ppermute | solution.py:17
  271.9 19.3 %collective-permute-start.29 = (f32[1,8,2,8,128]{4,3,1,2,0:T(8,128)S(1)}, f32[1,8,2,8,128]{4,3,1,2,0:T(8,128)S(1)}, u32[]{:S(2)}, u32[]{:S(2)}) collective-permute-start(f32[1,8,2,8,128]{4,3,1,2,0:T(8,128)S(1)} %add_select_fusion.4), channel_id=1, source_target_pairs={{0,8},{4,12},{8,16},{12,20},{16,24},{20,28},{24,32},{28,36},{32,40... | collective-permute-start | bytes 196616 | tf_op jit(solution)/shard_map/ppermute | solution.py:17
  278.1 19.0 %collective-permute-start.26 = (f32[1,8,2,8,128]{4,3,1,2,0:T(8,128)S(1)}, f32[1,8,2,8,128]{4,3,1,2,0:T(8,128)S(1)}, u32[]{:S(2)}, u32[]{:S(2)}) collective-permute-start(f32[1,8,2,8,128]{4,3,1,2,0:T(8,128)S(1)} %add_select_fusion.5), channel_id=1, source_target_pairs={{0,12},{4,16},{8,20},{12,24},{16,28},{20,32},{24,36},{28,40},{32,4... | collective-permute-start | bytes 196616 | tf_op jit(solution)/shard_map/ppermute | solution.py:17
  283.1 15.4 %collective-permute-start.17 = (f32[1,8,2,8,128]{4,3,1,2,0:T(8,128)S(1)}, f32[1,8,2,8,128]{4,3,1,2,0:T(8,128)S(1)}, u32[]{:S(2)}, u32[]{:S(2)}) collective-permute-start(f32[1,8,2,8,128]{4,3,1,2,0:T(8,128)S(1)} %fusion.167), channel_id=1, source_target_pairs={{12,0},{16,4},{20,8},{24,12},{28,16},{32,20},{36,24},{40,28},{44,3... | collective-permute-start | bytes 196616 | tf_op jit(solution)/shard_map/ppermute | solution.py:17
  284.4 22.8 %collective-permute-start.11 = (f32[1,8,2,8,128]{4,3,1,2,0:T(8,128)S(1)}, f32[1,8,2,8,128]{4,3,1,2,0:T(8,128)S(1)}, u32[]{:S(2)}, u32[]{:S(2)}) collective-permute-start(f32[1,8,2,8,128]{4,3,1,2,0:T(8,128)S(1)} %fusion.149), channel_id=1, source_target_pairs={{4,0},{8,4},{12,8},{16,12},{20,16},{24,20},{28,24},{32,28},{36,32}... | collective-permute-start | bytes 196616 | tf_op jit(solution)/shard_map/ppermute | solution.py:17
  285.8 21.5 %collective-permute-start.5 = (f32[1,8,2,8,128]{4,3,1,2,0:T(8,128)S(1)}, f32[1,8,2,8,128]{4,3,1,2,0:T(8,128)S(1)}, u32[]{:S(2)}, u32[]{:S(2)}) collective-permute-start(f32[1,8,2,8,128]{4,3,1,2,0:T(8,128)S(1)} %fusion.131), channel_id=1, source_target_pairs={{0,8},{4,12},{8,16},{12,20},{16,24},{20,28},{24,32},{28,36},{32,40... | collective-permute-start | bytes 196616 | tf_op jit(solution)/shard_map/ppermute | solution.py:17
  291.3 16.0 %collective-permute-start.8 = (f32[1,8,2,8,128]{4,3,1,2,0:T(8,128)S(1)}, f32[1,8,2,8,128]{4,3,1,2,0:T(8,128)S(1)}, u32[]{:S(2)}, u32[]{:S(2)}) collective-permute-start(f32[1,8,2,8,128]{4,3,1,2,0:T(8,128)S(1)} %fusion.140), channel_id=1, source_target_pairs={{0,4},{4,8},{8,12},{12,16},{16,20},{20,24},{24,28},{28,32},{32,36}... | collective-permute-start | bytes 196616 | tf_op jit(solution)/shard_map/ppermute | solution.py:17
  310.7 109.6 %reduce-scatter.2.cloned.1.call-start = ((), (), s32[]{:S(2)}) async-start(), calls=%async_computation.2 | async-start | bytes 655360 | tf_op jit(solution)/shard_map/reduce_scatter | solution.py:173
  (24 other events, 532.7 us)
Sparse Core Ops, SparseCore 0:
  310.8 85.8 all-gather.1
  401.1 19.1 reduce-scatter.1
where the time goes:
time: 433 us; the launch traced here: 429 us
  starting transfers between devices  155 us (36%)
  waiting for transfers between devices  140 us (32%)
  matrix products  72.9 us (17%)
  local copies, waits for them, and re-layouts  27.5 us (6%)
  other arithmetic  17.5 us (4%)
  between operations  16.8 us (4%)
    ppermute x48, starting transfers between devices, from_behind(): lax.ppermute(value, axis, [(source, source + steps) for source in range(f...  154 us
    all_gather x1, waiting for transfers between devices, per_device(): lax.all_gather(attention, 'dp', axis=1, tiled=True)  86 us
    dot_general x112, matrix products, attend_local(): jnp.einsum('rngqt,gtd->rngqd', weights, value_cache[holder], preferred_el...  40.6 us
    ppermute x48, waiting for transfers between devices, from_behind(): lax.ppermute(value, axis, [(source, source + steps) for source in range(f...  34.4 us
    dot_general x112, matrix products, attend_local(): jnp.einsum('rngqd,gtd->rngqt', grouped, key_cache[holder], preferred_elem...  26.8 us
    reduce_scatter x1, waiting for transfers between devices, per_device(): lax.psum_scatter(terms, 'tensor', scatter_dimension=1, tiled=True)  19.3 us
    gather x14, local copies, waits for them, and re-layouts, attend_local(): jnp.take(roots[round_index], safe_ids)  9.08 us
  transfers between devices with their start and end apart: 50, of which 15 were waited for; matrix products, arithmetic and copies ran while one was open for 17% of the time, Pallas kernels for 0%

commit v1 on v0

v1 whole, which is shorter than its diff:
```python
import math

import jax
import jax.numpy as jnp
from jax import lax
from jax.experimental import pallas as pl
from jax.experimental.pallas import tpu as pltpu
from jax.sharding import Mesh
from jax.sharding import PartitionSpec as P

FAMILY = 32
AXES = ("y", "zo", "zi", "c", "x")
SIZES = (4, 4, 2, 2, 4)
DP = ("y", "zo", "zi", "c")

HOLD = 8
ITEMS = 64
SLOTS = 128
CHUNKS = SLOTS // 8
HEADS = 16
KV = 2
GROUP = 8
HD = 128
FEAT = HEADS * HD
HALF = FEAT // 2
CACHE = 512
NEG = -1e30

VMEM = pl.BlockSpec(memory_space=pltpu.VMEM)
SMEM = pl.BlockSpec(memory_space=pltpu.SMEM)


def plan_kernel(ids_ref, anc_ref, sort_ref, parent_ref, flag_ref, unsort_ref, chunk_ref, count, current):
    first, own, zi, c = ids_ref[0], ids_ref[1], ids_ref[2], ids_ref[3]
    sort_ref[...] = jnp.zeros_like(sort_ref)
    parent_ref[...] = jnp.zeros_like(parent_ref)
    flag_ref[...] = jnp.zeros_like(flag_ref)
    for h in range(HOLD):
        count[h] = 0
        current[h] = 0
    for j in range(CHUNKS + 1):
        chunk_ref[j] = 0
    lane = lax.broadcasted_iota(jnp.int32, (1, 128), 1)

    def step(n, used):
        block, r, i = n // 16, (n // 8) % 2, n % 8
        place = ((zi ^ (block // 2)) * 2 + (c ^ (block % 2))) * 8 + i
        particle = first + place
        mother = anc_ref[1, particle]
        source = jnp.where(r == 1, mother, particle)
        root = anc_ref[0, source] - own
        here = jnp.logical_and(root >= 0, root < HOLD)
        h = jnp.clip(root, 0, HOLD - 1)
        seen = count[h]
        opens = jnp.logical_and(here, seen % 8 == 0)
        chunk = jnp.where(opens, used, current[h])
        current[h] = chunk
        count[h] = seen + jnp.where(here, 1, 0)
        slot = jnp.where(here, chunk * 8 + seen % 8, SLOTS)
        chunk_ref[jnp.where(opens, chunk, CHUNKS)] = h
        sort_ref[pl.ds(slot, 1), :] = jnp.where(lane == n, 1.0, 0.0)
        mp = mother - first
        device = mp // 8
        mblock = ((device // 2) ^ zi) * 2 + ((device % 2) ^ c)
        mn = mblock * 16 + mp % 8
        with_parent = jnp.where(r == 1, 1.0, 0.0)
        parent_ref[pl.ds(slot, 1), :] = jnp.where(lane == mn, 1.0, 0.0) * with_parent
        flag_ref[pl.ds(slot, 1), :] = jnp.zeros((1, 128), jnp.float32) + with_parent
        unsort_ref[pl.ds(r * FAMILY + place, 1), :] = jnp.where(lane == slot, 1.0, 0.0)
        return jnp.where(opens, used + 1, used)

    used = lax.fori_loop(0, ITEMS, step, jnp.int32(0))
    chunk_ref[CHUNKS] = used


def attend_kernel(
    ids_ref,
    chunk_ref,
    len_ref,
    sort_ref,
    parent_ref,
    flag_ref,
    unsort_ref,
    m0,
    m1,
    m2,
    m3,
    key_ref,
    value_ref,
    keep_ref,
    give_ref,
    message,
    ordered,
    mothers,
    answer,
):
    factor = 1.0 / math.sqrt(HD)
    zi, c = ids_ref[2], ids_ref[3]
    for b, m in enumerate((m0, m1, m2, m3)):
        message[b * 16 : b * 16 + 16, :] = m[...]
    sort = sort_ref[0:SLOTS, 0:ITEMS].astype(jnp.bfloat16)
    ordered[...] = jnp.dot(sort, message[...], preferred_element_type=jnp.float32)
    pick = parent_ref[0:SLOTS, 0:ITEMS].astype(jnp.bfloat16)
    mothers[...] = jnp.dot(pick, message[:, FEAT:], preferred_element_type=jnp.float32)
    answer[...] = jnp.zeros_like(answer)
    places = lax.broadcasted_iota(jnp.int32, (1, CACHE), 1)

    def tile(v):
        return jnp.concatenate([v] * GROUP, axis=0)

    def body(j, carry):
        h = chunk_ref[j]
        inside = places < len_ref[h]
        rows = pl.ds(pl.multiple_of(j * 8, 8), 8)
        flag = tile(flag_ref[rows, 0:1]) > 0.5
        for g in range(KV):
            q = jnp.concatenate(
                [ordered[rows, (g * GROUP + k) * HD : (g * GROUP + k + 1) * HD] for k in range(GROUP)], axis=0
            )
            scores = (
                lax.dot_general(
                    q.astype(jnp.bfloat16),
                    key_ref[h, g],
                    (((1,), (1,)), ((), ())),
                    preferred_element_type=jnp.float32,
                )
                * factor
            )
            scores = jnp.where(inside, scores, NEG)
            top = jnp.max(scores, axis=-1, keepdims=True)
            weights = jnp.where(inside, jnp.exp(scores - top), 0.0).astype(jnp.bfloat16)
            mass = jnp.sum(weights.astype(jnp.float32), axis=-1, keepdims=True)
            mix = jnp.dot(weights, value_ref[h, g], preferred_element_type=jnp.float32)
            own_k = tile(ordered[rows, FEAT + g * HD : FEAT + (g + 1) * HD])
            own_v = tile(ordered[rows, FEAT + (KV + g) * HD : FEAT + (KV + g + 1) * HD])
            par_k = tile(mothers[rows, g * HD : (g + 1) * HD])
            par_v = tile(mothers[rows, (KV + g) * HD : (KV + g + 1) * HD])
            own_s = jnp.sum(q * own_k, axis=-1, keepdims=True) * factor
            par_s = jnp.sum(q * par_k, axis=-1, keepdims=True) * factor
            par_s = jnp.where(flag, par_s, NEG)
            peak = jnp.maximum(jnp.maximum(top, own_s), par_s)
            e0 = jnp.exp(top - peak)
            e1 = jnp.exp(own_s - peak)
            e2 = jnp.where(flag, jnp.exp(par_s - peak), 0.0)
            out = (mix * e0 + own_v * e1 + par_v * e2) / (mass * e0 + e1 + e2)
            for k in range(GROUP):
                answer[g, rows, k * HD : (k + 1) * HD] = out[k * 8 : k * 8 + 8]
        return carry

    lax.fori_loop(0, chunk_ref[CHUNKS], body, 0)
    for cc, ref in ((0, keep_ref), (1, give_ref)):
        feats = answer[c ^ cc].astype(jnp.bfloat16)
        for zz in range(2):
            which = pl.ds(pl.multiple_of((zi ^ zz) * FAMILY, FAMILY), FAMILY)
            back = unsort_ref[which, :].astype(jnp.bfloat16)
            ref[zz] = jnp.dot(back, feats, preferred_element_type=jnp.float32).astype(jnp.bfloat16)


def project_kernel(ids_ref, mine_ref, other_ref, w_ref, *outs):
    c, x = ids_ref[3], ids_ref[4]
    lo = pl.ds(pl.multiple_of(c * HALF, HALF), HALF)
    hi = pl.ds(pl.multiple_of((1 - c) * HALF, HALF), HALF)
    for k, out in enumerate(outs):
        y = (x + k) % 4
        total = jnp.dot(mine_ref[...], w_ref[y, lo, :], preferred_element_type=jnp.float32)
        total += jnp.dot(other_ref[...], w_ref[y, hi, :], preferred_element_type=jnp.float32)
        out[...] = total.astype(jnp.bfloat16)


def permute(value, axes, move):
    sizes = [SIZES[AXES.index(a)] for a in axes]
    pairs = []
    total = math.prod(sizes)
    for n in range(total):
        coords, rest = [], n
        for s in reversed(sizes):
            coords.append(rest % s)
            rest //= s
        to = move(*reversed(coords))
        flat = 0
        for t, s in zip(to, sizes):
            flat = flat * s + t % s
        pairs.append((n, flat))
    return lax.ppermute(value, axes, pairs)


def swap_core(v):
    return permute(v, ("c",), lambda c: (1 - c,))


def swap_chip(v):
    return permute(v, ("zi",), lambda z: (1 - z,))


def per_device(queries, key_cache, value_cache, new_keys, new_values, lengths, ancestors, out_weight):
    y, zo, zi, c, x = (lax.axis_index(a) for a in AXES)
    family = y * 4 + zo
    ids = jnp.stack([family * FAMILY, family * FAMILY + (zi * 2 + c) * HOLD, zi, c, x]).astype(jnp.int32)
    weights = lax.all_gather(out_weight, "y", axis=0)
    m0 = jnp.concatenate([queries, new_keys, new_values], axis=-1).reshape(2 * HOLD, FEAT + 2 * KV * HD)
    m2 = swap_chip(m0)
    m1 = swap_core(m0)
    m3 = swap_core(m2)
    f32 = jnp.float32
    sort, parent, flag, unsort, chunk = pl.pallas_call(
        plan_kernel,
        out_shape=[
            jax.ShapeDtypeStruct((SLOTS + 8, 128), f32),
            jax.ShapeDtypeStruct((SLOTS + 8, 128), f32),
            jax.ShapeDtypeStruct((SLOTS + 8, 128), f32),
            jax.ShapeDtypeStruct((ITEMS, 128), f32),
            jax.ShapeDtypeStruct((CHUNKS + 1,), jnp.int32),
        ],
        in_specs=[SMEM, SMEM],
        out_specs=[VMEM, VMEM, VMEM, VMEM, SMEM],
        scratch_shapes=[pltpu.SMEM((HOLD,), jnp.int32), pltpu.SMEM((HOLD,), jnp.int32)],
        name="plan",
    )(ids, ancestors)
    block = jax.ShapeDtypeStruct((2, FAMILY, HALF), jnp.bfloat16)
    keep, give = pl.pallas_call(
        attend_kernel,
        out_shape=[block, block],
        in_specs=[SMEM, SMEM, SMEM] + [VMEM] * 10,
        out_specs=[VMEM, VMEM],
        scratch_shapes=[
            pltpu.VMEM((ITEMS, FEAT + 2 * KV * HD), jnp.bfloat16),
            pltpu.VMEM((SLOTS, FEAT + 2 * KV * HD), f32),
            pltpu.VMEM((SLOTS, 2 * KV * HD), f32),
            pltpu.VMEM((KV, SLOTS, HALF), f32),
        ],
        compiler_params=pltpu.CompilerParams(vmem_limit_bytes=24 * 2**20),
        name="attend",
    )(ids, chunk, lengths, sort, parent, flag, unsort, m0, m1, m2, m3, key_cache, value_cache)
    chip = keep + swap_core(give)
    ours = chip[0] + swap_chip(chip[1])
    gathered = lax.all_gather(ours, ("zi", "zo"), axis=0, tiled=True)
    other = swap_core(gathered)
    rows = gathered.shape[0]
    parts = pl.pallas_call(
        project_kernel,
        out_shape=[jax.ShapeDtypeStruct((rows, 128), jnp.bfloat16)] * 4,
        in_specs=[SMEM, VMEM, VMEM, VMEM],
        out_specs=[VMEM] * 4,
        compiler_params=pltpu.CompilerParams(vmem_limit_bytes=24 * 2**20),
        name="project",
    )(ids, gathered, other, weights)
    total = 0.0
    for k, part in enumerate(parts):
        total = total + permute(part, ("y", "x"), lambda y, x, k=k: (x + k, y)).astype(f32)
    return total.astype(jnp.bfloat16).reshape(2, rows // 2, 128)


def solution(mesh):
    fine = Mesh(mesh.devices.reshape(SIZES), AXES)
    in_specs = (
        P(None, DP, "x"),
        P(DP, "x", None, None),
        P(DP, "x", None, None),
        P(None, DP, "x"),
        P(None, DP, "x"),
        P(DP),
        P(),
        P("x", DP),
    )
    return jax.shard_map(
        per_device, mesh=fine, in_specs=in_specs, out_specs=P(None, "x", DP), check_vma=False
    )
```

time: 433 us -> 107 us (0.25)
  the two profiles are of different devices: /device:TPU:6 before, /device:TPU:48 now
where the time goes in v1:
time: 107 us
  blocking collectives  35 us (33%)
  waiting for transfers between devices  22.2 us (21%)
  between operations  13.5 us (13%)
  Pallas kernels  13.2 us (12%)
  local copies, waits for them, and re-layouts  10.8 us (10%)
  starting transfers between devices  10.4 us (10%)
  other arithmetic  1.59 us (1%)
    all_gather x1, blocking collectives, per_device(): gathered = lax.all_gather(ours, ('zi', 'zo'), axis=0, tiled=True)  35 us
    ppermute x10, waiting for transfers between devices, permute(): return lax.ppermute(value, axes, pairs)  21.5 us
    ppermute x10, starting transfers between devices, permute(): return lax.ppermute(value, axes, pairs)  10.4 us
    unnamed x22, local copies, waits for them, and re-layouts  10.1 us
    pallas_call x1, Pallas kernels, per_device(): pl.pallas_call(attend_kernel, out_shape=[block, block], in_specs=[SMEM, S...  6.48 us
    pallas_call x1, Pallas kernels, per_device(): pl.pallas_call(plan_kernel, out_shape=[jax.ShapeDtypeStruct((SLOTS + 8, 1...  4.93 us
  transfers between devices with their start and end apart: 11, of which 8 were waited for; matrix products, arithmetic and copies ran while one was open for 2% of the time, Pallas kernels for 11%

profile of v1, /device:TPU:48, one launch (start us, length us, event | category | flops | bytes accessed | tf_op | source)
XLA Modules:
  0.0 106.7 jit_solution(13978309333594421391)
XLA Ops:
  6.5 0.7 all-gather.3.cloned.1.call-update
  7.3 0.9 maximum_bitcast_fusion.m0
  8.1 0.1 collective-permute-start.1
  8.2 4.3 %collective-permute-done.1.m2 = bf16[16,2560]{1,0:T(8,128)(2,1)S(1)} collective-permute-done((bf16[16,2560]{1,0:T(8,128)(2,1)S(1)}, bf16[16,2560]{1,0:T(8,128)(2,1)S(1)}, u32[]{:S(2)}, u32[]{:S(2)}) %collective-permute-start.1) | collective-permute-done | bytes 81952 | tf_op jit(solution)/shard_map/ppermute | solution.py:184
  12.6 0.7 stack.23.ids_ref
  13.3 4.9 %plan.1 = (f32[136,128]{1,0:T(8,128)}, f32[136,128]{1,0:T(8,128)}, f32[136,128]{1,0:T(8,128)}, f32[64,128]{1,0:T(8,128)}, s32[17]{0:T(128)}) custom-call(s32[5]{0:T(128)} %stack.23.ids_ref, s32[2,512]{1,0:T(2,128)} %anc_ref.1), custom_call_target="tpu_custom_call" | custom-call | tf_op jit(solution)/shard_map/plan/pallas_call | solution.py:205
  18.2 1.6 %copy-done = bf16[8,2,512,128]{3,2,1,0:T(8,128)(2,1)S(1)} copy-done((bf16[8,2,512,128]{3,2,1,0:T(8,128)(2,1)S(1)}, bf16[8,2,512,128]{3,2,1,0:T(8,128)(2,1)}, u32[]{:S(2)}) %copy-start) | copy-done | bytes 2097176
  19.8 1.6 %copy-done.1 = bf16[8,2,512,128]{3,2,1,0:T(8,128)(2,1)S(1)} copy-done((bf16[8,2,512,128]{3,2,1,0:T(8,128)(2,1)S(1)}, bf16[8,2,512,128]{3,2,1,0:T(8,128)(2,1)}, u32[]{:S(2)}) %copy-start.1) | copy-done | bytes 2097176
  21.4 0.9 copy-done.3
  22.3 0.9 copy-done.4
  23.2 0.9 copy-done.5
  24.1 0.8 copy-done.6
  24.8 0.7 copy-done.7
  25.5 0.7 copy-done.9
  26.2 0.6 copy-done.10
  26.8 6.5 %attend.1 = (bf16[2,32,1024]{2,1,0:T(8,128)(2,1)S(1)}, bf16[2,32,1024]{2,1,0:T(8,128)(2,1)S(1)}) custom-call(s32[5]{0:T(128)S(1)} %copy-done.7, s32[17]{0:T(128)S(1)} %copy-done.10, s32[8]{0:T(128)S(1)} %copy-done.9, f32[136,128]{1,0:T(8,128)S(1)} %copy-done.3, f32[136,128]{1,0:T(8,128)S(1)} %copy-done.4, f32[136,128]{1,0:T(8,128)S(1)} %copy-done.5, ...), custom_call_target="tpu_custom_call" | custom-call | tf_op jit(solution)/shard_map/attend/pallas_call | solution.py:220
  33.3 0.1 collective-permute-start.3
  33.4 1.3 %collective-permute-done.3 = bf16[2,32,1024]{2,1,0:T(8,128)(2,1)S(1)} collective-permute-done((bf16[2,32,1024]{2,1,0:T(8,128)(2,1)S(1)}, bf16[2,32,1024]{2,1,0:T(8,128)(2,1)S(1)}, u32[]{:S(2)}, u32[]{:S(2)}) %collective-permute-start.3) | collective-permute-done | bytes 131104 | tf_op jit(solution)/shard_map/ppermute | solution.py:184
  34.9 4.3 %collective-permute-done.4 = bf16[32,1024]{1,0:T(8,128)(2,1)S(1)} collective-permute-done((bf16[32,1024]{1,0:T(8,128)(2,1)S(1)}, bf16[32,1024]{1,0:T(8,128)(2,1)S(1)}, u32[]{:S(2)}, u32[]{:S(2)}) %collective-permute-start.4) | collective-permute-done | bytes 65568 | tf_op jit(solution)/shard_map/ppermute | solution.py:184
  39.1 35.0 %all_gather.9.mine_ref = bf16[256,1024]{1,0:T(8,128)(2,1)S(1)} all-gather(bf16[32,1024]{1,0:T(8,128)(2,1)S(1)} %fusion), channel_id=1, replica_groups=mesh['y'=4,'zo'=4,'zi'=2,'c'=2,'x'=4] {'zi','zo'}, dimensions={0}, use_global_device_ids=true | all-gather | bytes 589824 | tf_op jit(solution)/shard_map/all_gather | solution.py:236
  74.1 1.9 %collective-permute-done.5.other_ref = bf16[256,1024]{1,0:T(8,128)(2,1)S(1)} collective-permute-done((bf16[256,1024]{1,0:T(8,128)(2,1)S(1)}, bf16[256,1024]{1,0:T(8,128)(2,1)S(1)}, u32[]{:S(2)}, u32[]{:S(2)}) %collective-permute-start.5) | collective-permute-done | bytes 524320 | tf_op jit(solution)/shard_map/ppermute | solution.py:184
  76.0 1.6 %copy-done.2 = bf16[8192,128]{1,0:T(8,128)(2,1)S(1)} copy-done((bf16[8192,128]{1,0:T(8,128)(2,1)S(1)}, bf16[8192,128]{1,0:T(8,128)(2,1)}, u32[]{:S(2)}) %copy-start.2) | copy-done | bytes 2097176
  77.6 1.8 %project.1 = (bf16[256,128]{1,0:T(8,128)(2,1)S(1)}, bf16[256,128]{1,0:T(8,128)(2,1)S(1)}, bf16[256,128]{1,0:T(8,128)(2,1)S(1)}, bf16[256,128]{1,0:T(8,128)(2,1)S(1)}) custom-call(s32[5]{0:T(128)S(1)} %copy-done.8, bf16[256,1024]{1,0:T(8,128)(2,1)S(1)} %all_gather.9.mine_ref, bf16[256,1024]{1,0:T(8,128)(2,1)S(1)} %collective-permute-done.5.other_ref, ...), custom_call_target="tpu_custom_call" | custom-call | tf_op jit(solution)/shard_map/project/pallas_call | solution.py:239
  79.4 4.2 %collective-permute-start.6 = (bf16[256,128]{1,0:T(8,128)(2,1)S(1)}, bf16[256,128]{1,0:T(8,128)(2,1)S(1)}, u32[]{:S(2)}, u32[]{:S(2)}) collective-permute-start(bf16[256,128]{1,0:T(8,128)(2,1)S(1)} %get-tuple-element.23), channel_id=1, source_target_pairs={{0,0},{1,64},{2,128},{3,192},{64,1},{65,65},{66,129},{67,193},{128... | collective-permute-start | bytes 196616 | tf_op jit(solution)/shard_map/ppermute | solution.py:184
  83.6 2.5 %collective-permute-start.7 = (bf16[256,128]{1,0:T(8,128)(2,1)S(1)}, bf16[256,128]{1,0:T(8,128)(2,1)S(1)}, u32[]{:S(2)}, u32[]{:S(2)}) collective-permute-start(bf16[256,128]{1,0:T(8,128)(2,1)S(1)} %get-tuple-element.24), channel_id=1, source_target_pairs={{0,64},{1,128},{2,192},{3,0},{64,65},{65,129},{66,193},{67,1},{128... | collective-permute-start | bytes 196616 | tf_op jit(solution)/shard_map/ppermute | solution.py:184
  86.1 1.2 %collective-permute-start.8 = (bf16[256,128]{1,0:T(8,128)(2,1)S(1)}, bf16[256,128]{1,0:T(8,128)(2,1)S(1)}, u32[]{:S(2)}, u32[]{:S(2)}) collective-permute-start(bf16[256,128]{1,0:T(8,128)(2,1)S(1)} %get-tuple-element.25), channel_id=1, source_target_pairs={{0,128},{1,192},{2,0},{3,64},{64,129},{65,193},{66,1},{67,65},{128... | collective-permute-start | bytes 196616 | tf_op jit(solution)/shard_map/ppermute | solution.py:184
  87.2 2.3 %collective-permute-start.9 = (bf16[256,128]{1,0:T(8,128)(2,1)S(1)}, bf16[256,128]{1,0:T(8,128)(2,1)S(1)}, u32[]{:S(2)}, u32[]{:S(2)}) collective-permute-start(bf16[256,128]{1,0:T(8,128)(2,1)S(1)} %get-tuple-element.26), channel_id=1, source_target_pairs={{0,192},{1,0},{2,64},{3,128},{64,193},{65,1},{66,65},{67,129},{128... | collective-permute-start | bytes 196616 | tf_op jit(solution)/shard_map/ppermute | solution.py:184
  89.5 0.6 collective-permute-done.6
  90.1 0.8 collective-permute-done.7
  90.9 2.0 %collective-permute-done.8 = bf16[256,128]{1,0:T(8,128)(2,1)S(1)} collective-permute-done((bf16[256,128]{1,0:T(8,128)(2,1)S(1)}, bf16[256,128]{1,0:T(8,128)(2,1)S(1)}, u32[]{:S(2)}, u32[]{:S(2)}) %collective-permute-start.8) | collective-permute-done | bytes 65568 | tf_op jit(solution)/shard_map/ppermute | solution.py:184
  92.9 6.3 %collective-permute-done.9 = bf16[256,128]{1,0:T(8,128)(2,1)S(1)} collective-permute-done((bf16[256,128]{1,0:T(8,128)(2,1)S(1)}, bf16[256,128]{1,0:T(8,128)(2,1)S(1)}, u32[]{:S(2)}, u32[]{:S(2)}) %collective-permute-start.9) | collective-permute-done | bytes 65568 | tf_op jit(solution)/shard_map/ppermute | solution.py:184
  99.2 0.7 add_convert_fusion
  (23 shorter events, 0.2 us)
Async XLA Ops:
  6.5 69.5 %all-gather.3.cloned.1.call-start = ((), (), s32[]{:S(2)}) async-start(), calls=%async_computation | async-start | bytes 2621440 | tf_op jit(solution)/shard_map/all_gather | solution.py:199
  8.1 4.4 %collective-permute-start.1 = (bf16[16,2560]{1,0:T(8,128)(2,1)S(1)}, bf16[16,2560]{1,0:T(8,128)(2,1)S(1)}, u32[]{:S(2)}, u32[]{:S(2)}) collective-permute-start(bf16[16,2560]{1,0:T(8,128)(2,1)S(1)} %maximum_bitcast_fusion.m0), channel_id=1, source_target_pairs={{0,8},{8,0},{1,9},{9,1},{2,10},{10,2},{3,11},{11,3},{4,12},{12,4},... | collective-permute-start | bytes 245768 | tf_op jit(solution)/shard_map/ppermute | solution.py:184
  8.2 10.0 %collective-permute-start = (bf16[16,2560]{1,0:T(8,128)(2,1)S(1)}, bf16[16,2560]{1,0:T(8,128)(2,1)S(1)}, u32[]{:S(2)}, u32[]{:S(2)}) collective-permute-start(bf16[16,2560]{1,0:T(8,128)(2,1)S(1)} %maximum_bitcast_fusion.m0), channel_id=1, source_target_pairs={{0,4},{4,0},{1,5},{5,1},{2,6},{6,2},{3,7},{7,3},{8,12},{12,8},{9,1... | collective-permute-start | bytes 245768 | tf_op jit(solution)/shard_map/ppermute | solution.py:184
  12.6 5.6 %collective-permute-start.2 = (bf16[16,2560]{1,0:T(8,128)(2,1)S(1)}, bf16[16,2560]{1,0:T(8,128)(2,1)S(1)}, u32[]{:S(2)}, u32[]{:S(2)}) collective-permute-start(bf16[16,2560]{1,0:T(8,128)(2,1)S(1)} %collective-permute-done.1.m2), channel_id=1, source_target_pairs={{0,4},{4,0},{1,5},{5,1},{2,6},{6,2},{3,7},{7,3},{8,12},{12,8},{9,1... | collective-permute-start | bytes 245768 | tf_op jit(solution)/shard_map/ppermute | solution.py:184
  18.2 1.6 %copy-start = (bf16[8,2,512,128]{3,2,1,0:T(8,128)(2,1)S(1)}, bf16[8,2,512,128]{3,2,1,0:T(8,128)(2,1)}, u32[]{:S(2)}) copy-start(bf16[8,2,512,128]{3,2,1,0:T(8,128)(2,1)} %key_ref.1) | copy-start | bytes 6291460
  19.8 1.6 %copy-start.1 = (bf16[8,2,512,128]{3,2,1,0:T(8,128)(2,1)S(1)}, bf16[8,2,512,128]{3,2,1,0:T(8,128)(2,1)}, u32[]{:S(2)}) copy-start(bf16[8,2,512,128]{3,2,1,0:T(8,128)(2,1)} %value_ref.1) | copy-start | bytes 6291460
  21.4 0.9 copy-start.3
  22.3 0.9 copy-start.4
  23.2 0.9 copy-start.5
  24.1 0.8 copy-start.6
  24.8 0.7 copy-start.7
  25.5 0.7 copy-start.9
  26.2 0.6 copy-start.10
  26.8 49.2 %copy-start.8 = (s32[5]{0:T(128)S(1)}, s32[5]{0:T(128)}, u32[]{:S(2)}) copy-start(s32[5]{0:T(128)} %stack.23.ids_ref) | copy-start | bytes 64
  33.3 1.4 %collective-permute-start.3 = (bf16[2,32,1024]{2,1,0:T(8,128)(2,1)S(1)}, bf16[2,32,1024]{2,1,0:T(8,128)(2,1)S(1)}, u32[]{:S(2)}, u32[]{:S(2)}) collective-permute-start(bf16[2,32,1024]{2,1,0:T(8,128)(2,1)S(1)} %get-tuple-element.22), channel_id=1, source_target_pairs={{0,4},{4,0},{1,5},{5,1},{2,6},{6,2},{3,7},{7,3},{8,12},{12,8},{9,1... | collective-permute-start | bytes 393224 | tf_op jit(solution)/shard_map/ppermute | solution.py:184
  34.8 4.4 %collective-permute-start.4 = (bf16[32,1024]{1,0:T(8,128)(2,1)S(1)}, bf16[32,1024]{1,0:T(8,128)(2,1)S(1)}, u32[]{:S(2)}, u32[]{:S(2)}) collective-permute-start(bf16[32,1024]{1,0:T(8,128)(2,1)S(1)} %slice_bitcast_fusion), channel_id=1, source_target_pairs={{0,8},{8,0},{1,9},{9,1},{2,10},{10,2},{3,11},{11,3},{4,12},{12,4},... | collective-permute-start | bytes 196616 | tf_op jit(solution)/shard_map/ppermute | solution.py:184
  74.1 1.9 %collective-permute-start.5 = (bf16[256,1024]{1,0:T(8,128)(2,1)S(1)}, bf16[256,1024]{1,0:T(8,128)(2,1)S(1)}, u32[]{:S(2)}, u32[]{:S(2)}) collective-permute-start(bf16[256,1024]{1,0:T(8,128)(2,1)S(1)} %all_gather.9.mine_ref), channel_id=1, source_target_pairs={{0,4},{4,0},{1,5},{5,1},{2,6},{6,2},{3,7},{7,3},{8,12},{12,8},{9,1... | collective-permute-start | bytes 1572872 | tf_op jit(solution)/shard_map/ppermute | solution.py:184
  76.0 1.6 %copy-start.2 = (bf16[8192,128]{1,0:T(8,128)(2,1)S(1)}, bf16[8192,128]{1,0:T(8,128)(2,1)}, u32[]{:S(2)}) copy-start(bf16[8192,128]{1,0:T(8,128)(2,1)} %all-gather.3.cloned.1.call-done) | copy-start | bytes 6291460
  79.4 10.7 %collective-permute-start.6 = (bf16[256,128]{1,0:T(8,128)(2,1)S(1)}, bf16[256,128]{1,0:T(8,128)(2,1)S(1)}, u32[]{:S(2)}, u32[]{:S(2)}) collective-permute-start(bf16[256,128]{1,0:T(8,128)(2,1)S(1)} %get-tuple-element.23), channel_id=1, source_target_pairs={{0,0},{1,64},{2,128},{3,192},{64,1},{65,65},{66,129},{67,193},{128... | collective-permute-start | bytes 196616 | tf_op jit(solution)/shard_map/ppermute | solution.py:184
  83.6 7.3 %collective-permute-start.7 = (bf16[256,128]{1,0:T(8,128)(2,1)S(1)}, bf16[256,128]{1,0:T(8,128)(2,1)S(1)}, u32[]{:S(2)}, u32[]{:S(2)}) collective-permute-start(bf16[256,128]{1,0:T(8,128)(2,1)S(1)} %get-tuple-element.24), channel_id=1, source_target_pairs={{0,64},{1,128},{2,192},{3,0},{64,65},{65,129},{66,193},{67,1},{128... | collective-permute-start | bytes 196616 | tf_op jit(solution)/shard_map/ppermute | solution.py:184
  86.1 6.8 %collective-permute-start.8 = (bf16[256,128]{1,0:T(8,128)(2,1)S(1)}, bf16[256,128]{1,0:T(8,128)(2,1)S(1)}, u32[]{:S(2)}, u32[]{:S(2)}) collective-permute-start(bf16[256,128]{1,0:T(8,128)(2,1)S(1)} %get-tuple-element.25), channel_id=1, source_target_pairs={{0,128},{1,192},{2,0},{3,64},{64,129},{65,193},{66,1},{67,65},{128... | collective-permute-start | bytes 196616 | tf_op jit(solution)/shard_map/ppermute | solution.py:184
  87.2 11.9 %collective-permute-start.9 = (bf16[256,128]{1,0:T(8,128)(2,1)S(1)}, bf16[256,128]{1,0:T(8,128)(2,1)S(1)}, u32[]{:S(2)}, u32[]{:S(2)}) collective-permute-start(bf16[256,128]{1,0:T(8,128)(2,1)S(1)} %get-tuple-element.26), channel_id=1, source_target_pairs={{0,192},{1,0},{2,64},{3,128},{64,193},{65,1},{66,65},{67,129},{128... | collective-permute-start | bytes 196616 | tf_op jit(solution)/shard_map/ppermute | solution.py:184
Sparse Core Ops, SparseCore 0:
  9.2 34.5 all-gather.2

commit v2 on v1

v2 whole, which is shorter than its diff:
```python
import math

import jax
import jax.numpy as jnp
from jax import lax
from jax.experimental import pallas as pl
from jax.experimental.pallas import tpu as pltpu
from jax.sharding import Mesh
from jax.sharding import PartitionSpec as P

FAMILY = 32
AXES = ("y", "zo", "zi", "c", "x")
SIZES = (4, 4, 2, 2, 4)
DP = ("y", "zo", "zi", "c")
Z = ("zo", "zi")

HOLD = 8
ITEMS = 64
CHUNKS = 16
SLOTS = CHUNKS * 8
KV = 2
GROUP = 8
HD = 128
HALF = GROUP * HD
FEAT = KV * HALF
WIDE = FEAT + 2 * KV * HD
CACHE = 512
NEG = -1e30

HBM = pl.BlockSpec(memory_space=pltpu.HBM)
VMEM = pl.BlockSpec(memory_space=pltpu.VMEM)
SMEM = pl.BlockSpec(memory_space=pltpu.SMEM)
F32 = jnp.float32
BF16 = jnp.bfloat16
LIMIT = pltpu.CompilerParams(vmem_limit_bytes=16 * 2**20)
TINY = pl.CostEstimate(flops=10**6, bytes_accessed=10**5, transcendentals=0)


def at(axis):
    return lax.axis_index(axis)


def plan_kernel(
    ancestors, lengths, key_ref, value_ref, w_ref,
    sort_ref, back_ref, chunk_ref, keys, values, w0,
    anc_ref, len_ref, count, current, sems,
):
    loads = [
        pltpu.make_async_copy(src, dst, sems.at[k])
        for k, (src, dst) in enumerate(
            ((ancestors, anc_ref), (lengths, len_ref), (key_ref, keys), (value_ref, values), (w_ref, w0))
        )
    ]
    for load in loads:
        load.start()
    zi, c = at("zi"), at("c")
    first = (at("y") * 4 + at("zo")) * FAMILY
    own = zi * 2 + c
    sort_ref[...] = jnp.zeros_like(sort_ref)
    for h in range(HOLD):
        count[h] = 0
        current[h] = 0
    for j in range(CHUNKS + 2):
        chunk_ref[j] = 0
    for load in loads[:2]:
        load.wait()
    for h in range(HOLD):
        chunk_ref[CHUNKS + 2 + h] = len_ref[h]
    lane = lax.broadcasted_iota(jnp.int32, (1, 128), 1)
    used = jnp.int32(0)
    for n in range(ITEMS):
        block, r, i = n // 16, (n // 8) % 2, n % 8
        place = (lax.bitwise_xor(zi, block // 2) * 2 + lax.bitwise_xor(c, block % 2)) * 8 + i
        particle = first + place
        if r:
            mother = anc_ref[1, particle]
            root = anc_ref[0, mother] - first
            mp = mother - first
            mn = (lax.bitwise_xor(mp >> 4, zi) * 2 + lax.bitwise_xor((mp >> 3) & 1, c)) * 16 + (mp & 7)
        else:
            root = anc_ref[0, particle] - first
        here = (root >> 3) == own
        h = root & 7
        seen = count[h]
        opens = jnp.logical_and(here, (seen & 7) == 0)
        chunk = jnp.where(opens, used, current[h])
        current[h] = chunk
        count[h] = seen + jnp.where(here, 1, 0)
        slot = jnp.where(here, chunk * 8 + (seen & 7), SLOTS)
        chunk_ref[jnp.where(opens, chunk, CHUNKS)] = h
        row = jnp.where(lane == n, 1.0, 0.0)
        if r:
            row = jnp.where(lane == mn + ITEMS, 1.0, row)
        sort_ref[pl.ds(slot, 1), :] = row
        back_ref[pl.ds(r * FAMILY + place, 1), :] = jnp.where(lane == slot, 1.0, 0.0)
        used = jnp.where(opens, used + 1, used)
    chunk_ref[CHUNKS + 1] = used
    for load in loads[2:]:
        load.wait()


def attend_kernel(
    plan, back, chunks, m0, m1, m2, m3, keys, values,
    keep0, keep1, give0, give1,
    message, ordered, mothers, answer,
):
    scale = math.log2(math.e) / math.sqrt(HD)
    zi, c = at("zi"), at("c")
    for b, m in enumerate((m0, m1, m2, m3)):
        message[b * 16 : b * 16 + 16, :] = m[...]
    answer[...] = jnp.zeros_like(answer)
    sort = plan[0:SLOTS, 0:ITEMS].astype(BF16)
    ordered[...] = jnp.dot(sort, message[...], preferred_element_type=F32)
    pick = plan[0:SLOTS, ITEMS : 2 * ITEMS].astype(BF16)
    mothers[...] = jnp.dot(pick, message[:, FEAT:], preferred_element_type=F32)
    places = lax.broadcasted_iota(jnp.int32, (1, CACHE), 1)
    lane = lax.broadcasted_iota(jnp.int32, (8, 128), 1)
    slot = lax.broadcasted_iota(jnp.int32, (8 * GROUP, 128), 0) & 7
    extra = lax.broadcasted_iota(jnp.int32, (8 * GROUP, 128), 1)
    is_own = extra == slot
    is_parent = extra == slot + 8
    blank = jnp.zeros((HD - 16, HD), F32)
    ones = jnp.ones((CACHE + HD, HD), BF16)

    def chunk(j):
        h = chunks[j]
        inside = places < chunks[CHUNKS + 2 + h]
        rows = pl.ds(pl.multiple_of(j * 8, 8), 8)
        has = jnp.sum(jnp.where(lane >= ITEMS, plan[rows, :], 0.0), axis=-1, keepdims=True)
        flag = jnp.concatenate([has] * GROUP, axis=0) > 0.5
        also = jnp.logical_or(is_own, jnp.logical_and(is_parent, flag))
        for g in range(KV):
            lo = g * HALF
            q = jnp.concatenate([ordered[rows, lo + k * HD : lo + (k + 1) * HD] for k in range(GROUP)], axis=0)
            q = q.astype(BF16)
            at_k, at_v = FEAT + g * HD, FEAT + (KV + g) * HD
            new_k = jnp.concatenate([ordered[rows, at_k : at_k + HD], mothers[rows, g * HD : (g + 1) * HD], blank])
            new_v = jnp.concatenate(
                [ordered[rows, at_v : at_v + HD], mothers[rows, (KV + g) * HD : (KV + g + 1) * HD], blank]
            )
            last = (((1,), (1,)), ((), ()))
            scores = lax.dot_general(q, keys[h, g], last, preferred_element_type=F32)
            new_s = lax.dot_general(q, new_k.astype(BF16), last, preferred_element_type=F32)
            scores = jnp.concatenate([jnp.where(inside, scores, NEG), jnp.where(also, new_s, NEG)], axis=1)
            top = jnp.max(scores, axis=-1, keepdims=True)
            weights = jnp.exp2(scores * scale - top * scale).astype(BF16)
            table = jnp.concatenate([values[h, g], new_v.astype(BF16)], axis=0)
            mixed = jnp.dot(weights, jnp.concatenate([table, ones], axis=1), preferred_element_type=F32)
            out = mixed[:, :HD] / mixed[:, HD:]
            for k in range(GROUP):
                answer[g, rows, k * HD : (k + 1) * HD] = out[k * 8 : k * 8 + 8]

    def body(p, carry):
        for u in range(4):
            chunk(4 * p + u)
        return carry

    lax.fori_loop(0, (chunks[CHUNKS + 1] + 3) // 4, body, 0)
    for cc, outs in ((0, (keep0, keep1)), (1, (give0, give1))):
        feats = answer[lax.bitwise_xor(c, cc)].astype(BF16)
        for zz, out in enumerate(outs):
            which = pl.ds(pl.multiple_of(lax.bitwise_xor(zi, zz) * FAMILY, FAMILY), FAMILY)
            out[...] = jnp.dot(back[which, :].astype(BF16), feats, preferred_element_type=F32).astype(BF16)


def halves_kernel(after_ref, w1, w3, lower_ref, upper_ref):
    lower_ref[...] = w1[:HALF]
    upper_ref[...] = w3[HALF:]


def spread_kernel(a_ref, b_ref, c_ref, d_ref, w2a, w2b, out_ref):
    total = (a_ref[...] + b_ref[...]) + (c_ref[...] + d_ref[...])
    for z in range(8):
        out_ref[z] = total


def half_rows(core):
    return pl.ds(pl.multiple_of(core * HALF, HALF), HALF)


def own_half_kernel(mine_ref, w0, w1, w2a, w2b, w3, acc_ref):
    c = at("c")
    rows = half_rows(c)
    for k, w in enumerate((w0[rows, :], w1[rows, :], jnp.where(c == 0, w2a[...], w2b[...]), w3[rows, :])):
        acc_ref[k] = jnp.dot(mine_ref[...], w, preferred_element_type=F32)


def other_half_kernel(other_ref, acc_ref, w0, w1, w2a, w2b, w3, o0, o1, o2, o3):
    c = at("c")
    rows = half_rows(1 - c)
    for k, w in enumerate((w0[rows, :], w1[rows, :], jnp.where(c == 0, w2b[...], w2a[...]), w3[rows, :])):
        total = acc_ref[k] + jnp.dot(other_ref[...], w, preferred_element_type=F32)
        total = total.astype(BF16)
        place = (at("y") - k - at("x")) & 3
        for s, out in enumerate((o0, o1, o2, o3)):

            @pl.when(place == s)
            def _(out=out, total=total):
                for zo in range(4):
                    for zi in range(2):
                        at_row = (zo * 2 + zi) * FAMILY
                        out[zi, zo * FAMILY : (zo + 1) * FAMILY, :] = total[at_row : at_row + FAMILY]


def permute(value, axes, move):
    sizes = [SIZES[AXES.index(a)] for a in axes]
    pairs = []
    for n in range(math.prod(sizes)):
        coords, rest = [], n
        for s in reversed(sizes):
            coords.append(rest % s)
            rest //= s
        flat = 0
        for t, s in zip(move(*reversed(coords)), sizes):
            flat = flat * s + t % s
        pairs.append((n, flat))
    return lax.ppermute(value, axes, pairs)


def swap_core(v):
    return permute(v, ("c",), lambda c: (1 - c,))


def swap_chip(v):
    return permute(v, ("zi",), lambda z: (1 - z,))


def swap_both(v):
    return permute(v, ("zi", "c"), lambda z, c: (1 - z, 1 - c))


def shape(*dims, dtype=BF16):
    return jax.ShapeDtypeStruct(dims, dtype)


def attend_call(*args):
    return pl.pallas_call(
        attend_kernel,
        out_shape=[shape(FAMILY, HALF)] * 4,
        in_specs=[VMEM, VMEM, SMEM] + [VMEM] * 6,
        out_specs=[VMEM] * 4,
        scratch_shapes=[
            pltpu.VMEM((ITEMS, WIDE), BF16),
            pltpu.VMEM((SLOTS, WIDE), F32),
            pltpu.VMEM((SLOTS, 2 * KV * HD), F32),
            pltpu.VMEM((KV, SLOTS, HALF), F32),
        ],
        compiler_params=LIMIT,
        cost_estimate=TINY,
        name="attend",
    )(*args)


def per_device(queries, key_cache, value_cache, new_keys, new_values, lengths, ancestors, out_weight):
    m0 = jnp.concatenate([queries, new_keys, new_values], axis=-1).reshape(2 * HOLD, WIDE)
    m3 = swap_both(m0)
    m2 = swap_chip(m0)
    m1 = swap_core(m0)
    w1 = permute(out_weight, ("y",), lambda y: (y + 1,))
    w3 = permute(out_weight, ("y",), lambda y: (y + 3,))
    sort, back, chunks, keys, values, w0 = pl.pallas_call(
        plan_kernel,
        out_shape=[
            shape(SLOTS + 8, 128, dtype=F32),
            shape(ITEMS, 128, dtype=F32),
            shape(CHUNKS + 2 + HOLD, dtype=jnp.int32),
            pltpu.VMEM(key_cache.shape, BF16),
            pltpu.VMEM(value_cache.shape, BF16),
            pltpu.VMEM(out_weight.shape, BF16),
        ],
        in_specs=[HBM] * 5,
        out_specs=[VMEM, VMEM, SMEM, VMEM, VMEM, VMEM],
        scratch_shapes=[
            pltpu.SMEM(ancestors.shape, jnp.int32),
            pltpu.SMEM((HOLD,), jnp.int32),
            pltpu.SMEM((HOLD,), jnp.int32),
            pltpu.SMEM((HOLD,), jnp.int32),
            pltpu.SemaphoreType.DMA((5,)),
        ],
        compiler_params=LIMIT,
        cost_estimate=TINY,
        name="plan",
    )(*(pltpu.with_memory_space_constraint(v, pltpu.HBM) for v in (ancestors, lengths, key_cache, value_cache, out_weight)))
    keep0, keep1, give0, give1 = attend_call(sort, back, chunks, m0, m1, m2, m3, keys, values)
    half = shape(HALF, 128)
    lower, upper = pl.pallas_call(
        halves_kernel,
        out_shape=[half, half],
        in_specs=[VMEM] * 3,
        out_specs=[VMEM] * 2,
        compiler_params=LIMIT,
        cost_estimate=TINY,
        name="halves",
    )(keep0, w1, w3)
    w2a = permute(lower, ("y",), lambda y: (y + 1,))
    w2b = permute(upper, ("y",), lambda y: (y + 3,))
    far = swap_both(give1)
    near = swap_chip(keep1)
    beside = swap_core(give0)
    spread = pl.pallas_call(
        spread_kernel,
        out_shape=shape(8, FAMILY, HALF),
        in_specs=[VMEM] * 6,
        out_specs=VMEM,
        compiler_params=pltpu.CompilerParams(vmem_limit_bytes=8 * 2**20),
        cost_estimate=pl.CostEstimate(flops=10**5, bytes_accessed=10**5, transcendentals=0),
        name="spread",
    )(keep0, far, near, beside, w2a, w2b)
    mine = lax.all_to_all(spread, Z, split_axis=0, concat_axis=0).reshape(8 * FAMILY, HALF)
    other = swap_core(mine)
    rows = 8 * FAMILY
    w_specs = [VMEM] * 5
    w = (w0, w1, w2a, w2b, w3)
    acc = pl.pallas_call(
        own_half_kernel,
        out_shape=shape(4, rows, 128, dtype=F32),
        in_specs=[VMEM] + w_specs,
        out_specs=VMEM,
        compiler_params=LIMIT,
        cost_estimate=pl.CostEstimate(flops=10**9, bytes_accessed=10**6, transcendentals=0),
        name="own_half",
    )(mine, *w)
    parts = pl.pallas_call(
        other_half_kernel,
        out_shape=[shape(2, rows // 2, 128)] * 4,
        in_specs=[VMEM, VMEM] + w_specs,
        out_specs=[VMEM] * 4,
        compiler_params=LIMIT,
        cost_estimate=pl.CostEstimate(flops=10**9, bytes_accessed=10**6, transcendentals=0),
        name="other_half",
    )(other, acc, *w)
    total = 0.0
    for k in (2, 1, 3, 0):
        total = total + permute(parts[k], ("y", "x"), lambda y, x, k=k: (x + k, y)).astype(F32)
    return total.astype(BF16)


def solution(mesh):
    fine = Mesh(mesh.devices.reshape(SIZES), AXES)
    in_specs = (
        P(None, DP, "x"),
        P(DP, "x", None, None),
        P(DP, "x", None, None),
        P(None, DP, "x"),
        P(None, DP, "x"),
        P(DP),
        P(),
        P("x", DP),
    )
    return jax.shard_map(
        per_device, mesh=fine, in_specs=in_specs, out_specs=P(None, "x", DP), check_vma=False
    )
```

time: 107 us -> 70.6 us (0.66)
  the two profiles are of different devices: /device:TPU:48 before, /device:TPU:6 now
where the time goes in v2:
time: 70.6 us; the launch traced here: 70.3 us
  blocking collectives  25.7 us (36%)
  starting transfers between devices  19.2 us (27%)
  waiting for transfers between devices  16.3 us (23%)
  Pallas kernels  7.49 us (11%)
  other arithmetic  1.55 us (2%)
    all_to_all x1, blocking collectives, per_device(): lax.all_to_all(spread, Z, split_axis=0, concat_axis=0)  25.7 us
    ppermute x15, starting transfers between devices, permute(): return lax.ppermute(value, axes, pairs)  19.2 us
    ppermute x15, waiting for transfers between devices, permute(): return lax.ppermute(value, axes, pairs)  16.3 us
    pallas_call x1, Pallas kernels, per_device(): pl.pallas_call(plan_kernel, out_shape=[shape(SLOTS + 8, 128, dtype=F32),...  2.94 us
    pallas_call x1, Pallas kernels, attend_call(): pl.pallas_call(attend_kernel, out_shape=[shape(FAMILY, HALF)] * 4, in_spe...  2.42 us
  transfers between devices with their start and end apart: 15, of which 8 were waited for; matrix products, arithmetic and copies ran while one was open for 1% of the time, Pallas kernels for 9%

profile of v2, /device:TPU:6, one launch (start us, length us, event | category | flops | bytes accessed | tf_op | source)
XLA Modules:
  0.0 70.3 jit_solution(2998074753142885187)
XLA Ops:
  0.0 1.6 %collective-permute-start.6 = (bf16[2048,128]{1,0:T(8,128)(2,1)}, bf16[2048,128]{1,0:T(8,128)(2,1)S(1)}, u32[]{:S(2)}, u32[]{:S(2)}) collective-permute-start(bf16[2048,128]{1,0:T(8,128)(2,1)} %w_ref.1), channel_id=1, source_target_pairs={{0,64},{64,128},{128,192},{192,0},{1,65},{65,129},{129,193},{193,1... | collective-permute-start | bytes 1572872 | tf_op jit(solution)/shard_map/ppermute | solution.py:217
  1.6 1.7 %collective-permute-start.7 = (bf16[2048,128]{1,0:T(8,128)(2,1)}, bf16[2048,128]{1,0:T(8,128)(2,1)S(1)}, u32[]{:S(2)}, u32[]{:S(2)}) collective-permute-start(bf16[2048,128]{1,0:T(8,128)(2,1)} %w_ref.1), channel_id=1, source_target_pairs={{0,192},{64,0},{128,64},{192,128},{1,193},{65,1},{129,65},{193,129... | collective-permute-start | bytes 1572872 | tf_op jit(solution)/shard_map/ppermute | solution.py:217
  3.2 0.9 %maximum_bitcast_fusion.m0 = bf16[16,2560]{1,0:T(8,128)(2,1)S(1)} fusion(bf16[2,8,256]{2,1,0:T(8,128)(2,1)} %param.12, bf16[2,8,256]{2,1,0:T(8,128)(2,1)} %param.11, bf16[2,8,2048]{2,1,0:T(8,128)(2,1)} %param.8), kind=kLoop, calls=%fused_computation.1 | loop fusion | flops 245760 | bytes 163840 | tf_op jit(solution)/shard_map/reshape | solution.py:255
  4.1 2.0 %collective-permute-start.1 = (bf16[16,2560]{1,0:T(8,128)(2,1)S(1)}, bf16[16,2560]{1,0:T(8,128)(2,1)S(1)}, u32[]{:S(2)}, u32[]{:S(2)}) collective-permute-start(bf16[16,2560]{1,0:T(8,128)(2,1)S(1)} %maximum_bitcast_fusion.m0), channel_id=1, source_target_pairs={{0,8},{8,0},{1,9},{9,1},{2,10},{10,2},{3,11},{11,3},{4,12},{12,4},... | collective-permute-start | bytes 245768 | tf_op jit(solution)/shard_map/ppermute | solution.py:217
  6.1 0.1 collective-permute-start.2
  6.2 2.9 %plan.1 = (f32[136,128]{1,0:T(8,128)S(1)}, f32[64,128]{1,0:T(8,128)S(1)}, s32[26]{0:T(128)S(1)}, bf16[8,2,512,128]{3,2,1,0:T(8,128)(2,1)S(1)}, bf16[8,2,512,128]...) custom-call(s32[2,512]{1,0:T(2,128)} %ancestors.1, s32[8]{0:T(128)} %lengths.1, bf16[8,2,512,128]{3,2,1,0:T(8,128)(2,1)} %key_ref.1, ...), custom_call_target="tpu_custom_call" | custom-call | flops 1000000 | bytes 100000 | tf_op jit(solution)/shard_map/plan/pallas_call | solution.py:261
  9.1 0.0 collective-permute-done.m1
  9.1 0.0 collective-permute-done.1.m2
  9.2 1.5 %collective-permute-done.2.m3 = bf16[16,2560]{1,0:T(8,128)(2,1)S(1)} collective-permute-done((bf16[16,2560]{1,0:T(8,128)(2,1)S(1)}, bf16[16,2560]{1,0:T(8,128)(2,1)S(1)}, u32[]{:S(2)}, u32[]{:S(2)}) %collective-permute-start.2) | collective-permute-done | bytes 81952 | tf_op jit(solution)/shard_map/ppermute | solution.py:217
  10.6 2.4 %attend.1 = (bf16[32,1024]{1,0:T(8,128)(2,1)S(1)}, bf16[32,1024]{1,0:T(8,128)(2,1)S(1)}, bf16[32,1024]{1,0:T(8,128)(2,1)S(1)}, bf16[32,1024]{1,0:T(8,128)(2,1)S(1)}) custom-call(f32[136,128]{1,0:T(8,128)S(1)} %get-tuple-element.21.plan, f32[64,128]{1,0:T(8,128)S(1)} %get-tuple-element.22.back, s32[26]{0:T(128)S(1)} %get-tuple-element.23.chunks, ...), custom_call_target="tpu_custom_call" | custom-call | flops 1000000 | bytes 100000 | tf_op jit(solution)/shard_map/attend/pallas_call | solution.py:237
  13.0 2.1 %collective-permute-done.6.w1 = bf16[2048,128]{1,0:T(8,128)(2,1)S(1)} collective-permute-done((bf16[2048,128]{1,0:T(8,128)(2,1)}, bf16[2048,128]{1,0:T(8,128)(2,1)S(1)}, u32[]{:S(2)}, u32[]{:S(2)}) %collective-permute-start.6) | collective-permute-done | bytes 524320 | tf_op jit(solution)/shard_map/ppermute | solution.py:217
  15.1 0.0 collective-permute-done.7.w3
  15.2 1.7 %collective-permute-start.8 = (bf16[1024,128]{1,0:T(8,128)(2,1)S(1)}, bf16[1024,128]{1,0:T(8,128)(2,1)S(1)}, u32[]{:S(2)}, u32[]{:S(2)}) collective-permute-start(bf16[1024,128]{1,0:T(8,128)(2,1)S(1)} %get-tuple-element.30), channel_id=1, source_target_pairs={{0,64},{64,128},{128,192},{192,0},{1,65},{65,129},{129,193},{193,1... | collective-permute-start | bytes 786440 | tf_op jit(solution)/shard_map/ppermute | solution.py:217
  16.9 1.7 %collective-permute-start.9 = (bf16[1024,128]{1,0:T(8,128)(2,1)S(1)}, bf16[1024,128]{1,0:T(8,128)(2,1)S(1)}, u32[]{:S(2)}, u32[]{:S(2)}) collective-permute-start(bf16[1024,128]{1,0:T(8,128)(2,1)S(1)} %get-tuple-element.31), channel_id=1, source_target_pairs={{0,192},{64,0},{128,64},{192,128},{1,193},{65,1},{129,65},{193,129... | collective-permute-start | bytes 786440 | tf_op jit(solution)/shard_map/ppermute | solution.py:217
  18.5 0.4 collective-permute-start.3
  18.9 1.6 %collective-permute-start.4 = (bf16[32,1024]{1,0:T(8,128)(2,1)S(1)}, bf16[32,1024]{1,0:T(8,128)(2,1)S(1)}, u32[]{:S(2)}, u32[]{:S(2)}) collective-permute-start(bf16[32,1024]{1,0:T(8,128)(2,1)S(1)} %get-tuple-element.28), channel_id=1, source_target_pairs={{0,8},{8,0},{1,9},{9,1},{2,10},{10,2},{3,11},{11,3},{4,12},{12,4},... | collective-permute-start | bytes 196616 | tf_op jit(solution)/shard_map/ppermute | solution.py:217
  20.5 0.1 collective-permute-start.5
  20.6 2.0 %collective-permute-done.3.b_ref = bf16[32,1024]{1,0:T(8,128)(2,1)S(1)} collective-permute-done((bf16[32,1024]{1,0:T(8,128)(2,1)S(1)}, bf16[32,1024]{1,0:T(8,128)(2,1)S(1)}, u32[]{:S(2)}, u32[]{:S(2)}) %collective-permute-start.3) | collective-permute-done | bytes 65568 | tf_op jit(solution)/shard_map/ppermute | solution.py:217
  22.5 1.5 %collective-permute-done.4.c_ref = bf16[32,1024]{1,0:T(8,128)(2,1)S(1)} collective-permute-done((bf16[32,1024]{1,0:T(8,128)(2,1)S(1)}, bf16[32,1024]{1,0:T(8,128)(2,1)S(1)}, u32[]{:S(2)}, u32[]{:S(2)}) %collective-permute-start.4) | collective-permute-done | bytes 65568 | tf_op jit(solution)/shard_map/ppermute | solution.py:217
  24.1 0.2 collective-permute-done.8.w2a
  24.3 25.7 %all_to_all.5 = bf16[8,32,1024]{2,1,0:T(8,128)(2,1)S(1)} all-to-all(bf16[8,32,1024]{2,1,0:T(8,128)(2,1)S(1)} %spread.1), channel_id=1, replica_groups=mesh['y'=4,'zo'=4,'zi'=2,'c'=2,'x'=4] {'zo','zi'}, dimensions={0} | all-to-all | bytes 1048576 | tf_op jit(solution)/shard_map/all_to_all | solution.py:309
  50.0 0.0 collective-permute-start.10
  50.0 0.7 %own_half.1.acc_ref = f32[4,256,128]{2,1,0:T(8,128)S(1)} custom-call(bf16[256,1024]{1,0:T(8,128)(2,1)S(1)} %bitcast.4, bf16[2048,128]{1,0:T(8,128)(2,1)S(1)} %get-tuple-element.32.w0, bf16[2048,128]{1,0:T(8,128)(2,1)S(1)} %collective-permute-done.6.w1, bf16[1024,128]{1,0:T(8,128)(2,1)S(1)} %collective-permute-done.8.w2a, ...), custom_call_target="tpu_custom_call" | custom-call | flops 1000000000 | bytes 1000000 | tf_op jit(solution)/shard_map/own_half/pallas_call | solution.py:314
  50.7 1.2 %collective-permute-done.10.other_ref = bf16[256,1024]{1,0:T(8,128)(2,1)S(1)} collective-permute-done((bf16[256,1024]{1,0:T(8,128)(2,1)S(1)}, bf16[256,1024]{1,0:T(8,128)(2,1)S(1)}, u32[]{:S(2)}, u32[]{:S(2)}) %collective-permute-start.10) | collective-permute-done | bytes 524320 | tf_op jit(solution)/shard_map/ppermute | solution.py:217
  51.9 1.3 %other_half.1 = (bf16[2,128,128]{2,1,0:T(8,128)(2,1)S(1)}, bf16[2,128,128]{2,1,0:T(8,128)(2,1)S(1)}, bf16[2,128,128]{2,1,0:T(8,128)(2,1)S(1)}, bf16[2,128,128]{2,1,0:T(8,128)(2,1)S(1)}) custom-call(bf16[256,1024]{1,0:T(8,128)(2,1)S(1)} %collective-permute-done.10.other_ref, f32[4,256,128]{2,1,0:T(8,128)S(1)} %own_half.1.acc_ref, ...), custom_call_target="tpu_custom_call" | custom-call | flops 1000000000 | bytes 1000000 | tf_op jit(solution)/shard_map/other_half/pallas_call | solution.py:323
  53.3 0.4 collective-permute-start.11
  53.6 1.9 %collective-permute-start.12 = (bf16[2,128,128]{2,1,0:T(8,128)(2,1)S(1)}, bf16[2,128,128]{2,1,0:T(8,128)(2,1)S(1)}, u32[]{:S(2)}, u32[]{:S(2)}) collective-permute-start(bf16[2,128,128]{2,1,0:T(8,128)(2,1)S(1)} %get-tuple-element.34), channel_id=1, source_target_pairs={{0,64},{1,128},{2,192},{3,0},{64,65},{65,129},{66,193},{67,1},{128... | collective-permute-start | bytes 196616 | tf_op jit(solution)/shard_map/ppermute | solution.py:217
  55.5 4.3 %collective-permute-start.13 = (bf16[2,128,128]{2,1,0:T(8,128)(2,1)S(1)}, bf16[2,128,128]{2,1,0:T(8,128)(2,1)S(1)}, u32[]{:S(2)}, u32[]{:S(2)}) collective-permute-start(bf16[2,128,128]{2,1,0:T(8,128)(2,1)S(1)} %get-tuple-element.35), channel_id=1, source_target_pairs={{0,192},{1,0},{2,64},{3,128},{64,193},{65,1},{66,65},{67,129},{128... | collective-permute-start | bytes 196616 | tf_op jit(solution)/shard_map/ppermute | solution.py:217
  59.8 2.0 %collective-permute-start.14 = (bf16[2,128,128]{2,1,0:T(8,128)(2,1)S(1)}, bf16[2,128,128]{2,1,0:T(8,128)(2,1)S(1)}, u32[]{:S(2)}, u32[]{:S(2)}) collective-permute-start(bf16[2,128,128]{2,1,0:T(8,128)(2,1)S(1)} %get-tuple-element.36), channel_id=1, source_target_pairs={{0,0},{1,64},{2,128},{3,192},{64,1},{65,65},{66,129},{67,193},{128... | collective-permute-start | bytes 196616 | tf_op jit(solution)/shard_map/ppermute | solution.py:217
  61.8 1.6 %collective-permute-done.13 = bf16[2,128,128]{2,1,0:T(8,128)(2,1)S(1)} collective-permute-done((bf16[2,128,128]{2,1,0:T(8,128)(2,1)S(1)}, bf16[2,128,128]{2,1,0:T(8,128)(2,1)S(1)}, u32[]{:S(2)}, u32[]{:S(2)}) %collective-permute-start.13) | collective-permute-done | bytes 65568 | tf_op jit(solution)/shard_map/ppermute | solution.py:217
  63.4 6.3 %collective-permute-done.14 = bf16[2,128,128]{2,1,0:T(8,128)(2,1)S(1)} collective-permute-done((bf16[2,128,128]{2,1,0:T(8,128)(2,1)S(1)}, bf16[2,128,128]{2,1,0:T(8,128)(2,1)S(1)}, u32[]{:S(2)}, u32[]{:S(2)}) %collective-permute-start.14) | collective-permute-done | bytes 65568 | tf_op jit(solution)/shard_map/ppermute | solution.py:217
  69.6 0.7 add_convert_fusion
  (7 shorter events, 0.1 us)
Async XLA Ops:
  0.0 15.1 %collective-permute-start.6 = (bf16[2048,128]{1,0:T(8,128)(2,1)}, bf16[2048,128]{1,0:T(8,128)(2,1)S(1)}, u32[]{:S(2)}, u32[]{:S(2)}) collective-permute-start(bf16[2048,128]{1,0:T(8,128)(2,1)} %w_ref.1), channel_id=1, source_target_pairs={{0,64},{64,128},{128,192},{192,0},{1,65},{65,129},{129,193},{193,1... | collective-permute-start | bytes 1572872 | tf_op jit(solution)/shard_map/ppermute | solution.py:217
  1.6 13.6 %collective-permute-start.7 = (bf16[2048,128]{1,0:T(8,128)(2,1)}, bf16[2048,128]{1,0:T(8,128)(2,1)S(1)}, u32[]{:S(2)}, u32[]{:S(2)}) collective-permute-start(bf16[2048,128]{1,0:T(8,128)(2,1)} %w_ref.1), channel_id=1, source_target_pairs={{0,192},{64,0},{128,64},{192,128},{1,193},{65,1},{129,65},{193,129... | collective-permute-start | bytes 1572872 | tf_op jit(solution)/shard_map/ppermute | solution.py:217
  4.1 5.0 %collective-permute-start = (bf16[16,2560]{1,0:T(8,128)(2,1)S(1)}, bf16[16,2560]{1,0:T(8,128)(2,1)S(1)}, u32[]{:S(2)}, u32[]{:S(2)}) collective-permute-start(bf16[16,2560]{1,0:T(8,128)(2,1)S(1)} %maximum_bitcast_fusion.m0), channel_id=1, source_target_pairs={{0,4},{4,0},{1,5},{5,1},{2,6},{6,2},{3,7},{7,3},{8,12},{12,8},{9,1... | collective-permute-start | bytes 245768 | tf_op jit(solution)/shard_map/ppermute | solution.py:217
  4.1 5.0 %collective-permute-start.1 = (bf16[16,2560]{1,0:T(8,128)(2,1)S(1)}, bf16[16,2560]{1,0:T(8,128)(2,1)S(1)}, u32[]{:S(2)}, u32[]{:S(2)}) collective-permute-start(bf16[16,2560]{1,0:T(8,128)(2,1)S(1)} %maximum_bitcast_fusion.m0), channel_id=1, source_target_pairs={{0,8},{8,0},{1,9},{9,1},{2,10},{10,2},{3,11},{11,3},{4,12},{12,4},... | collective-permute-start | bytes 245768 | tf_op jit(solution)/shard_map/ppermute | solution.py:217
  6.1 4.5 %collective-permute-start.2 = (bf16[16,2560]{1,0:T(8,128)(2,1)S(1)}, bf16[16,2560]{1,0:T(8,128)(2,1)S(1)}, u32[]{:S(2)}, u32[]{:S(2)}) collective-permute-start(bf16[16,2560]{1,0:T(8,128)(2,1)S(1)} %maximum_bitcast_fusion.m0), channel_id=1, source_target_pairs={{0,12},{4,8},{8,4},{12,0},{1,13},{5,9},{9,5},{13,1},{2,14},{6,10},... | collective-permute-start | bytes 245768 | tf_op jit(solution)/shard_map/ppermute | solution.py:217
  15.2 9.1 %collective-permute-start.8 = (bf16[1024,128]{1,0:T(8,128)(2,1)S(1)}, bf16[1024,128]{1,0:T(8,128)(2,1)S(1)}, u32[]{:S(2)}, u32[]{:S(2)}) collective-permute-start(bf16[1024,128]{1,0:T(8,128)(2,1)S(1)} %get-tuple-element.30), channel_id=1, source_target_pairs={{0,64},{64,128},{128,192},{192,0},{1,65},{65,129},{129,193},{193,1... | collective-permute-start | bytes 786440 | tf_op jit(solution)/shard_map/ppermute | solution.py:217
  16.9 7.4 %collective-permute-start.9 = (bf16[1024,128]{1,0:T(8,128)(2,1)S(1)}, bf16[1024,128]{1,0:T(8,128)(2,1)S(1)}, u32[]{:S(2)}, u32[]{:S(2)}) collective-permute-start(bf16[1024,128]{1,0:T(8,128)(2,1)S(1)} %get-tuple-element.31), channel_id=1, source_target_pairs={{0,192},{64,0},{128,64},{192,128},{1,193},{65,1},{129,65},{193,129... | collective-permute-start | bytes 786440 | tf_op jit(solution)/shard_map/ppermute | solution.py:217
  18.5 4.0 %collective-permute-start.3 = (bf16[32,1024]{1,0:T(8,128)(2,1)S(1)}, bf16[32,1024]{1,0:T(8,128)(2,1)S(1)}, u32[]{:S(2)}, u32[]{:S(2)}) collective-permute-start(bf16[32,1024]{1,0:T(8,128)(2,1)S(1)} %get-tuple-element.27), channel_id=1, source_target_pairs={{0,12},{4,8},{8,4},{12,0},{1,13},{5,9},{9,5},{13,1},{2,14},{6,10},... | collective-permute-start | bytes 196616 | tf_op jit(solution)/shard_map/ppermute | solution.py:217
  18.9 5.2 %collective-permute-start.4 = (bf16[32,1024]{1,0:T(8,128)(2,1)S(1)}, bf16[32,1024]{1,0:T(8,128)(2,1)S(1)}, u32[]{:S(2)}, u32[]{:S(2)}) collective-permute-start(bf16[32,1024]{1,0:T(8,128)(2,1)S(1)} %get-tuple-element.28), channel_id=1, source_target_pairs={{0,8},{8,0},{1,9},{9,1},{2,10},{10,2},{3,11},{11,3},{4,12},{12,4},... | collective-permute-start | bytes 196616 | tf_op jit(solution)/shard_map/ppermute | solution.py:217
  20.5 3.6 %collective-permute-start.5 = (bf16[32,1024]{1,0:T(8,128)(2,1)S(1)}, bf16[32,1024]{1,0:T(8,128)(2,1)S(1)}, u32[]{:S(2)}, u32[]{:S(2)}) collective-permute-start(bf16[32,1024]{1,0:T(8,128)(2,1)S(1)} %get-tuple-element.29), channel_id=1, source_target_pairs={{0,4},{4,0},{1,5},{5,1},{2,6},{6,2},{3,7},{7,3},{8,12},{12,8},{9,1... | collective-permute-start | bytes 196616 | tf_op jit(solution)/shard_map/ppermute | solution.py:217
  50.0 1.9 %collective-permute-start.10 = (bf16[256,1024]{1,0:T(8,128)(2,1)S(1)}, bf16[256,1024]{1,0:T(8,128)(2,1)S(1)}, u32[]{:S(2)}, u32[]{:S(2)}) collective-permute-start(bf16[256,1024]{1,0:T(8,128)(2,1)S(1)} %bitcast.3), channel_id=1, source_target_pairs={{0,4},{4,0},{1,5},{5,1},{2,6},{6,2},{3,7},{7,3},{8,12},{12,8},{9,1... | collective-permute-start | bytes 1572872 | tf_op jit(solution)/shard_map/ppermute | solution.py:217
  53.3 8.5 %collective-permute-start.11 = (bf16[2,128,128]{2,1,0:T(8,128)(2,1)S(1)}, bf16[2,128,128]{2,1,0:T(8,128)(2,1)S(1)}, u32[]{:S(2)}, u32[]{:S(2)}) collective-permute-start(bf16[2,128,128]{2,1,0:T(8,128)(2,1)S(1)} %get-tuple-element.33), channel_id=1, source_target_pairs={{0,128},{1,192},{2,0},{3,64},{64,129},{65,193},{66,1},{67,65},{128... | collective-permute-start | bytes 196616 | tf_op jit(solution)/shard_map/ppermute | solution.py:217
  53.6 8.2 %collective-permute-start.12 = (bf16[2,128,128]{2,1,0:T(8,128)(2,1)S(1)}, bf16[2,128,128]{2,1,0:T(8,128)(2,1)S(1)}, u32[]{:S(2)}, u32[]{:S(2)}) collective-permute-start(bf16[2,128,128]{2,1,0:T(8,128)(2,1)S(1)} %get-tuple-element.34), channel_id=1, source_target_pairs={{0,64},{1,128},{2,192},{3,0},{64,65},{65,129},{66,193},{67,1},{128... | collective-permute-start | bytes 196616 | tf_op jit(solution)/shard_map/ppermute | solution.py:217
  55.5 7.9 %collective-permute-start.13 = (bf16[2,128,128]{2,1,0:T(8,128)(2,1)S(1)}, bf16[2,128,128]{2,1,0:T(8,128)(2,1)S(1)}, u32[]{:S(2)}, u32[]{:S(2)}) collective-permute-start(bf16[2,128,128]{2,1,0:T(8,128)(2,1)S(1)} %get-tuple-element.35), channel_id=1, source_target_pairs={{0,192},{1,0},{2,64},{3,128},{64,193},{65,1},{66,65},{67,129},{128... | collective-permute-start | bytes 196616 | tf_op jit(solution)/shard_map/ppermute | solution.py:217
  59.8 9.9 %collective-permute-start.14 = (bf16[2,128,128]{2,1,0:T(8,128)(2,1)S(1)}, bf16[2,128,128]{2,1,0:T(8,128)(2,1)S(1)}, u32[]{:S(2)}, u32[]{:S(2)}) collective-permute-start(bf16[2,128,128]{2,1,0:T(8,128)(2,1)S(1)} %get-tuple-element.36), channel_id=1, source_target_pairs={{0,0},{1,64},{2,128},{3,192},{64,1},{65,65},{66,129},{67,193},{128... | collective-permute-start | bytes 196616 | tf_op jit(solution)/shard_map/ppermute | solution.py:217

commit v3 on v2

--- a/solution.py
+++ b/solution.py
@@ -163,15 +163,19 @@
             out[...] = jnp.dot(back[which, :].astype(BF16), feats, preferred_element_type=F32).astype(BF16)
 
 
-def halves_kernel(after_ref, w1, w3, lower_ref, upper_ref):
+def halves_kernel(w1, w3, lower_ref, upper_ref):
     lower_ref[...] = w1[:HALF]
     upper_ref[...] = w3[HALF:]
 
 
-def spread_kernel(a_ref, b_ref, c_ref, d_ref, w2a, w2b, out_ref):
+def spread_kernel(a_ref, b_ref, c_ref, d_ref, w1, w3, out_ref):
     total = (a_ref[...] + b_ref[...]) + (c_ref[...] + d_ref[...])
     for z in range(8):
         out_ref[z] = total
+
+
+def hold_kernel(mine_ref, w2a, w2b, out_ref):
+    pass
 
 
 def half_rows(core):
@@ -185,21 +189,18 @@
         acc_ref[k] = jnp.dot(mine_ref[...], w, preferred_element_type=F32)
 
 
-def other_half_kernel(other_ref, acc_ref, w0, w1, w2a, w2b, w3, o0, o1, o2, o3):
+def other_half_kernel(other_ref, acc_ref, w0, w1, w2a, w2b, w3, o0, o1, o2, o3, blocks):
     c = at("c")
     rows = half_rows(1 - c)
     for k, w in enumerate((w0[rows, :], w1[rows, :], jnp.where(c == 0, w2b[...], w2a[...]), w3[rows, :])):
         total = acc_ref[k] + jnp.dot(other_ref[...], w, preferred_element_type=F32)
         total = total.astype(BF16)
-        place = (at("y") - k - at("x")) & 3
-        for s, out in enumerate((o0, o1, o2, o3)):
-
-            @pl.when(place == s)
-            def _(out=out, total=total):
-                for zo in range(4):
-                    for zi in range(2):
-                        at_row = (zo * 2 + zi) * FAMILY
-                        out[zi, zo * FAMILY : (zo + 1) * FAMILY, :] = total[at_row : at_row + FAMILY]
+        for zo in range(4):
+            for zi in range(2):
+                at_row = (zo * 2 + zi) * FAMILY
+                blocks[k, zi, zo * FAMILY : (zo + 1) * FAMILY, :] = total[at_row : at_row + FAMILY]
+    for s, out in enumerate((o0, o1, o2, o3)):
+        out[...] = blocks[(at("y") - at("x") - s) & 3]
 
 
 def permute(value, axes, move):
@@ -253,9 +254,9 @@
 
 def per_device(queries, key_cache, value_cache, new_keys, new_values, lengths, ancestors, out_weight):
     m0 = jnp.concatenate([queries, new_keys, new_values], axis=-1).reshape(2 * HOLD, WIDE)
+    m1 = swap_core(m0)
+    m2 = swap_chip(m0)
     m3 = swap_both(m0)
-    m2 = swap_chip(m0)
-    m1 = swap_core(m0)
     w1 = permute(out_weight, ("y",), lambda y: (y + 1,))
     w3 = permute(out_weight, ("y",), lambda y: (y + 3,))
     sort, back, chunks, keys, values, w0 = pl.pallas_call(
@@ -286,12 +287,12 @@
     lower, upper = pl.pallas_call(
         halves_kernel,
         out_shape=[half, half],
-        in_specs=[VMEM] * 3,
+        in_specs=[VMEM] * 2,
         out_specs=[VMEM] * 2,
         compiler_params=LIMIT,
         cost_estimate=TINY,
         name="halves",
-    )(keep0, w1, w3)
+    )(w1, w3)
     w2a = permute(lower, ("y",), lambda y: (y + 1,))
     w2b = permute(upper, ("y",), lambda y: (y + 3,))
     far = swap_both(give1)
@@ -305,12 +306,22 @@
         compiler_params=pltpu.CompilerParams(vmem_limit_bytes=8 * 2**20),
         cost_estimate=pl.CostEstimate(flops=10**5, bytes_accessed=10**5, transcendentals=0),
         name="spread",
-    )(keep0, far, near, beside, w2a, w2b)
+    )(keep0, far, near, beside, w1, w3)
     mine = lax.all_to_all(spread, Z, split_axis=0, concat_axis=0).reshape(8 * FAMILY, HALF)
-    other = swap_core(mine)
     rows = 8 * FAMILY
     w_specs = [VMEM] * 5
     w = (w0, w1, w2a, w2b, w3)
+    mine = pl.pallas_call(
+        hold_kernel,
+        out_shape=shape(8 * FAMILY, HALF),
+        in_specs=[VMEM] * 3,
+        out_specs=VMEM,
+        input_output_aliases={0: 0},
+        compiler_params=LIMIT,
+        cost_estimate=TINY,
+        name="hold",
+    )(mine, w2a, w2b)
+    other = swap_core(mine)
     acc = pl.pallas_call(
         own_half_kernel,
         out_shape=shape(4, rows, 128, dtype=F32),
@@ -325,6 +336,7 @@
         out_shape=[shape(2, rows // 2, 128)] * 4,
         in_specs=[VMEM, VMEM] + w_specs,
         out_specs=[VMEM] * 4,
+        scratch_shapes=[pltpu.VMEM((4, 2, rows // 2, 128), BF16)],
         compiler_params=LIMIT,
         cost_estimate=pl.CostEstimate(flops=10**9, bytes_accessed=10**6, transcendentals=0),
         name="other_half",

time: 70.6 us -> 66.2 us (0.938)
  blocking collectives: 25.7 us -> 0 us
  waiting for transfers between devices: 16.3 us -> 28.2 us
  starting transfers between devices: 19.2 us -> 27.3 us
  Pallas kernels: 7.49 us -> 8.94 us
    all_to_all x1 -> x0, blocking collectives: 25.7 us -> none  [per_device(): lax.all_to_all(spread, Z, split_axis=0, concat_axis=0)]
    all_to_all x0 -> x1, waiting for transfers between devices: none -> 8.4 us  [per_device(): lax.all_to_all(spread, Z, split_axis=0, concat_axis=0)]
    all_to_all x0 -> x1, starting transfers between devices: none -> 8.16 us  [per_device(): lax.all_to_all(spread, Z, split_axis=0, concat_axis=0)]
    ppermute x15, waiting for transfers between devices: 16.3 us -> 19.8 us  [permute(): return lax.ppermute(value, axes, pairs)]
    pallas_call x1, Pallas kernels: 2.42 us -> 3.68 us  [attend_call(): pl.pallas_call(attend_kernel, out_shape=[shape(FAMILY, HALF)] * 4, in_spe...]
    pallas_call x1, Pallas kernels: 0.04 us -> 0.83 us  [per_device(): pl.pallas_call(spread_kernel, out_shape=shape(8, FAMILY, HALF), in_specs=...]
  transfers between devices with their start and end apart: 15 -> 16, of which waited for: 8 -> 8; matrix products, arithmetic and copies ran while one was open for 1% -> 1% of each run, Pallas kernels for 9% -> 11%
where the time goes in v3:
time: 66.2 us; the launch traced here: 66.1 us
  waiting for transfers between devices  28.2 us (43%)
  starting transfers between devices  27.3 us (41%)
  Pallas kernels  8.94 us (14%)
  other arithmetic  1.55 us (2%)
    ppermute x15, waiting for transfers between devices, permute(): return lax.ppermute(value, axes, pairs)  19.8 us
    ppermute x15, starting transfers between devices, permute(): return lax.ppermute(value, axes, pairs)  19.2 us
    all_to_all x1, waiting for transfers between devices, per_device(): lax.all_to_all(spread, Z, split_axis=0, concat_axis=0)  8.4 us
    all_to_all x1, starting transfers between devices, per_device(): lax.all_to_all(spread, Z, split_axis=0, concat_axis=0)  8.16 us
    pallas_call x1, Pallas kernels, attend_call(): pl.pallas_call(attend_kernel, out_shape=[shape(FAMILY, HALF)] * 4, in_spe...  3.68 us
    pallas_call x1, Pallas kernels, per_device(): pl.pallas_call(plan_kernel, out_shape=[shape(SLOTS + 8, 128, dtype=F32),...  2.94 us
  transfers between devices with their start and end apart: 16, of which 8 were waited for; matrix products, arithmetic and copies ran while one was open for 1% of the time, Pallas kernels for 11%

profile of v3, /device:TPU:6, one launch (start us, length us, event | category | flops | bytes accessed | tf_op | source)
XLA Modules:
  0.0 66.1 jit_solution(12404690648877558881)
XLA Ops:
  0.0 1.6 %collective-permute-start.6 = (bf16[2048,128]{1,0:T(8,128)(2,1)}, bf16[2048,128]{1,0:T(8,128)(2,1)S(1)}, u32[]{:S(2)}, u32[]{:S(2)}) collective-permute-start(bf16[2048,128]{1,0:T(8,128)(2,1)} %w_ref.1), channel_id=1, source_target_pairs={{0,64},{64,128},{128,192},{192,0},{1,65},{65,129},{129,193},{193,1... | collective-permute-start | bytes 1572872 | tf_op jit(solution)/shard_map/ppermute | solution.py:218
  1.6 1.7 %collective-permute-start.7 = (bf16[2048,128]{1,0:T(8,128)(2,1)}, bf16[2048,128]{1,0:T(8,128)(2,1)S(1)}, u32[]{:S(2)}, u32[]{:S(2)}) collective-permute-start(bf16[2048,128]{1,0:T(8,128)(2,1)} %w_ref.1), channel_id=1, source_target_pairs={{0,192},{64,0},{128,64},{192,128},{1,193},{65,1},{129,65},{193,129... | collective-permute-start | bytes 1572872 | tf_op jit(solution)/shard_map/ppermute | solution.py:218
  3.2 0.9 %maximum_bitcast_fusion.m0 = bf16[16,2560]{1,0:T(8,128)(2,1)S(1)} fusion(bf16[2,8,256]{2,1,0:T(8,128)(2,1)} %param.12, bf16[2,8,256]{2,1,0:T(8,128)(2,1)} %param.11, bf16[2,8,2048]{2,1,0:T(8,128)(2,1)} %param.8), kind=kLoop, calls=%fused_computation.1 | loop fusion | flops 245760 | bytes 163840 | tf_op jit(solution)/shard_map/reshape | solution.py:256
  4.1 2.0 %collective-permute-start.1 = (bf16[16,2560]{1,0:T(8,128)(2,1)S(1)}, bf16[16,2560]{1,0:T(8,128)(2,1)S(1)}, u32[]{:S(2)}, u32[]{:S(2)}) collective-permute-start(bf16[16,2560]{1,0:T(8,128)(2,1)S(1)} %maximum_bitcast_fusion.m0), channel_id=1, source_target_pairs={{0,8},{8,0},{1,9},{9,1},{2,10},{10,2},{3,11},{11,3},{4,12},{12,4},... | collective-permute-start | bytes 245768 | tf_op jit(solution)/shard_map/ppermute | solution.py:218
  6.1 0.1 collective-permute-start.2
  6.2 2.9 %plan.1 = (f32[136,128]{1,0:T(8,128)S(1)}, f32[64,128]{1,0:T(8,128)S(1)}, s32[26]{0:T(128)S(1)}, bf16[8,2,512,128]{3,2,1,0:T(8,128)(2,1)S(1)}, bf16[8,2,512,128]...) custom-call(s32[2,512]{1,0:T(2,128)} %ancestors.1, s32[8]{0:T(128)} %lengths.1, bf16[8,2,512,128]{3,2,1,0:T(8,128)(2,1)} %key_ref.1, ...), custom_call_target="tpu_custom_call" | custom-call | flops 1000000 | bytes 100000 | tf_op jit(solution)/shard_map/plan/pallas_call | solution.py:262
  9.1 0.0 collective-permute-done.m1
  9.1 0.0 collective-permute-done.1.m2
  9.2 1.5 %collective-permute-done.2.m3 = bf16[16,2560]{1,0:T(8,128)(2,1)S(1)} collective-permute-done((bf16[16,2560]{1,0:T(8,128)(2,1)S(1)}, bf16[16,2560]{1,0:T(8,128)(2,1)S(1)}, u32[]{:S(2)}, u32[]{:S(2)}) %collective-permute-start.2) | collective-permute-done | bytes 81952 | tf_op jit(solution)/shard_map/ppermute | solution.py:218
  10.6 3.7 %attend.1 = (bf16[32,1024]{1,0:T(8,128)(2,1)S(1)}, bf16[32,1024]{1,0:T(8,128)(2,1)S(1)}, bf16[32,1024]{1,0:T(8,128)(2,1)S(1)}, bf16[32,1024]{1,0:T(8,128)(2,1)S(1)}) custom-call(f32[136,128]{1,0:T(8,128)S(1)} %get-tuple-element.21.plan, f32[64,128]{1,0:T(8,128)S(1)} %get-tuple-element.22.back, s32[26]{0:T(128)S(1)} %get-tuple-element.23.chunks, ...), custom_call_target="tpu_custom_call" | custom-call | flops 1000000 | bytes 100000 | tf_op jit(solution)/shard_map/attend/pallas_call | solution.py:238
  14.3 0.6 collective-permute-start.3
  14.9 1.5 %collective-permute-start.4 = (bf16[32,1024]{1,0:T(8,128)(2,1)S(1)}, bf16[32,1024]{1,0:T(8,128)(2,1)S(1)}, u32[]{:S(2)}, u32[]{:S(2)}) collective-permute-start(bf16[32,1024]{1,0:T(8,128)(2,1)S(1)} %get-tuple-element.28), channel_id=1, source_target_pairs={{0,8},{8,0},{1,9},{9,1},{2,10},{10,2},{3,11},{11,3},{4,12},{12,4},... | collective-permute-start | bytes 196616 | tf_op jit(solution)/shard_map/ppermute | solution.py:218
  16.4 0.0 collective-permute-start.5
  16.4 1.8 %collective-permute-done.3.b_ref = bf16[32,1024]{1,0:T(8,128)(2,1)S(1)} collective-permute-done((bf16[32,1024]{1,0:T(8,128)(2,1)S(1)}, bf16[32,1024]{1,0:T(8,128)(2,1)S(1)}, u32[]{:S(2)}, u32[]{:S(2)}) %collective-permute-start.3) | collective-permute-done | bytes 65568 | tf_op jit(solution)/shard_map/ppermute | solution.py:218
  18.2 2.0 %collective-permute-done.4.c_ref = bf16[32,1024]{1,0:T(8,128)(2,1)S(1)} collective-permute-done((bf16[32,1024]{1,0:T(8,128)(2,1)S(1)}, bf16[32,1024]{1,0:T(8,128)(2,1)S(1)}, u32[]{:S(2)}, u32[]{:S(2)}) %collective-permute-start.4) | collective-permute-done | bytes 65568 | tf_op jit(solution)/shard_map/ppermute | solution.py:218
  20.2 0.8 %spread.1 = bf16[8,32,1024]{2,1,0:T(8,128)(2,1)} custom-call(bf16[32,1024]{1,0:T(8,128)(2,1)S(1)} %get-tuple-element.26.a_ref, bf16[32,1024]{1,0:T(8,128)(2,1)S(1)} %collective-permute-done.3.b_ref, bf16[32,1024]{1,0:T(8,128)(2,1)S(1)} %collective-permute-done.4.c_ref, bf16[32,1024]{1,0:T(8,128)(2,1)S(1)} %collective-permute-done.5.d_ref, ...), custom_call_target="tpu_custom_call" | custom-call | flops 100000 | bytes 100000 | tf_op jit(solution)/shard_map/spread/pallas_call | solution.py:301
  21.0 8.2 %all-to-all-start = ((bf16[8,32,1024]{2,1,0:T(8,128)(2,1)}), bf16[8,32,1024]{2,1,0:T(8,128)(2,1)S(1)}, u32[]{:S(2)}, u32[]{:S(2)}) async-start(bf16[8,32,1024]{2,1,0:T(8,128)(2,1)} %spread.1), calls=%async_computation | async-start | bytes 1048576 | tf_op jit(solution)/shard_map/all_to_all | solution.py:310
  29.2 0.1 collective-permute-start.8
  29.3 3.2 %collective-permute-start.9 = (bf16[1024,128]{1,0:T(8,128)(2,1)S(1)}, bf16[1024,128]{1,0:T(8,128)(2,1)S(1)}, u32[]{:S(2)}, u32[]{:S(2)}) collective-permute-start(bf16[1024,128]{1,0:T(8,128)(2,1)S(1)} %get-tuple-element.31), channel_id=1, source_target_pairs={{0,192},{64,0},{128,64},{192,128},{1,193},{65,1},{129,65},{193,129... | collective-permute-start | bytes 786440 | tf_op jit(solution)/shard_map/ppermute | solution.py:218
  32.5 5.0 %collective-permute-done.8.w2a = bf16[1024,128]{1,0:T(8,128)(2,1)S(1)} collective-permute-done((bf16[1024,128]{1,0:T(8,128)(2,1)S(1)}, bf16[1024,128]{1,0:T(8,128)(2,1)S(1)}, u32[]{:S(2)}, u32[]{:S(2)}) %collective-permute-start.8) | collective-permute-done | bytes 262176 | tf_op jit(solution)/shard_map/ppermute | solution.py:218
  37.6 0.0 collective-permute-done.9.w2b
  37.6 8.4 %all-to-all-done = bf16[8,32,1024]{2,1,0:T(8,128)(2,1)S(1)} async-done(((bf16[8,32,1024]{2,1,0:T(8,128)(2,1)}), bf16[8,32,1024]{2,1,0:T(8,128)(2,1)S(1)}, u32[]{:S(2)}, u32[]{:S(2)}) %all-to-all-start) | async-done | bytes 524320 | tf_op jit(solution)/shard_map/all_to_all | solution.py:310
  46.0 0.7 %own_half.1.acc_ref = f32[4,256,128]{2,1,0:T(8,128)S(1)} custom-call(bf16[256,1024]{1,0:T(8,128)(2,1)S(1)} %hold.1.mine_ref, bf16[2048,128]{1,0:T(8,128)(2,1)S(1)} %get-tuple-element.32.w0, bf16[2048,128]{1,0:T(8,128)(2,1)S(1)} %collective-permute-done.6.w1, bf16[1024,128]{1,0:T(8,128)(2,1)S(1)} %collective-permute-done.8.w2a, ...), custom_call_target="tpu_custom_call" | custom-call | flops 1000000000 | bytes 1000000 | tf_op jit(solution)/shard_map/own_half/pallas_call | solution.py:325
  46.7 1.2 %collective-permute-done.10.other_ref = bf16[256,1024]{1,0:T(8,128)(2,1)S(1)} collective-permute-done((bf16[256,1024]{1,0:T(8,128)(2,1)S(1)}, bf16[256,1024]{1,0:T(8,128)(2,1)S(1)}, u32[]{:S(2)}, u32[]{:S(2)}) %collective-permute-start.10) | collective-permute-done | bytes 524320 | tf_op jit(solution)/shard_map/ppermute | solution.py:218
  47.9 0.7 %other_half.1 = (bf16[2,128,128]{2,1,0:T(8,128)(2,1)S(1)}, bf16[2,128,128]{2,1,0:T(8,128)(2,1)S(1)}, bf16[2,128,128]{2,1,0:T(8,128)(2,1)S(1)}, bf16[2,128,128]{2,1,0:T(8,128)(2,1)S(1)}) custom-call(bf16[256,1024]{1,0:T(8,128)(2,1)S(1)} %collective-permute-done.10.other_ref, f32[4,256,128]{2,1,0:T(8,128)S(1)} %own_half.1.acc_ref, ...), custom_call_target="tpu_custom_call" | custom-call | flops 1000000000 | bytes 1000000 | tf_op jit(solution)/shard_map/other_half/pallas_call | solution.py:334
  48.6 0.1 collective-permute-start.11
  48.7 2.6 %collective-permute-start.12 = (bf16[2,128,128]{2,1,0:T(8,128)(2,1)S(1)}, bf16[2,128,128]{2,1,0:T(8,128)(2,1)S(1)}, u32[]{:S(2)}, u32[]{:S(2)}) collective-permute-start(bf16[2,128,128]{2,1,0:T(8,128)(2,1)S(1)} %get-tuple-element.34), channel_id=1, source_target_pairs={{0,64},{1,128},{2,192},{3,0},{64,65},{65,129},{66,193},{67,1},{128... | collective-permute-start | bytes 196616 | tf_op jit(solution)/shard_map/ppermute | solution.py:218
  51.3 3.9 %collective-permute-start.13 = (bf16[2,128,128]{2,1,0:T(8,128)(2,1)S(1)}, bf16[2,128,128]{2,1,0:T(8,128)(2,1)S(1)}, u32[]{:S(2)}, u32[]{:S(2)}) collective-permute-start(bf16[2,128,128]{2,1,0:T(8,128)(2,1)S(1)} %get-tuple-element.35), channel_id=1, source_target_pairs={{0,192},{1,0},{2,64},{3,128},{64,193},{65,1},{66,65},{67,129},{128... | collective-permute-start | bytes 196616 | tf_op jit(solution)/shard_map/ppermute | solution.py:218
  55.2 1.9 %collective-permute-start.14 = (bf16[2,128,128]{2,1,0:T(8,128)(2,1)S(1)}, bf16[2,128,128]{2,1,0:T(8,128)(2,1)S(1)}, u32[]{:S(2)}, u32[]{:S(2)}) collective-permute-start(bf16[2,128,128]{2,1,0:T(8,128)(2,1)S(1)} %get-tuple-element.36), channel_id=1, source_target_pairs={{0,0},{1,64},{2,128},{3,192},{64,1},{65,65},{66,129},{67,193},{128... | collective-permute-start | bytes 196616 | tf_op jit(solution)/shard_map/ppermute | solution.py:218
  57.1 2.1 %collective-permute-done.13 = bf16[2,128,128]{2,1,0:T(8,128)(2,1)S(1)} collective-permute-done((bf16[2,128,128]{2,1,0:T(8,128)(2,1)S(1)}, bf16[2,128,128]{2,1,0:T(8,128)(2,1)S(1)}, u32[]{:S(2)}, u32[]{:S(2)}) %collective-permute-start.13) | collective-permute-done | bytes 65568 | tf_op jit(solution)/shard_map/ppermute | solution.py:218
  59.2 6.3 %collective-permute-done.14 = bf16[2,128,128]{2,1,0:T(8,128)(2,1)S(1)} collective-permute-done((bf16[2,128,128]{2,1,0:T(8,128)(2,1)S(1)}, bf16[2,128,128]{2,1,0:T(8,128)(2,1)S(1)}, u32[]{:S(2)}, u32[]{:S(2)}) %collective-permute-start.14) | collective-permute-done | bytes 65568 | tf_op jit(solution)/shard_map/ppermute | solution.py:218
  65.4 0.7 %add_convert_fusion = bf16[2,128,128]{2,1,0:T(8,128)(2,1)} fusion(bf16[2,128,128]{2,1,0:T(8,128)(2,1)S(1)} %collective-permute-done.14, bf16[2,128,128]{2,1,0:T(8,128)(2,1)S(1)} %collective-permute-done.13, bf16[2,128,128]{2,1,0:T(8,128)(2,1)S(1)} %collective-permute-done.12, bf16[2,128,128]{2,1,0:T(8,128)(2,1)S(1)} %collective-permute-done.11), kind=kLoop, calls=%fused_computation | loop fusion | flops 262144 | bytes 327680 | tf_op jit(solution)/shard_map/convert_element_type | solution.py:347
  (9 shorter events, 0.1 us)
Async XLA Ops:
  0.0 20.2 %collective-permute-start.6 = (bf16[2048,128]{1,0:T(8,128)(2,1)}, bf16[2048,128]{1,0:T(8,128)(2,1)S(1)}, u32[]{:S(2)}, u32[]{:S(2)}) collective-permute-start(bf16[2048,128]{1,0:T(8,128)(2,1)} %w_ref.1), channel_id=1, source_target_pairs={{0,64},{64,128},{128,192},{192,0},{1,65},{65,129},{129,193},{193,1... | collective-permute-start | bytes 1572872 | tf_op jit(solution)/shard_map/ppermute | solution.py:218
  1.6 18.6 %collective-permute-start.7 = (bf16[2048,128]{1,0:T(8,128)(2,1)}, bf16[2048,128]{1,0:T(8,128)(2,1)S(1)}, u32[]{:S(2)}, u32[]{:S(2)}) collective-permute-start(bf16[2048,128]{1,0:T(8,128)(2,1)} %w_ref.1), channel_id=1, source_target_pairs={{0,192},{64,0},{128,64},{192,128},{1,193},{65,1},{129,65},{193,129... | collective-permute-start | bytes 1572872 | tf_op jit(solution)/shard_map/ppermute | solution.py:218
  4.1 5.0 %collective-permute-start = (bf16[16,2560]{1,0:T(8,128)(2,1)S(1)}, bf16[16,2560]{1,0:T(8,128)(2,1)S(1)}, u32[]{:S(2)}, u32[]{:S(2)}) collective-permute-start(bf16[16,2560]{1,0:T(8,128)(2,1)S(1)} %maximum_bitcast_fusion.m0), channel_id=1, source_target_pairs={{0,4},{4,0},{1,5},{5,1},{2,6},{6,2},{3,7},{7,3},{8,12},{12,8},{9,1... | collective-permute-start | bytes 245768 | tf_op jit(solution)/shard_map/ppermute | solution.py:218
  4.1 5.0 %collective-permute-start.1 = (bf16[16,2560]{1,0:T(8,128)(2,1)S(1)}, bf16[16,2560]{1,0:T(8,128)(2,1)S(1)}, u32[]{:S(2)}, u32[]{:S(2)}) collective-permute-start(bf16[16,2560]{1,0:T(8,128)(2,1)S(1)} %maximum_bitcast_fusion.m0), channel_id=1, source_target_pairs={{0,8},{8,0},{1,9},{9,1},{2,10},{10,2},{3,11},{11,3},{4,12},{12,4},... | collective-permute-start | bytes 245768 | tf_op jit(solution)/shard_map/ppermute | solution.py:218
  6.1 4.5 %collective-permute-start.2 = (bf16[16,2560]{1,0:T(8,128)(2,1)S(1)}, bf16[16,2560]{1,0:T(8,128)(2,1)S(1)}, u32[]{:S(2)}, u32[]{:S(2)}) collective-permute-start(bf16[16,2560]{1,0:T(8,128)(2,1)S(1)} %maximum_bitcast_fusion.m0), channel_id=1, source_target_pairs={{0,12},{4,8},{8,4},{12,0},{1,13},{5,9},{9,5},{13,1},{2,14},{6,10},... | collective-permute-start | bytes 245768 | tf_op jit(solution)/shard_map/ppermute | solution.py:218
  14.3 3.9 %collective-permute-start.3 = (bf16[32,1024]{1,0:T(8,128)(2,1)S(1)}, bf16[32,1024]{1,0:T(8,128)(2,1)S(1)}, u32[]{:S(2)}, u32[]{:S(2)}) collective-permute-start(bf16[32,1024]{1,0:T(8,128)(2,1)S(1)} %get-tuple-element.27), channel_id=1, source_target_pairs={{0,12},{4,8},{8,4},{12,0},{1,13},{5,9},{9,5},{13,1},{2,14},{6,10},... | collective-permute-start | bytes 196616 | tf_op jit(solution)/shard_map/ppermute | solution.py:218
  14.9 5.3 %collective-permute-start.4 = (bf16[32,1024]{1,0:T(8,128)(2,1)S(1)}, bf16[32,1024]{1,0:T(8,128)(2,1)S(1)}, u32[]{:S(2)}, u32[]{:S(2)}) collective-permute-start(bf16[32,1024]{1,0:T(8,128)(2,1)S(1)} %get-tuple-element.28), channel_id=1, source_target_pairs={{0,8},{8,0},{1,9},{9,1},{2,10},{10,2},{3,11},{11,3},{4,12},{12,4},... | collective-permute-start | bytes 196616 | tf_op jit(solution)/shard_map/ppermute | solution.py:218
  16.4 3.7 %collective-permute-start.5 = (bf16[32,1024]{1,0:T(8,128)(2,1)S(1)}, bf16[32,1024]{1,0:T(8,128)(2,1)S(1)}, u32[]{:S(2)}, u32[]{:S(2)}) collective-permute-start(bf16[32,1024]{1,0:T(8,128)(2,1)S(1)} %get-tuple-element.29), channel_id=1, source_target_pairs={{0,4},{4,0},{1,5},{5,1},{2,6},{6,2},{3,7},{7,3},{8,12},{12,8},{9,1... | collective-permute-start | bytes 196616 | tf_op jit(solution)/shard_map/ppermute | solution.py:218
  21.0 25.0 %all-to-all-start = ((bf16[8,32,1024]{2,1,0:T(8,128)(2,1)}), bf16[8,32,1024]{2,1,0:T(8,128)(2,1)S(1)}, u32[]{:S(2)}, u32[]{:S(2)}) async-start(bf16[8,32,1024]{2,1,0:T(8,128)(2,1)} %spread.1), calls=%async_computation | async-start | bytes 1048576 | tf_op jit(solution)/shard_map/all_to_all | solution.py:310
  29.2 8.3 %collective-permute-start.8 = (bf16[1024,128]{1,0:T(8,128)(2,1)S(1)}, bf16[1024,128]{1,0:T(8,128)(2,1)S(1)}, u32[]{:S(2)}, u32[]{:S(2)}) collective-permute-start(bf16[1024,128]{1,0:T(8,128)(2,1)S(1)} %get-tuple-element.30), channel_id=1, source_target_pairs={{0,64},{64,128},{128,192},{192,0},{1,65},{65,129},{129,193},{193,1... | collective-permute-start | bytes 786440 | tf_op jit(solution)/shard_map/ppermute | solution.py:218
  29.3 8.3 %collective-permute-start.9 = (bf16[1024,128]{1,0:T(8,128)(2,1)S(1)}, bf16[1024,128]{1,0:T(8,128)(2,1)S(1)}, u32[]{:S(2)}, u32[]{:S(2)}) collective-permute-start(bf16[1024,128]{1,0:T(8,128)(2,1)S(1)} %get-tuple-element.31), channel_id=1, source_target_pairs={{0,192},{64,0},{128,64},{192,128},{1,193},{65,1},{129,65},{193,129... | collective-permute-start | bytes 786440 | tf_op jit(solution)/shard_map/ppermute | solution.py:218
  46.0 1.9 %collective-permute-start.10 = (bf16[256,1024]{1,0:T(8,128)(2,1)S(1)}, bf16[256,1024]{1,0:T(8,128)(2,1)S(1)}, u32[]{:S(2)}, u32[]{:S(2)}) collective-permute-start(bf16[256,1024]{1,0:T(8,128)(2,1)S(1)} %hold.1.mine_ref), channel_id=1, source_target_pairs={{0,4},{4,0},{1,5},{5,1},{2,6},{6,2},{3,7},{7,3},{8,12},{12,8},{9,1... | collective-permute-start | bytes 1572872 | tf_op jit(solution)/shard_map/ppermute | solution.py:218
  48.6 8.4 %collective-permute-start.11 = (bf16[2,128,128]{2,1,0:T(8,128)(2,1)S(1)}, bf16[2,128,128]{2,1,0:T(8,128)(2,1)S(1)}, u32[]{:S(2)}, u32[]{:S(2)}) collective-permute-start(bf16[2,128,128]{2,1,0:T(8,128)(2,1)S(1)} %get-tuple-element.33), channel_id=1, source_target_pairs={{0,128},{1,192},{2,0},{3,64},{64,129},{65,193},{66,1},{67,65},{128... | collective-permute-start | bytes 196616 | tf_op jit(solution)/shard_map/ppermute | solution.py:218
  48.7 8.4 %collective-permute-start.12 = (bf16[2,128,128]{2,1,0:T(8,128)(2,1)S(1)}, bf16[2,128,128]{2,1,0:T(8,128)(2,1)S(1)}, u32[]{:S(2)}, u32[]{:S(2)}) collective-permute-start(bf16[2,128,128]{2,1,0:T(8,128)(2,1)S(1)} %get-tuple-element.34), channel_id=1, source_target_pairs={{0,64},{1,128},{2,192},{3,0},{64,65},{65,129},{66,193},{67,1},{128... | collective-permute-start | bytes 196616 | tf_op jit(solution)/shard_map/ppermute | solution.py:218
  51.3 7.9 %collective-permute-start.13 = (bf16[2,128,128]{2,1,0:T(8,128)(2,1)S(1)}, bf16[2,128,128]{2,1,0:T(8,128)(2,1)S(1)}, u32[]{:S(2)}, u32[]{:S(2)}) collective-permute-start(bf16[2,128,128]{2,1,0:T(8,128)(2,1)S(1)} %get-tuple-element.35), channel_id=1, source_target_pairs={{0,192},{1,0},{2,64},{3,128},{64,193},{65,1},{66,65},{67,129},{128... | collective-permute-start | bytes 196616 | tf_op jit(solution)/shard_map/ppermute | solution.py:218
  55.2 10.3 %collective-permute-start.14 = (bf16[2,128,128]{2,1,0:T(8,128)(2,1)S(1)}, bf16[2,128,128]{2,1,0:T(8,128)(2,1)S(1)}, u32[]{:S(2)}, u32[]{:S(2)}) collective-permute-start(bf16[2,128,128]{2,1,0:T(8,128)(2,1)S(1)} %get-tuple-element.36), channel_id=1, source_target_pairs={{0,0},{1,64},{2,128},{3,192},{64,1},{65,65},{66,129},{67,193},{128... | collective-permute-start | bytes 196616 | tf_op jit(solution)/shard_map/ppermute | solution.py:218

commit v4 on v3

v4 whole, which is shorter than its diff:
```python
import math

import jax
import jax.numpy as jnp
from jax import lax
from jax.experimental import pallas as pl
from jax.experimental.pallas import tpu as pltpu
from jax.sharding import Mesh
from jax.sharding import PartitionSpec as P

FAMILY = 32
AXES = ("y", "zo", "zi", "c", "x")
SIZES = (4, 4, 2, 2, 4)
DP = ("y", "zo", "zi", "c")
Z = ("zo", "zi")

HOLD = 8
ITEMS = 64
CHUNKS = 16
SLOTS = CHUNKS * 8
KV = 2
GROUP = 8
HD = 128
HALF = GROUP * HD
FEAT = KV * HALF
WIDE = FEAT + 2 * KV * HD
CACHE = 512
NEG = -1e30

HBM = pl.BlockSpec(memory_space=pltpu.HBM)
VMEM = pl.BlockSpec(memory_space=pltpu.VMEM)
SMEM = pl.BlockSpec(memory_space=pltpu.SMEM)
F32 = jnp.float32
BF16 = jnp.bfloat16
LIMIT = pltpu.CompilerParams(vmem_limit_bytes=16 * 2**20)
TINY = pl.CostEstimate(flops=10**6, bytes_accessed=10**5, transcendentals=0)


def at(axis):
    return lax.axis_index(axis)


def plan_kernel(
    ancestors, lengths, key_ref, value_ref, w_ref,
    sort_ref, back_ref, chunk_ref, keys, values, w0,
    anc_ref, len_ref, free, sems,
):
    loads = [
        pltpu.make_async_copy(src, dst, sems.at[k])
        for k, (src, dst) in enumerate(
            ((ancestors, anc_ref), (lengths, len_ref), (key_ref, keys), (value_ref, values), (w_ref, w0))
        )
    ]
    for load in loads:
        load.start()
    first = (at("y") * 4 + at("zo")) * FAMILY
    own = at("zi") * 2 + at("c")
    sort_ref[...] = jnp.zeros_like(sort_ref)
    for j in range(CHUNKS + 2):
        chunk_ref[j] = 0
    for h in range(HOLD):
        free[h] = 0
    free[HOLD] = SLOTS + 1
    lane = lax.broadcasted_iota(jnp.int32, (1, 128), 1)
    used = jnp.int32(0)
    for load in loads[:2]:
        load.wait()
    for h in range(HOLD):
        chunk_ref[CHUNKS + 2 + h] = len_ref[h]
    for block in range(4):
        place = lax.bitwise_xor(own, block) * 8
        for r in range(2):
            for i in range(8):
                n = block * 16 + r * 8 + i
                row = lane == n
                source = first + place + i
                if r:
                    source = anc_ref[1, source]
                    mp = source - first
                    row = jnp.logical_or(row, lane == lax.bitwise_xor(mp >> 3, own) * 16 + (mp & 7) + ITEMS)
                root = anc_ref[0, source] - first
                here = (root >> 3) == own
                h = jnp.where(here, root & 7, HOLD)
                slot = free[h]
                opens = (slot & 7) == 0
                slot = jnp.where(opens, used * 8, slot)
                free[h] = slot + jnp.where(here, 1, 0)
                chunk_ref[jnp.where(opens, used, CHUNKS)] = h
                used = used + jnp.where(opens, 1, 0)
                sort_ref[pl.ds(slot, 1), :] = jnp.where(row, 1.0, 0.0)
                back_ref[pl.ds(r * FAMILY + place + i, 1), :] = jnp.where(lane == slot, 1.0, 0.0)
    chunk_ref[CHUNKS + 1] = used
    for load in loads[2:]:
        load.wait()


def attend_kernel(
    plan, back, chunks, m0, m1, m2, m3, keys, values,
    keep0, keep1, give0, give1,
    message, ordered, mothers, answer,
):
    scale = math.log2(math.e) / math.sqrt(HD)
    zi, c = at("zi"), at("c")
    for b, m in enumerate((m0, m1, m2, m3)):
        message[b * 16 : b * 16 + 16, :] = m[...]
    answer[...] = jnp.zeros_like(answer)
    sort = plan[0:SLOTS, 0:ITEMS].astype(BF16)
    ordered[...] = jnp.dot(sort, message[...], preferred_element_type=F32)
    pick = plan[0:SLOTS, ITEMS : 2 * ITEMS].astype(BF16)
    mothers[...] = jnp.dot(pick, message[:, FEAT:], preferred_element_type=F32)
    places = lax.broadcasted_iota(jnp.int32, (1, CACHE), 1)
    lane = lax.broadcasted_iota(jnp.int32, (8, 128), 1)
    slot = lax.broadcasted_iota(jnp.int32, (8 * GROUP, 128), 0) & 7
    extra = lax.broadcasted_iota(jnp.int32, (8 * GROUP, 128), 1)
    ones = jnp.ones((HD, HD), BF16)
    last = (((1,), (1,)), ((), ()))

    def body(p, carry):
        jobs = []
        for u in range(4):
            j = 4 * p + u
            h = chunks[j]
            inside = places < chunks[CHUNKS + 2 + h]
            rows = pl.ds(pl.multiple_of(j * 8, 8), 8)
            has = jnp.sum(jnp.where(lane >= ITEMS, plan[rows, :], 0.0), axis=-1, keepdims=True)
            flag = jnp.concatenate([has] * GROUP, axis=0) > 0.5
            for g in range(KV):
                lo = g * HALF
                q = jnp.concatenate([ordered[rows, lo + k * HD : lo + (k + 1) * HD] for k in range(GROUP)], axis=0)
                at_k, at_v = FEAT + g * HD, FEAT + (KV + g) * HD
                new_k = [ordered[rows, at_k : at_k + HD], mothers[rows, g * HD : (g + 1) * HD]]
                new_v = [ordered[rows, at_v : at_v + HD], mothers[rows, (KV + g) * HD : (KV + g + 1) * HD]]
                base = 16 * len(jobs)
                also = jnp.logical_or(extra == slot + base, jnp.logical_and(extra == slot + base + 8, flag))
                jobs.append((h, g, rows, inside, also, q.astype(BF16), new_k, new_v))
        new_k = jnp.concatenate([v for job in jobs for v in job[6]]).astype(BF16)
        new_v = jnp.concatenate([v for job in jobs for v in job[7]]).astype(BF16)
        new_s = lax.dot_general(
            jnp.concatenate([job[5] for job in jobs]), new_k, last, preferred_element_type=F32
        )
        mixes, new_w, folded, rest = [], [], [], []
        for w, (h, g, rows, inside, also, q, _, _) in enumerate(jobs):
            scores = lax.dot_general(q, keys[h, g], last, preferred_element_type=F32)
            fresh = new_s[w * 8 * GROUP : (w + 1) * 8 * GROUP]
            scores = jnp.concatenate([jnp.where(inside, scores, NEG), jnp.where(also, fresh, NEG)], axis=1)
            top = jnp.max(scores, axis=-1, keepdims=True)
            weights = jnp.exp2(scores * scale - top * scale).astype(BF16)
            parts = [weights[:, n * 128 : (n + 1) * 128].astype(F32) for n in range(5)]
            total = ((parts[0] + parts[1]) + (parts[2] + parts[3])) + parts[4]
            folded.append(total.astype(BF16))
            rest.append((total - folded[-1].astype(F32)).astype(BF16))
            mixes.append(jnp.dot(weights[:, :CACHE], values[h, g], preferred_element_type=F32))
            new_w.append(weights[:, CACHE:])
        new_mix = jnp.dot(jnp.concatenate(new_w), new_v, preferred_element_type=F32)
        mass = jnp.dot(jnp.concatenate(folded), ones, preferred_element_type=F32)
        mass += jnp.dot(jnp.concatenate(rest), ones, preferred_element_type=F32)
        for w, (h, g, rows, _, _, _, _, _) in enumerate(jobs):
            mine = slice(w * 8 * GROUP, (w + 1) * 8 * GROUP)
            out = (mixes[w] + new_mix[mine]) / mass[mine]
            for k in range(GROUP):
                answer[g, rows, k * HD : (k + 1) * HD] = out[k * 8 : k * 8 + 8]
        return carry

    lax.fori_loop(0, (chunks[CHUNKS + 1] + 3) // 4, body, 0)
    which = [pl.ds(pl.multiple_of(lax.bitwise_xor(zi, zz) * FAMILY, FAMILY), FAMILY) for zz in range(2)]
    turn = jnp.concatenate([back[w, :] for w in which]).astype(BF16)
    for cc, outs in ((0, (keep0, keep1)), (1, (give0, give1))):
        feats = answer[lax.bitwise_xor(c, cc)].astype(BF16)
        both = jnp.dot(turn, feats, preferred_element_type=F32).astype(BF16)
        for zz, out in enumerate(outs):
            out[...] = both[zz * FAMILY : (zz + 1) * FAMILY]


def spread_kernel(a_ref, b_ref, c_ref, d_ref, w1, w3, out_ref):
    total = (a_ref[...] + b_ref[...]) + (c_ref[...] + d_ref[...])
    for z in range(8):
        out_ref[z] = total


def hold_kernel(*refs):
    pass


def half_rows(core):
    return pl.ds(pl.multiple_of(core * HALF, HALF), HALF)


def own_half_kernel(mine_ref, w0, w1, w2, w3, acc_ref):
    rows = half_rows(at("c"))
    for k, w in enumerate((w0, w1, w2, w3)):
        acc_ref[k] = jnp.dot(mine_ref[...], w[rows, :], preferred_element_type=F32)


def other_half_kernel(other_ref, acc_ref, w0, w1, w2, w3, o0, o1, o2, o3, blocks):
    c = at("c")
    rows = half_rows(1 - c)
    for k, w in enumerate((w0, w1, w2, w3)):
        total = acc_ref[k] + jnp.dot(other_ref[...], w[rows, :], preferred_element_type=F32)
        total = total.astype(BF16)
        where = jnp.where(c == 0, k, (4 - k) & 3)
        for zo in range(4):
            for zi in range(2):
                at_row = (zo * 2 + zi) * FAMILY
                blocks[where, zi, zo * FAMILY : (zo + 1) * FAMILY, :] = total[at_row : at_row + FAMILY]
    for s, out in enumerate((o0, o1, o2, o3)):
        out[...] = blocks[(at("y") - at("x") - s) & 3]


def permute(value, axes, move):
    sizes = [SIZES[AXES.index(a)] for a in axes]
    pairs = []
    for n in range(math.prod(sizes)):
        coords, rest = [], n
        for s in reversed(sizes):
            coords.append(rest % s)
            rest //= s
        flat = 0
        for t, s in zip(move(*reversed(coords)), sizes):
            flat = flat * s + t % s
        pairs.append((n, flat))
    return lax.ppermute(value, axes, pairs)


def swap_core(v):
    return permute(v, ("c",), lambda c: (1 - c,))


def swap_chip(v):
    return permute(v, ("zi",), lambda z: (1 - z,))


def swap_both(v):
    return permute(v, ("zi", "c"), lambda z, c: (1 - z, 1 - c))


def shape(*dims, dtype=BF16):
    return jax.ShapeDtypeStruct(dims, dtype)


def attend_call(*args):
    return pl.pallas_call(
        attend_kernel,
        out_shape=[shape(FAMILY, HALF)] * 4,
        in_specs=[VMEM, VMEM, SMEM] + [VMEM] * 6,
        out_specs=[VMEM] * 4,
        scratch_shapes=[
            pltpu.VMEM((ITEMS, WIDE), BF16),
            pltpu.VMEM((SLOTS, WIDE), F32),
            pltpu.VMEM((SLOTS, 2 * KV * HD), F32),
            pltpu.VMEM((KV, SLOTS, HALF), F32),
        ],
        compiler_params=LIMIT,
        cost_estimate=TINY,
        name="attend",
    )(*args)


def per_device(queries, key_cache, value_cache, new_keys, new_values, lengths, ancestors, out_weight):
    m0 = jnp.concatenate([queries, new_keys, new_values], axis=-1).reshape(2 * HOLD, WIDE)
    m1 = swap_core(m0)
    m2 = swap_chip(m0)
    sort, back, chunks, keys, values, w0 = pl.pallas_call(
        plan_kernel,
        out_shape=[
            shape(SLOTS + 8, 128, dtype=F32),
            shape(ITEMS, 128, dtype=F32),
            shape(CHUNKS + 2 + HOLD, dtype=jnp.int32),
            pltpu.VMEM(key_cache.shape, BF16),
            pltpu.VMEM(value_cache.shape, BF16),
            pltpu.VMEM(out_weight.shape, BF16),
        ],
        in_specs=[HBM] * 5,
        out_specs=[VMEM, VMEM, SMEM, VMEM, VMEM, VMEM],
        scratch_shapes=[
            pltpu.SMEM(ancestors.shape, jnp.int32),
            pltpu.SMEM((HOLD,), jnp.int32),
            pltpu.SMEM((HOLD + 1,), jnp.int32),
            pltpu.SemaphoreType.DMA((5,)),
        ],
        compiler_params=LIMIT,
        cost_estimate=TINY,
        name="plan",
    )(*(pltpu.with_memory_space_constraint(v, pltpu.HBM) for v in (ancestors, lengths, key_cache, value_cache, out_weight)))
    def along(v):
        return permute(v, ("y", "c"), lambda y, c: (y + 1 + 2 * c, c))

    w_next = along(out_weight)
    w0_x = swap_core(out_weight)
    w_far = along(w_next)
    w_back = swap_core(along(w0_x))

    m2 = pl.pallas_call(
        hold_kernel,
        out_shape=shape(2 * HOLD, WIDE),
        in_specs=[VMEM] * 2,
        out_specs=VMEM,
        input_output_aliases={0: 0},
        compiler_params=LIMIT,
        cost_estimate=TINY,
        name="relay",
    )(m2, back)
    m3 = swap_core(m2)
    keep0, keep1, give0, give1 = attend_call(sort, back, chunks, m0, m1, m2, m3, keys, values)
    far = swap_both(give1)
    near = swap_chip(keep1)
    beside = swap_core(give0)
    spread = pl.pallas_call(
        spread_kernel,
        out_shape=shape(8, FAMILY, HALF),
        in_specs=[VMEM] * 6,
        out_specs=VMEM,
        compiler_params=pltpu.CompilerParams(vmem_limit_bytes=8 * 2**20),
        cost_estimate=pl.CostEstimate(flops=10**5, bytes_accessed=10**5, transcendentals=0),
        name="spread",
    )(keep0, far, near, beside, w_next, w0_x)
    mine = lax.all_to_all(spread, Z, split_axis=0, concat_axis=0).reshape(8 * FAMILY, HALF)
    rows = 8 * FAMILY
    w_specs = [VMEM] * 4
    w = (w0, w_next, w_far, w_back)
    mine = pl.pallas_call(
        hold_kernel,
        out_shape=shape(8 * FAMILY, HALF),
        in_specs=[VMEM] * 3,
        out_specs=VMEM,
        input_output_aliases={0: 0},
        compiler_params=LIMIT,
        cost_estimate=TINY,
        name="hold",
    )(mine, w_far, w_back)
    other = swap_core(mine)
    acc = pl.pallas_call(
        own_half_kernel,
        out_shape=shape(4, rows, 128, dtype=F32),
        in_specs=[VMEM] + w_specs,
        out_specs=VMEM,
        compiler_params=LIMIT,
        cost_estimate=pl.CostEstimate(flops=10**9, bytes_accessed=10**6, transcendentals=0),
        name="own_half",
    )(mine, *w)
    parts = pl.pallas_call(
        other_half_kernel,
        out_shape=[shape(2, rows // 2, 128)] * 4,
        in_specs=[VMEM, VMEM] + w_specs,
        out_specs=[VMEM] * 4,
        scratch_shapes=[pltpu.VMEM((4, 2, rows // 2, 128), BF16)],
        compiler_params=LIMIT,
        cost_estimate=pl.CostEstimate(flops=10**9, bytes_accessed=10**6, transcendentals=0),
        name="other_half",
    )(other, acc, *w)
    total = 0.0
    for k in (2, 1, 3, 0):
        total = total + permute(parts[k], ("y", "x"), lambda y, x, k=k: (x + k, y)).astype(F32)
    return total.astype(BF16)


def solution(mesh):
    fine = Mesh(mesh.devices.reshape(SIZES), AXES)
    in_specs = (
        P(None, DP, "x"),
        P(DP, "x", None, None),
        P(DP, "x", None, None),
        P(None, DP, "x"),
        P(None, DP, "x"),
        P(DP),
        P(),
        P("x", DP),
    )
    return jax.shard_map(
        per_device, mesh=fine, in_specs=in_specs, out_specs=P(None, "x", DP), check_vma=False
    )
```

time: 66.2 us -> 64.4 us (0.973)
  Pallas kernels: 8.94 us -> 7.36 us
  starting transfers between devices: 27.3 us -> 26.3 us
  waiting for transfers between devices: 28.2 us -> 28.9 us
    ppermute x15 -> x16, waiting for transfers between devices: 19.8 us -> 21.9 us  [permute(): return lax.ppermute(value, axes, pairs)]
    pallas_call x1, Pallas kernels: 3.68 us -> 2.14 us  [attend_call(): pl.pallas_call(attend_kernel, out_shape=[shape(FAMILY, HALF)] * 4, in_spe...]
    all_to_all x1, waiting for transfers between devices: 8.4 us -> 6.94 us  [per_device(): lax.all_to_all(spread, Z, split_axis=0, concat_axis=0)]
    ppermute x15 -> x16, starting transfers between devices: 19.2 us -> 18.6 us  [permute(): return lax.ppermute(value, axes, pairs)]
  transfers between devices with their start and end apart: 16 -> 17, of which waited for: 8 -> 8; matrix products, arithmetic and copies ran while one was open for 1% -> 1% of each run, Pallas kernels for 11% -> 10%
where the time goes in v4:
time: 64.4 us; the launch traced here: 64.2 us
  waiting for transfers between devices  28.9 us (45%)
  starting transfers between devices  26.3 us (41%)
  Pallas kernels  7.36 us (11%)
  other arithmetic  1.55 us (2%)
    ppermute x16, waiting for transfers between devices, permute(): return lax.ppermute(value, axes, pairs)  21.9 us
    ppermute x16, starting transfers between devices, permute(): return lax.ppermute(value, axes, pairs)  18.6 us
    all_to_all x1, starting transfers between devices, per_device(): lax.all_to_all(spread, Z, split_axis=0, concat_axis=0)  7.7 us
    all_to_all x1, waiting for transfers between devices, per_device(): lax.all_to_all(spread, Z, split_axis=0, concat_axis=0)  6.94 us
    pallas_call x1, Pallas kernels, per_device(): pl.pallas_call(plan_kernel, out_shape=[shape(SLOTS + 8, 128, dtype=F32),...  2.94 us
    pallas_call x1, Pallas kernels, attend_call(): pl.pallas_call(attend_kernel, out_shape=[shape(FAMILY, HALF)] * 4, in_spe...  2.14 us
  transfers between devices with their start and end apart: 17, of which 8 were waited for; matrix products, arithmetic and copies ran while one was open for 1% of the time, Pallas kernels for 10%

profile of v4, /device:TPU:6, one launch (start us, length us, event | category | flops | bytes accessed | tf_op | source)
XLA Modules:
  0.0 64.2 jit_solution(11590940824544331036)
XLA Ops:
  0.0 1.6 %collective-permute-start.6 = (bf16[2048,128]{1,0:T(8,128)(2,1)}, bf16[2048,128]{1,0:T(8,128)(2,1)S(1)}, u32[]{:S(2)}, u32[]{:S(2)}) collective-permute-start(bf16[2048,128]{1,0:T(8,128)(2,1)} %w_ref.1), channel_id=1, source_target_pairs={{0,64},{4,196},{64,128},{68,4},{128,192},{132,68},{192,0},{196,132... | collective-permute-start | bytes 1572872 | tf_op jit(solution)/shard_map/ppermute | solution.py:221
  1.6 0.9 %maximum_bitcast_fusion.m0 = bf16[16,2560]{1,0:T(8,128)(2,1)S(1)} fusion(bf16[2,8,256]{2,1,0:T(8,128)(2,1)} %param.12, bf16[2,8,256]{2,1,0:T(8,128)(2,1)} %param.11, bf16[2,8,2048]{2,1,0:T(8,128)(2,1)} %param.8), kind=kLoop, calls=%fused_computation.1 | loop fusion | flops 245760 | bytes 163840 | tf_op jit(solution)/shard_map/reshape | solution.py:259
  2.5 1.9 %collective-permute-start.1 = (bf16[16,2560]{1,0:T(8,128)(2,1)S(1)}, bf16[16,2560]{1,0:T(8,128)(2,1)S(1)}, u32[]{:S(2)}, u32[]{:S(2)}) collective-permute-start(bf16[16,2560]{1,0:T(8,128)(2,1)S(1)} %maximum_bitcast_fusion.m0), channel_id=1, source_target_pairs={{0,8},{8,0},{1,9},{9,1},{2,10},{10,2},{3,11},{11,3},{4,12},{12,4},... | collective-permute-start | bytes 245768 | tf_op jit(solution)/shard_map/ppermute | solution.py:221
  4.4 1.4 %collective-permute-start = (bf16[16,2560]{1,0:T(8,128)(2,1)S(1)}, bf16[16,2560]{1,0:T(8,128)(2,1)S(1)}, u32[]{:S(2)}, u32[]{:S(2)}) collective-permute-start(bf16[16,2560]{1,0:T(8,128)(2,1)S(1)} %maximum_bitcast_fusion.m0), channel_id=1, source_target_pairs={{0,4},{4,0},{1,5},{5,1},{2,6},{6,2},{3,7},{7,3},{8,12},{12,8},{9,1... | collective-permute-start | bytes 245768 | tf_op jit(solution)/shard_map/ppermute | solution.py:221
  5.8 2.9 %plan.1 = (f32[136,128]{1,0:T(8,128)S(1)}, f32[64,128]{1,0:T(8,128)S(1)}, s32[26]{0:T(128)S(1)}, bf16[8,2,512,128]{3,2,1,0:T(8,128)(2,1)S(1)}, bf16[8,2,512,128]...) custom-call(s32[2,512]{1,0:T(2,128)} %ancestors.1, s32[8]{0:T(128)} %lengths.1, bf16[8,2,512,128]{3,2,1,0:T(8,128)(2,1)} %key_ref.1, ...), custom_call_target="tpu_custom_call" | custom-call | flops 1000000 | bytes 100000 | tf_op jit(solution)/shard_map/plan/pallas_call | solution.py:262
  8.7 0.0 collective-permute-done.1.refs_0_
  8.7 0.1 collective-permute-start.2
  8.8 0.7 %collective-permute-start.9 = (bf16[2048,128]{1,0:T(8,128)(2,1)S(1)}, bf16[2048,128]{1,0:T(8,128)(2,1)S(1)}, u32[]{:S(2)}, u32[]{:S(2)}) collective-permute-start(bf16[2048,128]{1,0:T(8,128)(2,1)S(1)} %collective-permute-done.7.w3), channel_id=1, source_target_pairs={{0,64},{4,196},{64,128},{68,4},{128,192},{132,68},{192,0},{196,132... | collective-permute-start | bytes 1572872 | tf_op jit(solution)/shard_map/ppermute | solution.py:221
  9.5 0.0 collective-permute-done.m1
  9.5 0.6 collective-permute-done.2.m3
  10.1 2.1 %attend.1 = (bf16[32,1024]{1,0:T(8,128)(2,1)S(1)}, bf16[32,1024]{1,0:T(8,128)(2,1)S(1)}, bf16[32,1024]{1,0:T(8,128)(2,1)S(1)}, bf16[32,1024]{1,0:T(8,128)(2,1)S(1)}) custom-call(f32[136,128]{1,0:T(8,128)S(1)} %get-tuple-element.19.plan, f32[64,128]{1,0:T(8,128)S(1)} %get-tuple-element.20.refs_1_.back, s32[26]{0:T(128)S(1)} %get-tuple-element.21.chunks, ...), custom_call_target="tpu_custom_call" | custom-call | flops 1000000 | bytes 100000 | tf_op jit(solution)/shard_map/attend/pallas_call | solution.py:241
  12.2 2.0 %collective-permute-start.3 = (bf16[32,1024]{1,0:T(8,128)(2,1)S(1)}, bf16[32,1024]{1,0:T(8,128)(2,1)S(1)}, u32[]{:S(2)}, u32[]{:S(2)}) collective-permute-start(bf16[32,1024]{1,0:T(8,128)(2,1)S(1)} %get-tuple-element.25), channel_id=1, source_target_pairs={{0,12},{4,8},{8,4},{12,0},{1,13},{5,9},{9,5},{13,1},{2,14},{6,10},... | collective-permute-start | bytes 196616 | tf_op jit(solution)/shard_map/ppermute | solution.py:221
  14.3 0.9 %collective-permute-start.4 = (bf16[32,1024]{1,0:T(8,128)(2,1)S(1)}, bf16[32,1024]{1,0:T(8,128)(2,1)S(1)}, u32[]{:S(2)}, u32[]{:S(2)}) collective-permute-start(bf16[32,1024]{1,0:T(8,128)(2,1)S(1)} %get-tuple-element.26), channel_id=1, source_target_pairs={{0,8},{8,0},{1,9},{9,1},{2,10},{10,2},{3,11},{11,3},{4,12},{12,4},... | collective-permute-start | bytes 196616 | tf_op jit(solution)/shard_map/ppermute | solution.py:221
  15.1 0.0 collective-permute-start.5
  15.1 1.5 %collective-permute-done.3.b_ref = bf16[32,1024]{1,0:T(8,128)(2,1)S(1)} collective-permute-done((bf16[32,1024]{1,0:T(8,128)(2,1)S(1)}, bf16[32,1024]{1,0:T(8,128)(2,1)S(1)}, u32[]{:S(2)}, u32[]{:S(2)}) %collective-permute-start.3) | collective-permute-done | bytes 65568 | tf_op jit(solution)/shard_map/ppermute | solution.py:221
  16.6 2.2 %collective-permute-done.4.c_ref = bf16[32,1024]{1,0:T(8,128)(2,1)S(1)} collective-permute-done((bf16[32,1024]{1,0:T(8,128)(2,1)S(1)}, bf16[32,1024]{1,0:T(8,128)(2,1)S(1)}, u32[]{:S(2)}, u32[]{:S(2)}) %collective-permute-start.4) | collective-permute-done | bytes 65568 | tf_op jit(solution)/shard_map/ppermute | solution.py:221
  18.8 0.8 %spread.1 = bf16[8,32,1024]{2,1,0:T(8,128)(2,1)} custom-call(bf16[32,1024]{1,0:T(8,128)(2,1)S(1)} %get-tuple-element.24.a_ref, bf16[32,1024]{1,0:T(8,128)(2,1)S(1)} %collective-permute-done.3.b_ref, bf16[32,1024]{1,0:T(8,128)(2,1)S(1)} %collective-permute-done.4.c_ref, bf16[32,1024]{1,0:T(8,128)(2,1)S(1)} %collective-permute-done.5.d_ref, ...), custom_call_target="tpu_custom_call" | custom-call | flops 100000 | bytes 100000 | tf_op jit(solution)/shard_map/spread/pallas_call | solution.py:307
  19.6 7.7 %all-to-all-start = ((bf16[8,32,1024]{2,1,0:T(8,128)(2,1)}), bf16[8,32,1024]{2,1,0:T(8,128)(2,1)S(1)}, u32[]{:S(2)}, u32[]{:S(2)}) async-start(bf16[8,32,1024]{2,1,0:T(8,128)(2,1)} %spread.1), calls=%async_computation | async-start | bytes 1048576 | tf_op jit(solution)/shard_map/all_to_all | solution.py:316
  27.3 0.7 %collective-permute-start.8 = (bf16[2048,128]{1,0:T(8,128)(2,1)S(1)}, bf16[2048,128]{1,0:T(8,128)(2,1)S(1)}, u32[]{:S(2)}, u32[]{:S(2)}) collective-permute-start(bf16[2048,128]{1,0:T(8,128)(2,1)S(1)} %collective-permute-done.6.w1), channel_id=1, source_target_pairs={{0,64},{4,196},{64,128},{68,4},{128,192},{132,68},{192,0},{196,132... | collective-permute-start | bytes 1572872 | tf_op jit(solution)/shard_map/ppermute | solution.py:221
  28.0 0.4 collective-permute-start.10
  28.5 9.3 %collective-permute-done.8.refs_1_.w2 = bf16[2048,128]{1,0:T(8,128)(2,1)S(1)} collective-permute-done((bf16[2048,128]{1,0:T(8,128)(2,1)S(1)}, bf16[2048,128]{1,0:T(8,128)(2,1)S(1)}, u32[]{:S(2)}, u32[]{:S(2)}) %collective-permute-start.8) | collective-permute-done | bytes 524320 | tf_op jit(solution)/shard_map/ppermute | solution.py:221
  37.7 6.9 %all-to-all-done = bf16[8,32,1024]{2,1,0:T(8,128)(2,1)S(1)} async-done(((bf16[8,32,1024]{2,1,0:T(8,128)(2,1)}), bf16[8,32,1024]{2,1,0:T(8,128)(2,1)S(1)}, u32[]{:S(2)}, u32[]{:S(2)}) %all-to-all-start) | async-done | bytes 524320 | tf_op jit(solution)/shard_map/all_to_all | solution.py:316
  44.7 0.7 %own_half.1.acc_ref = f32[4,256,128]{2,1,0:T(8,128)S(1)} custom-call(bf16[256,1024]{1,0:T(8,128)(2,1)S(1)} %hold.1.mine_ref, bf16[2048,128]{1,0:T(8,128)(2,1)S(1)} %get-tuple-element.28.w0, bf16[2048,128]{1,0:T(8,128)(2,1)S(1)} %collective-permute-done.6.w1, bf16[2048,128]{1,0:T(8,128)(2,1)S(1)} %collective-permute-done.8.refs_1_.w2, ...), custom_call_target="tpu_custom_call" | custom-call | flops 1000000000 | bytes 1000000 | tf_op jit(solution)/shard_map/own_half/pallas_call | solution.py:331
  45.4 1.2 %collective-permute-done.11.other_ref = bf16[256,1024]{1,0:T(8,128)(2,1)S(1)} collective-permute-done((bf16[256,1024]{1,0:T(8,128)(2,1)S(1)}, bf16[256,1024]{1,0:T(8,128)(2,1)S(1)}, u32[]{:S(2)}, u32[]{:S(2)}) %collective-permute-start.11) | collective-permute-done | bytes 524320 | tf_op jit(solution)/shard_map/ppermute | solution.py:221
  46.6 0.7 %other_half.1 = (bf16[2,128,128]{2,1,0:T(8,128)(2,1)S(1)}, bf16[2,128,128]{2,1,0:T(8,128)(2,1)S(1)}, bf16[2,128,128]{2,1,0:T(8,128)(2,1)S(1)}, bf16[2,128,128]{2,1,0:T(8,128)(2,1)S(1)}) custom-call(bf16[256,1024]{1,0:T(8,128)(2,1)S(1)} %collective-permute-done.11.other_ref, f32[4,256,128]{2,1,0:T(8,128)S(1)} %own_half.1.acc_ref, ...), custom_call_target="tpu_custom_call" | custom-call | flops 1000000000 | bytes 1000000 | tf_op jit(solution)/shard_map/other_half/pallas_call | solution.py:340
  47.3 0.7 %collective-permute-start.12 = (bf16[2,128,128]{2,1,0:T(8,128)(2,1)S(1)}, bf16[2,128,128]{2,1,0:T(8,128)(2,1)S(1)}, u32[]{:S(2)}, u32[]{:S(2)}) collective-permute-start(bf16[2,128,128]{2,1,0:T(8,128)(2,1)S(1)} %get-tuple-element.29), channel_id=1, source_target_pairs={{0,128},{1,192},{2,0},{3,64},{64,129},{65,193},{66,1},{67,65},{128... | collective-permute-start | bytes 196616 | tf_op jit(solution)/shard_map/ppermute | solution.py:221
  48.0 1.2 %collective-permute-start.13 = (bf16[2,128,128]{2,1,0:T(8,128)(2,1)S(1)}, bf16[2,128,128]{2,1,0:T(8,128)(2,1)S(1)}, u32[]{:S(2)}, u32[]{:S(2)}) collective-permute-start(bf16[2,128,128]{2,1,0:T(8,128)(2,1)S(1)} %get-tuple-element.30), channel_id=1, source_target_pairs={{0,64},{1,128},{2,192},{3,0},{64,65},{65,129},{66,193},{67,1},{128... | collective-permute-start | bytes 196616 | tf_op jit(solution)/shard_map/ppermute | solution.py:221
  49.2 4.6 %collective-permute-start.14 = (bf16[2,128,128]{2,1,0:T(8,128)(2,1)S(1)}, bf16[2,128,128]{2,1,0:T(8,128)(2,1)S(1)}, u32[]{:S(2)}, u32[]{:S(2)}) collective-permute-start(bf16[2,128,128]{2,1,0:T(8,128)(2,1)S(1)} %get-tuple-element.31), channel_id=1, source_target_pairs={{0,192},{1,0},{2,64},{3,128},{64,193},{65,1},{66,65},{67,129},{128... | collective-permute-start | bytes 196616 | tf_op jit(solution)/shard_map/ppermute | solution.py:221
  53.8 2.4 %collective-permute-start.15 = (bf16[2,128,128]{2,1,0:T(8,128)(2,1)S(1)}, bf16[2,128,128]{2,1,0:T(8,128)(2,1)S(1)}, u32[]{:S(2)}, u32[]{:S(2)}) collective-permute-start(bf16[2,128,128]{2,1,0:T(8,128)(2,1)S(1)} %get-tuple-element.32), channel_id=1, source_target_pairs={{0,0},{1,64},{2,128},{3,192},{64,1},{65,65},{66,129},{67,193},{128... | collective-permute-start | bytes 196616 | tf_op jit(solution)/shard_map/ppermute | solution.py:221
  56.3 1.2 %collective-permute-done.14 = bf16[2,128,128]{2,1,0:T(8,128)(2,1)S(1)} collective-permute-done((bf16[2,128,128]{2,1,0:T(8,128)(2,1)S(1)}, bf16[2,128,128]{2,1,0:T(8,128)(2,1)S(1)}, u32[]{:S(2)}, u32[]{:S(2)}) %collective-permute-start.14) | collective-permute-done | bytes 65568 | tf_op jit(solution)/shard_map/ppermute | solution.py:221
  57.4 6.1 %collective-permute-done.15 = bf16[2,128,128]{2,1,0:T(8,128)(2,1)S(1)} collective-permute-done((bf16[2,128,128]{2,1,0:T(8,128)(2,1)S(1)}, bf16[2,128,128]{2,1,0:T(8,128)(2,1)S(1)}, u32[]{:S(2)}, u32[]{:S(2)}) %collective-permute-start.15) | collective-permute-done | bytes 65568 | tf_op jit(solution)/shard_map/ppermute | solution.py:221
  63.5 0.7 %add_convert_fusion = bf16[2,128,128]{2,1,0:T(8,128)(2,1)} fusion(bf16[2,128,128]{2,1,0:T(8,128)(2,1)S(1)} %collective-permute-done.15, bf16[2,128,128]{2,1,0:T(8,128)(2,1)S(1)} %collective-permute-done.14, bf16[2,128,128]{2,1,0:T(8,128)(2,1)S(1)} %collective-permute-done.13, bf16[2,128,128]{2,1,0:T(8,128)(2,1)S(1)} %collective-permute-done.12), kind=kLoop, calls=%fused_computation | loop fusion | flops 262144 | bytes 327680 | tf_op jit(solution)/shard_map/convert_element_type | solution.py:353
  (11 shorter events, 0.0 us)
Async XLA Ops:
  0.0 8.8 %collective-permute-start.7 = (bf16[2048,128]{1,0:T(8,128)(2,1)}, bf16[2048,128]{1,0:T(8,128)(2,1)S(1)}, u32[]{:S(2)}, u32[]{:S(2)}) collective-permute-start(bf16[2048,128]{1,0:T(8,128)(2,1)} %w_ref.1), channel_id=1, source_target_pairs={{0,4},{4,0},{1,5},{5,1},{2,6},{6,2},{3,7},{7,3},{8,12},{12,8},{9,1... | collective-permute-start | bytes 1572872 | tf_op jit(solution)/shard_map/ppermute | solution.py:221
  0.0 18.8 %collective-permute-start.6 = (bf16[2048,128]{1,0:T(8,128)(2,1)}, bf16[2048,128]{1,0:T(8,128)(2,1)S(1)}, u32[]{:S(2)}, u32[]{:S(2)}) collective-permute-start(bf16[2048,128]{1,0:T(8,128)(2,1)} %w_ref.1), channel_id=1, source_target_pairs={{0,64},{4,196},{64,128},{68,4},{128,192},{132,68},{192,0},{196,132... | collective-permute-start | bytes 1572872 | tf_op jit(solution)/shard_map/ppermute | solution.py:221
  2.5 6.3 %collective-permute-start.1 = (bf16[16,2560]{1,0:T(8,128)(2,1)S(1)}, bf16[16,2560]{1,0:T(8,128)(2,1)S(1)}, u32[]{:S(2)}, u32[]{:S(2)}) collective-permute-start(bf16[16,2560]{1,0:T(8,128)(2,1)S(1)} %maximum_bitcast_fusion.m0), channel_id=1, source_target_pairs={{0,8},{8,0},{1,9},{9,1},{2,10},{10,2},{3,11},{11,3},{4,12},{12,4},... | collective-permute-start | bytes 245768 | tf_op jit(solution)/shard_map/ppermute | solution.py:221
  4.4 5.1 %collective-permute-start = (bf16[16,2560]{1,0:T(8,128)(2,1)S(1)}, bf16[16,2560]{1,0:T(8,128)(2,1)S(1)}, u32[]{:S(2)}, u32[]{:S(2)}) collective-permute-start(bf16[16,2560]{1,0:T(8,128)(2,1)S(1)} %maximum_bitcast_fusion.m0), channel_id=1, source_target_pairs={{0,4},{4,0},{1,5},{5,1},{2,6},{6,2},{3,7},{7,3},{8,12},{12,8},{9,1... | collective-permute-start | bytes 245768 | tf_op jit(solution)/shard_map/ppermute | solution.py:221
  8.7 1.4 %collective-permute-start.2 = (bf16[16,2560]{1,0:T(8,128)(2,1)S(1)}, bf16[16,2560]{1,0:T(8,128)(2,1)S(1)}, u32[]{:S(2)}, u32[]{:S(2)}) collective-permute-start(bf16[16,2560]{1,0:T(8,128)(2,1)S(1)} %relay.1.m2), channel_id=1, source_target_pairs={{0,4},{4,0},{1,5},{5,1},{2,6},{6,2},{3,7},{7,3},{8,12},{12,8},{9,1... | collective-permute-start | bytes 245768 | tf_op jit(solution)/shard_map/ppermute | solution.py:221
  8.8 19.2 %collective-permute-start.9 = (bf16[2048,128]{1,0:T(8,128)(2,1)S(1)}, bf16[2048,128]{1,0:T(8,128)(2,1)S(1)}, u32[]{:S(2)}, u32[]{:S(2)}) collective-permute-start(bf16[2048,128]{1,0:T(8,128)(2,1)S(1)} %collective-permute-done.7.w3), channel_id=1, source_target_pairs={{0,64},{4,196},{64,128},{68,4},{128,192},{132,68},{192,0},{196,132... | collective-permute-start | bytes 1572872 | tf_op jit(solution)/shard_map/ppermute | solution.py:221
  12.2 4.4 %collective-permute-start.3 = (bf16[32,1024]{1,0:T(8,128)(2,1)S(1)}, bf16[32,1024]{1,0:T(8,128)(2,1)S(1)}, u32[]{:S(2)}, u32[]{:S(2)}) collective-permute-start(bf16[32,1024]{1,0:T(8,128)(2,1)S(1)} %get-tuple-element.25), channel_id=1, source_target_pairs={{0,12},{4,8},{8,4},{12,0},{1,13},{5,9},{9,5},{13,1},{2,14},{6,10},... | collective-permute-start | bytes 196616 | tf_op jit(solution)/shard_map/ppermute | solution.py:221
  14.3 4.5 %collective-permute-start.4 = (bf16[32,1024]{1,0:T(8,128)(2,1)S(1)}, bf16[32,1024]{1,0:T(8,128)(2,1)S(1)}, u32[]{:S(2)}, u32[]{:S(2)}) collective-permute-start(bf16[32,1024]{1,0:T(8,128)(2,1)S(1)} %get-tuple-element.26), channel_id=1, source_target_pairs={{0,8},{8,0},{1,9},{9,1},{2,10},{10,2},{3,11},{11,3},{4,12},{12,4},... | collective-permute-start | bytes 196616 | tf_op jit(solution)/shard_map/ppermute | solution.py:221
  15.1 3.6 %collective-permute-start.5 = (bf16[32,1024]{1,0:T(8,128)(2,1)S(1)}, bf16[32,1024]{1,0:T(8,128)(2,1)S(1)}, u32[]{:S(2)}, u32[]{:S(2)}) collective-permute-start(bf16[32,1024]{1,0:T(8,128)(2,1)S(1)} %get-tuple-element.27), channel_id=1, source_target_pairs={{0,4},{4,0},{1,5},{5,1},{2,6},{6,2},{3,7},{7,3},{8,12},{12,8},{9,1... | collective-permute-start | bytes 196616 | tf_op jit(solution)/shard_map/ppermute | solution.py:221
  19.6 25.0 %all-to-all-start = ((bf16[8,32,1024]{2,1,0:T(8,128)(2,1)}), bf16[8,32,1024]{2,1,0:T(8,128)(2,1)S(1)}, u32[]{:S(2)}, u32[]{:S(2)}) async-start(bf16[8,32,1024]{2,1,0:T(8,128)(2,1)} %spread.1), calls=%async_computation | async-start | bytes 1048576 | tf_op jit(solution)/shard_map/all_to_all | solution.py:316
  27.3 10.4 %collective-permute-start.8 = (bf16[2048,128]{1,0:T(8,128)(2,1)S(1)}, bf16[2048,128]{1,0:T(8,128)(2,1)S(1)}, u32[]{:S(2)}, u32[]{:S(2)}) collective-permute-start(bf16[2048,128]{1,0:T(8,128)(2,1)S(1)} %collective-permute-done.6.w1), channel_id=1, source_target_pairs={{0,64},{4,196},{64,128},{68,4},{128,192},{132,68},{192,0},{196,132... | collective-permute-start | bytes 1572872 | tf_op jit(solution)/shard_map/ppermute | solution.py:221
  28.0 16.6 %collective-permute-start.10 = (bf16[2048,128]{1,0:T(8,128)(2,1)S(1)}, bf16[2048,128]{1,0:T(8,128)(2,1)S(1)}, u32[]{:S(2)}, u32[]{:S(2)}) collective-permute-start(bf16[2048,128]{1,0:T(8,128)(2,1)S(1)} %collective-permute-done.9), channel_id=1, source_target_pairs={{0,4},{4,0},{1,5},{5,1},{2,6},{6,2},{3,7},{7,3},{8,12},{12,8},{9,1... | collective-permute-start | bytes 1572872 | tf_op jit(solution)/shard_map/ppermute | solution.py:221
  44.7 1.9 %collective-permute-start.11 = (bf16[256,1024]{1,0:T(8,128)(2,1)S(1)}, bf16[256,1024]{1,0:T(8,128)(2,1)S(1)}, u32[]{:S(2)}, u32[]{:S(2)}) collective-permute-start(bf16[256,1024]{1,0:T(8,128)(2,1)S(1)} %hold.1.mine_ref), channel_id=1, source_target_pairs={{0,4},{4,0},{1,5},{5,1},{2,6},{6,2},{3,7},{7,3},{8,12},{12,8},{9,1... | collective-permute-start | bytes 1572872 | tf_op jit(solution)/shard_map/ppermute | solution.py:221
  47.3 8.9 %collective-permute-start.12 = (bf16[2,128,128]{2,1,0:T(8,128)(2,1)S(1)}, bf16[2,128,128]{2,1,0:T(8,128)(2,1)S(1)}, u32[]{:S(2)}, u32[]{:S(2)}) collective-permute-start(bf16[2,128,128]{2,1,0:T(8,128)(2,1)S(1)} %get-tuple-element.29), channel_id=1, source_target_pairs={{0,128},{1,192},{2,0},{3,64},{64,129},{65,193},{66,1},{67,65},{128... | collective-permute-start | bytes 196616 | tf_op jit(solution)/shard_map/ppermute | solution.py:221
  48.0 8.2 %collective-permute-start.13 = (bf16[2,128,128]{2,1,0:T(8,128)(2,1)S(1)}, bf16[2,128,128]{2,1,0:T(8,128)(2,1)S(1)}, u32[]{:S(2)}, u32[]{:S(2)}) collective-permute-start(bf16[2,128,128]{2,1,0:T(8,128)(2,1)S(1)} %get-tuple-element.30), channel_id=1, source_target_pairs={{0,64},{1,128},{2,192},{3,0},{64,65},{65,129},{66,193},{67,1},{128... | collective-permute-start | bytes 196616 | tf_op jit(solution)/shard_map/ppermute | solution.py:221
  49.2 8.2 %collective-permute-start.14 = (bf16[2,128,128]{2,1,0:T(8,128)(2,1)S(1)}, bf16[2,128,128]{2,1,0:T(8,128)(2,1)S(1)}, u32[]{:S(2)}, u32[]{:S(2)}) collective-permute-start(bf16[2,128,128]{2,1,0:T(8,128)(2,1)S(1)} %get-tuple-element.31), channel_id=1, source_target_pairs={{0,192},{1,0},{2,64},{3,128},{64,193},{65,1},{66,65},{67,129},{128... | collective-permute-start | bytes 196616 | tf_op jit(solution)/shard_map/ppermute | solution.py:221
  53.8 9.7 %collective-permute-start.15 = (bf16[2,128,128]{2,1,0:T(8,128)(2,1)S(1)}, bf16[2,128,128]{2,1,0:T(8,128)(2,1)S(1)}, u32[]{:S(2)}, u32[]{:S(2)}) collective-permute-start(bf16[2,128,128]{2,1,0:T(8,128)(2,1)S(1)} %get-tuple-element.32), channel_id=1, source_target_pairs={{0,0},{1,64},{2,128},{3,192},{64,1},{65,65},{66,129},{67,193},{128... | collective-permute-start | bytes 196616 | tf_op jit(solution)/shard_map/ppermute | solution.py:221

commit v5 on v4

--- a/solution.py
+++ b/solution.py
@@ -171,7 +171,7 @@
             out[...] = both[zz * FAMILY : (zz + 1) * FAMILY]
 
 
-def spread_kernel(a_ref, b_ref, c_ref, d_ref, w1, w3, out_ref):
+def spread_kernel(a_ref, b_ref, c_ref, d_ref, out_ref):
     total = (a_ref[...] + b_ref[...]) + (c_ref[...] + d_ref[...])
     for z in range(8):
         out_ref[z] = total
@@ -250,7 +250,7 @@
             pltpu.VMEM((KV, SLOTS, HALF), F32),
         ],
         compiler_params=LIMIT,
-        cost_estimate=TINY,
+        cost_estimate=pl.CostEstimate(flops=70 * 10**8, bytes_accessed=10**6, transcendentals=0),
         name="attend",
     )(*args)
 
@@ -307,12 +307,12 @@
     spread = pl.pallas_call(
         spread_kernel,
         out_shape=shape(8, FAMILY, HALF),
-        in_specs=[VMEM] * 6,
+        in_specs=[VMEM] * 4,
         out_specs=VMEM,
         compiler_params=pltpu.CompilerParams(vmem_limit_bytes=8 * 2**20),
-        cost_estimate=pl.CostEstimate(flops=10**5, bytes_accessed=10**5, transcendentals=0),
+        cost_estimate=pl.CostEstimate(flops=12 * 10**9, bytes_accessed=10**5, transcendentals=0),
         name="spread",
-    )(keep0, far, near, beside, w_next, w0_x)
+    )(keep0, far, near, beside)
     mine = lax.all_to_all(spread, Z, split_axis=0, concat_axis=0).reshape(8 * FAMILY, HALF)
     rows = 8 * FAMILY
     w_specs = [VMEM] * 4

time: 64.4 us -> 63.9 us (level)
  waiting for transfers between devices: 28.9 us -> 27.6 us
  Pallas kernels: 7.36 us -> 8.42 us
    ppermute x16, waiting for transfers between devices: 21.9 us -> 20.6 us  [permute(): return lax.ppermute(value, axes, pairs)]
    pallas_call x1, Pallas kernels: 2.14 us -> 3.19 us  [attend_call(): pl.pallas_call(attend_kernel, out_shape=[shape(FAMILY, HALF)] * 4, in_spe...]
  transfers between devices with their start and end apart: 17 -> 17, of which waited for: 8 -> 8; matrix products, arithmetic and copies ran while one was open for 1% -> 0% of each run, Pallas kernels for 10% -> 12%
where the time goes in v5:
time: 63.9 us
  waiting for transfers between devices  27.6 us (43%)
  starting transfers between devices  26.2 us (41%)
  Pallas kernels  8.42 us (13%)
  other arithmetic  1.55 us (2%)
    ppermute x16, waiting for transfers between devices, permute(): return lax.ppermute(value, axes, pairs)  20.6 us
    ppermute x16, starting transfers between devices, permute(): return lax.ppermute(value, axes, pairs)  18.4 us
    all_to_all x1, starting transfers between devices, per_device(): lax.all_to_all(spread, Z, split_axis=0, concat_axis=0)  7.78 us
    all_to_all x1, waiting for transfers between devices, per_device(): lax.all_to_all(spread, Z, split_axis=0, concat_axis=0)  6.96 us
    pallas_call x1, Pallas kernels, attend_call(): pl.pallas_call(attend_kernel, out_shape=[shape(FAMILY, HALF)] * 4, in_spe...  3.19 us
    pallas_call x1, Pallas kernels, per_device(): pl.pallas_call(plan_kernel, out_shape=[shape(SLOTS + 8, 128, dtype=F32),...  2.94 us
  transfers between devices with their start and end apart: 17, of which 8 were waited for; matrix products, arithmetic and copies ran while one was open for 0% of the time, Pallas kernels for 12%

profile of v5, /device:TPU:6, one launch (start us, length us, event | category | flops | bytes accessed | tf_op | source)
XLA Modules:
  0.0 63.9 jit_solution(1808035945554186606)
XLA Ops:
  0.0 0.9 %maximum_bitcast_fusion.m0 = bf16[16,2560]{1,0:T(8,128)(2,1)S(1)} fusion(bf16[2,8,256]{2,1,0:T(8,128)(2,1)} %param.12, bf16[2,8,256]{2,1,0:T(8,128)(2,1)} %param.11, bf16[2,8,2048]{2,1,0:T(8,128)(2,1)} %param.8), kind=kLoop, calls=%fused_computation.1 | loop fusion | flops 245760 | bytes 163840 | tf_op jit(solution)/shard_map/reshape | solution.py:259
  0.9 2.0 %collective-permute-start.1 = (bf16[16,2560]{1,0:T(8,128)(2,1)S(1)}, bf16[16,2560]{1,0:T(8,128)(2,1)S(1)}, u32[]{:S(2)}, u32[]{:S(2)}) collective-permute-start(bf16[16,2560]{1,0:T(8,128)(2,1)S(1)} %maximum_bitcast_fusion.m0), channel_id=1, source_target_pairs={{0,8},{8,0},{1,9},{9,1},{2,10},{10,2},{3,11},{11,3},{4,12},{12,4},... | collective-permute-start | bytes 245768 | tf_op jit(solution)/shard_map/ppermute | solution.py:221
  2.9 2.9 %plan.1 = (f32[136,128]{1,0:T(8,128)S(1)}, f32[64,128]{1,0:T(8,128)S(1)}, s32[26]{0:T(128)S(1)}, bf16[8,2,512,128]{3,2,1,0:T(8,128)(2,1)S(1)}, bf16[8,2,512,128]...) custom-call(s32[2,512]{1,0:T(2,128)} %ancestors.1, s32[8]{0:T(128)} %lengths.1, bf16[8,2,512,128]{3,2,1,0:T(8,128)(2,1)} %key_ref.1, ...), custom_call_target="tpu_custom_call" | custom-call | flops 1000000 | bytes 100000 | tf_op jit(solution)/shard_map/plan/pallas_call | solution.py:262
  5.8 0.0 collective-permute-done.1.refs_0_
  5.9 0.6 collective-permute-start.2
  6.5 0.1 collective-permute-start.8
  6.6 0.8 %collective-permute-done.2.m3 = bf16[16,2560]{1,0:T(8,128)(2,1)S(1)} collective-permute-done((bf16[16,2560]{1,0:T(8,128)(2,1)S(1)}, bf16[16,2560]{1,0:T(8,128)(2,1)S(1)}, u32[]{:S(2)}, u32[]{:S(2)}) %collective-permute-start.2) | collective-permute-done | bytes 81952 | tf_op jit(solution)/shard_map/ppermute | solution.py:221
  7.4 3.2 %attend.1 = (bf16[32,1024]{1,0:T(8,128)(2,1)S(1)}, bf16[32,1024]{1,0:T(8,128)(2,1)S(1)}, bf16[32,1024]{1,0:T(8,128)(2,1)S(1)}, bf16[32,1024]{1,0:T(8,128)(2,1)S(1)}) custom-call(f32[136,128]{1,0:T(8,128)S(1)} %get-tuple-element.19.plan, f32[64,128]{1,0:T(8,128)S(1)} %get-tuple-element.20.refs_1_.back, s32[26]{0:T(128)S(1)} %get-tuple-element.21.chunks, ...), custom_call_target="tpu_custom_call" | custom-call | flops 7000000000 | bytes 1000000 | tf_op jit(solution)/shard_map/attend/pallas_call | solution.py:241
  10.6 1.1 %collective-permute-start.3 = (bf16[32,1024]{1,0:T(8,128)(2,1)S(1)}, bf16[32,1024]{1,0:T(8,128)(2,1)S(1)}, u32[]{:S(2)}, u32[]{:S(2)}) collective-permute-start(bf16[32,1024]{1,0:T(8,128)(2,1)S(1)} %get-tuple-element.25), channel_id=1, source_target_pairs={{0,12},{4,8},{8,4},{12,0},{1,13},{5,9},{9,5},{13,1},{2,14},{6,10},... | collective-permute-start | bytes 196616 | tf_op jit(solution)/shard_map/ppermute | solution.py:221
  11.6 1.0 %collective-permute-start.4 = (bf16[32,1024]{1,0:T(8,128)(2,1)S(1)}, bf16[32,1024]{1,0:T(8,128)(2,1)S(1)}, u32[]{:S(2)}, u32[]{:S(2)}) collective-permute-start(bf16[32,1024]{1,0:T(8,128)(2,1)S(1)} %get-tuple-element.26), channel_id=1, source_target_pairs={{0,8},{8,0},{1,9},{9,1},{2,10},{10,2},{3,11},{11,3},{4,12},{12,4},... | collective-permute-start | bytes 196616 | tf_op jit(solution)/shard_map/ppermute | solution.py:221
  12.6 0.0 collective-permute-start.5
  12.6 1.5 %collective-permute-start.6 = (bf16[2048,128]{1,0:T(8,128)(2,1)S(1)}, bf16[2048,128]{1,0:T(8,128)(2,1)S(1)}, u32[]{:S(2)}, u32[]{:S(2)}) collective-permute-start(bf16[2048,128]{1,0:T(8,128)(2,1)S(1)} %copy-done), channel_id=1, source_target_pairs={{0,64},{4,196},{64,128},{68,4},{128,192},{132,68},{192,0},{196,132... | collective-permute-start | bytes 1572872 | tf_op jit(solution)/shard_map/ppermute | solution.py:221
  14.1 1.7 %collective-permute-start.9 = (bf16[2048,128]{1,0:T(8,128)(2,1)S(1)}, bf16[2048,128]{1,0:T(8,128)(2,1)S(1)}, u32[]{:S(2)}, u32[]{:S(2)}) collective-permute-start(bf16[2048,128]{1,0:T(8,128)(2,1)S(1)} %collective-permute-done.8), channel_id=1, source_target_pairs={{0,64},{4,196},{64,128},{68,4},{128,192},{132,68},{192,0},{196,132... | collective-permute-start | bytes 1572872 | tf_op jit(solution)/shard_map/ppermute | solution.py:221
  15.8 0.7 %collective-permute-done.4.c_ref = bf16[32,1024]{1,0:T(8,128)(2,1)S(1)} collective-permute-done((bf16[32,1024]{1,0:T(8,128)(2,1)S(1)}, bf16[32,1024]{1,0:T(8,128)(2,1)S(1)}, u32[]{:S(2)}, u32[]{:S(2)}) %collective-permute-start.4) | collective-permute-done | bytes 65568 | tf_op jit(solution)/shard_map/ppermute | solution.py:221
  16.5 0.0 collective-permute-done.5.d_ref
  16.5 0.8 %spread.1 = bf16[8,32,1024]{2,1,0:T(8,128)(2,1)} custom-call(bf16[32,1024]{1,0:T(8,128)(2,1)S(1)} %get-tuple-element.24.a_ref, bf16[32,1024]{1,0:T(8,128)(2,1)S(1)} %collective-permute-done.3.b_ref, bf16[32,1024]{1,0:T(8,128)(2,1)S(1)} %collective-permute-done.4.c_ref, bf16[32,1024]{1,0:T(8,128)(2,1)S(1)} %collective-permute-done.5.d_ref), custom_call_target="tpu_custom_call" | custom-call | flops 12000000000 | bytes 100000 | tf_op jit(solution)/shard_map/spread/pallas_call | solution.py:307
  17.3 7.8 %all-to-all-start = ((bf16[8,32,1024]{2,1,0:T(8,128)(2,1)}), bf16[8,32,1024]{2,1,0:T(8,128)(2,1)S(1)}, u32[]{:S(2)}, u32[]{:S(2)}) async-start(bf16[8,32,1024]{2,1,0:T(8,128)(2,1)} %spread.1), calls=%async_computation | async-start | bytes 1048576 | tf_op jit(solution)/shard_map/all_to_all | solution.py:316
  25.1 1.2 %collective-permute-start.7 = (bf16[2048,128]{1,0:T(8,128)(2,1)S(1)}, bf16[2048,128]{1,0:T(8,128)(2,1)S(1)}, u32[]{:S(2)}, u32[]{:S(2)}) collective-permute-start(bf16[2048,128]{1,0:T(8,128)(2,1)S(1)} %collective-permute-done.6.w1), channel_id=1, source_target_pairs={{0,64},{4,196},{64,128},{68,4},{128,192},{132,68},{192,0},{196,132... | collective-permute-start | bytes 1572872 | tf_op jit(solution)/shard_map/ppermute | solution.py:221
  26.3 2.4 %collective-permute-done.9 = bf16[2048,128]{1,0:T(8,128)(2,1)S(1)} collective-permute-done((bf16[2048,128]{1,0:T(8,128)(2,1)S(1)}, bf16[2048,128]{1,0:T(8,128)(2,1)S(1)}, u32[]{:S(2)}, u32[]{:S(2)}) %collective-permute-start.9) | collective-permute-done | bytes 524320 | tf_op jit(solution)/shard_map/ppermute | solution.py:221
  28.7 6.9 %collective-permute-done.7.refs_1_.w2 = bf16[2048,128]{1,0:T(8,128)(2,1)S(1)} collective-permute-done((bf16[2048,128]{1,0:T(8,128)(2,1)S(1)}, bf16[2048,128]{1,0:T(8,128)(2,1)S(1)}, u32[]{:S(2)}, u32[]{:S(2)}) %collective-permute-start.7) | collective-permute-done | bytes 524320 | tf_op jit(solution)/shard_map/ppermute | solution.py:221
  35.6 7.0 %all-to-all-done = bf16[8,32,1024]{2,1,0:T(8,128)(2,1)S(1)} async-done(((bf16[8,32,1024]{2,1,0:T(8,128)(2,1)}), bf16[8,32,1024]{2,1,0:T(8,128)(2,1)S(1)}, u32[]{:S(2)}, u32[]{:S(2)}) %all-to-all-start) | async-done | bytes 524320 | tf_op jit(solution)/shard_map/all_to_all | solution.py:316
  42.5 0.0 collective-permute-start.11
  42.5 0.7 %own_half.1.acc_ref = f32[4,256,128]{2,1,0:T(8,128)S(1)} custom-call(bf16[256,1024]{1,0:T(8,128)(2,1)S(1)} %hold.1.mine_ref, bf16[2048,128]{1,0:T(8,128)(2,1)S(1)} %get-tuple-element.28.w0, bf16[2048,128]{1,0:T(8,128)(2,1)S(1)} %collective-permute-done.6.w1, bf16[2048,128]{1,0:T(8,128)(2,1)S(1)} %collective-permute-done.7.refs_1_.w2, ...), custom_call_target="tpu_custom_call" | custom-call | flops 1000000000 | bytes 1000000 | tf_op jit(solution)/shard_map/own_half/pallas_call | solution.py:331
  43.2 1.2 %collective-permute-done.11.other_ref = bf16[256,1024]{1,0:T(8,128)(2,1)S(1)} collective-permute-done((bf16[256,1024]{1,0:T(8,128)(2,1)S(1)}, bf16[256,1024]{1,0:T(8,128)(2,1)S(1)}, u32[]{:S(2)}, u32[]{:S(2)}) %collective-permute-start.11) | collective-permute-done | bytes 524320 | tf_op jit(solution)/shard_map/ppermute | solution.py:221
  44.4 0.7 %other_half.1 = (bf16[2,128,128]{2,1,0:T(8,128)(2,1)S(1)}, bf16[2,128,128]{2,1,0:T(8,128)(2,1)S(1)}, bf16[2,128,128]{2,1,0:T(8,128)(2,1)S(1)}, bf16[2,128,128]{2,1,0:T(8,128)(2,1)S(1)}) custom-call(bf16[256,1024]{1,0:T(8,128)(2,1)S(1)} %collective-permute-done.11.other_ref, f32[4,256,128]{2,1,0:T(8,128)S(1)} %own_half.1.acc_ref, ...), custom_call_target="tpu_custom_call" | custom-call | flops 1000000000 | bytes 1000000 | tf_op jit(solution)/shard_map/other_half/pallas_call | solution.py:340
  45.2 1.1 %collective-permute-start.12 = (bf16[2,128,128]{2,1,0:T(8,128)(2,1)S(1)}, bf16[2,128,128]{2,1,0:T(8,128)(2,1)S(1)}, u32[]{:S(2)}, u32[]{:S(2)}) collective-permute-start(bf16[2,128,128]{2,1,0:T(8,128)(2,1)S(1)} %get-tuple-element.29), channel_id=1, source_target_pairs={{0,128},{1,192},{2,0},{3,64},{64,129},{65,193},{66,1},{67,65},{128... | collective-permute-start | bytes 196616 | tf_op jit(solution)/shard_map/ppermute | solution.py:221
  46.3 2.2 %collective-permute-start.13 = (bf16[2,128,128]{2,1,0:T(8,128)(2,1)S(1)}, bf16[2,128,128]{2,1,0:T(8,128)(2,1)S(1)}, u32[]{:S(2)}, u32[]{:S(2)}) collective-permute-start(bf16[2,128,128]{2,1,0:T(8,128)(2,1)S(1)} %get-tuple-element.30), channel_id=1, source_target_pairs={{0,64},{1,128},{2,192},{3,0},{64,65},{65,129},{66,193},{67,1},{128... | collective-permute-start | bytes 196616 | tf_op jit(solution)/shard_map/ppermute | solution.py:221
  48.5 3.2 %collective-permute-start.14 = (bf16[2,128,128]{2,1,0:T(8,128)(2,1)S(1)}, bf16[2,128,128]{2,1,0:T(8,128)(2,1)S(1)}, u32[]{:S(2)}, u32[]{:S(2)}) collective-permute-start(bf16[2,128,128]{2,1,0:T(8,128)(2,1)S(1)} %get-tuple-element.31), channel_id=1, source_target_pairs={{0,192},{1,0},{2,64},{3,128},{64,193},{65,1},{66,65},{67,129},{128... | collective-permute-start | bytes 196616 | tf_op jit(solution)/shard_map/ppermute | solution.py:221
  51.7 2.8 %collective-permute-start.15 = (bf16[2,128,128]{2,1,0:T(8,128)(2,1)S(1)}, bf16[2,128,128]{2,1,0:T(8,128)(2,1)S(1)}, u32[]{:S(2)}, u32[]{:S(2)}) collective-permute-start(bf16[2,128,128]{2,1,0:T(8,128)(2,1)S(1)} %get-tuple-element.32), channel_id=1, source_target_pairs={{0,0},{1,64},{2,128},{3,192},{64,1},{65,65},{66,129},{67,193},{128... | collective-permute-start | bytes 196616 | tf_op jit(solution)/shard_map/ppermute | solution.py:221
  54.5 1.9 %collective-permute-done.14 = bf16[2,128,128]{2,1,0:T(8,128)(2,1)S(1)} collective-permute-done((bf16[2,128,128]{2,1,0:T(8,128)(2,1)S(1)}, bf16[2,128,128]{2,1,0:T(8,128)(2,1)S(1)}, u32[]{:S(2)}, u32[]{:S(2)}) %collective-permute-start.14) | collective-permute-done | bytes 65568 | tf_op jit(solution)/shard_map/ppermute | solution.py:221
  56.4 6.8 %collective-permute-done.15 = bf16[2,128,128]{2,1,0:T(8,128)(2,1)S(1)} collective-permute-done((bf16[2,128,128]{2,1,0:T(8,128)(2,1)S(1)}, bf16[2,128,128]{2,1,0:T(8,128)(2,1)S(1)}, u32[]{:S(2)}, u32[]{:S(2)}) %collective-permute-start.15) | collective-permute-done | bytes 65568 | tf_op jit(solution)/shard_map/ppermute | solution.py:221
  63.2 0.7 %add_convert_fusion = bf16[2,128,128]{2,1,0:T(8,128)(2,1)} fusion(bf16[2,128,128]{2,1,0:T(8,128)(2,1)S(1)} %collective-permute-done.15, bf16[2,128,128]{2,1,0:T(8,128)(2,1)S(1)} %collective-permute-done.14, bf16[2,128,128]{2,1,0:T(8,128)(2,1)S(1)} %collective-permute-done.13, bf16[2,128,128]{2,1,0:T(8,128)(2,1)S(1)} %collective-permute-done.12), kind=kLoop, calls=%fused_computation | loop fusion | flops 262144 | bytes 327680 | tf_op jit(solution)/shard_map/convert_element_type | solution.py:353
  (13 shorter events, 0.0 us)
Async XLA Ops:
  0.9 5.6 %copy-start = (bf16[2048,128]{1,0:T(8,128)(2,1)S(1)}, bf16[2048,128]{1,0:T(8,128)(2,1)}, u32[]{:S(2)}) copy-start(bf16[2048,128]{1,0:T(8,128)(2,1)} %w_ref.1) | copy-start | bytes 1572868
  0.9 5.0 %collective-permute-start.1 = (bf16[16,2560]{1,0:T(8,128)(2,1)S(1)}, bf16[16,2560]{1,0:T(8,128)(2,1)S(1)}, u32[]{:S(2)}, u32[]{:S(2)}) collective-permute-start(bf16[16,2560]{1,0:T(8,128)(2,1)S(1)} %maximum_bitcast_fusion.m0), channel_id=1, source_target_pairs={{0,8},{8,0},{1,9},{9,1},{2,10},{10,2},{3,11},{11,3},{4,12},{12,4},... | collective-permute-start | bytes 245768 | tf_op jit(solution)/shard_map/ppermute | solution.py:221
  2.9 3.7 %collective-permute-start = (bf16[16,2560]{1,0:T(8,128)(2,1)S(1)}, bf16[16,2560]{1,0:T(8,128)(2,1)S(1)}, u32[]{:S(2)}, u32[]{:S(2)}) collective-permute-start(bf16[16,2560]{1,0:T(8,128)(2,1)S(1)} %maximum_bitcast_fusion.m0), channel_id=1, source_target_pairs={{0,4},{4,0},{1,5},{5,1},{2,6},{6,2},{3,7},{7,3},{8,12},{12,8},{9,1... | collective-permute-start | bytes 245768 | tf_op jit(solution)/shard_map/ppermute | solution.py:221
  5.9 1.5 %collective-permute-start.2 = (bf16[16,2560]{1,0:T(8,128)(2,1)S(1)}, bf16[16,2560]{1,0:T(8,128)(2,1)S(1)}, u32[]{:S(2)}, u32[]{:S(2)}) collective-permute-start(bf16[16,2560]{1,0:T(8,128)(2,1)S(1)} %relay.1.m2), channel_id=1, source_target_pairs={{0,4},{4,0},{1,5},{5,1},{2,6},{6,2},{3,7},{7,3},{8,12},{12,8},{9,1... | collective-permute-start | bytes 245768 | tf_op jit(solution)/shard_map/ppermute | solution.py:221
  6.5 7.6 %collective-permute-start.8 = (bf16[2048,128]{1,0:T(8,128)(2,1)S(1)}, bf16[2048,128]{1,0:T(8,128)(2,1)S(1)}, u32[]{:S(2)}, u32[]{:S(2)}) collective-permute-start(bf16[2048,128]{1,0:T(8,128)(2,1)S(1)} %copy-done), channel_id=1, source_target_pairs={{0,4},{4,0},{1,5},{5,1},{2,6},{6,2},{3,7},{7,3},{8,12},{12,8},{9,1... | collective-permute-start | bytes 1572872 | tf_op jit(solution)/shard_map/ppermute | solution.py:221
  10.6 5.2 %collective-permute-start.3 = (bf16[32,1024]{1,0:T(8,128)(2,1)S(1)}, bf16[32,1024]{1,0:T(8,128)(2,1)S(1)}, u32[]{:S(2)}, u32[]{:S(2)}) collective-permute-start(bf16[32,1024]{1,0:T(8,128)(2,1)S(1)} %get-tuple-element.25), channel_id=1, source_target_pairs={{0,12},{4,8},{8,4},{12,0},{1,13},{5,9},{9,5},{13,1},{2,14},{6,10},... | collective-permute-start | bytes 196616 | tf_op jit(solution)/shard_map/ppermute | solution.py:221
  11.6 4.8 %collective-permute-start.4 = (bf16[32,1024]{1,0:T(8,128)(2,1)S(1)}, bf16[32,1024]{1,0:T(8,128)(2,1)S(1)}, u32[]{:S(2)}, u32[]{:S(2)}) collective-permute-start(bf16[32,1024]{1,0:T(8,128)(2,1)S(1)} %get-tuple-element.26), channel_id=1, source_target_pairs={{0,8},{8,0},{1,9},{9,1},{2,10},{10,2},{3,11},{11,3},{4,12},{12,4},... | collective-permute-start | bytes 196616 | tf_op jit(solution)/shard_map/ppermute | solution.py:221
  12.6 3.8 %collective-permute-start.5 = (bf16[32,1024]{1,0:T(8,128)(2,1)S(1)}, bf16[32,1024]{1,0:T(8,128)(2,1)S(1)}, u32[]{:S(2)}, u32[]{:S(2)}) collective-permute-start(bf16[32,1024]{1,0:T(8,128)(2,1)S(1)} %get-tuple-element.27), channel_id=1, source_target_pairs={{0,4},{4,0},{1,5},{5,1},{2,6},{6,2},{3,7},{7,3},{8,12},{12,8},{9,1... | collective-permute-start | bytes 196616 | tf_op jit(solution)/shard_map/ppermute | solution.py:221
  12.6 12.4 %collective-permute-start.6 = (bf16[2048,128]{1,0:T(8,128)(2,1)S(1)}, bf16[2048,128]{1,0:T(8,128)(2,1)S(1)}, u32[]{:S(2)}, u32[]{:S(2)}) collective-permute-start(bf16[2048,128]{1,0:T(8,128)(2,1)S(1)} %copy-done), channel_id=1, source_target_pairs={{0,64},{4,196},{64,128},{68,4},{128,192},{132,68},{192,0},{196,132... | collective-permute-start | bytes 1572872 | tf_op jit(solution)/shard_map/ppermute | solution.py:221
  14.1 14.6 %collective-permute-start.9 = (bf16[2048,128]{1,0:T(8,128)(2,1)S(1)}, bf16[2048,128]{1,0:T(8,128)(2,1)S(1)}, u32[]{:S(2)}, u32[]{:S(2)}) collective-permute-start(bf16[2048,128]{1,0:T(8,128)(2,1)S(1)} %collective-permute-done.8), channel_id=1, source_target_pairs={{0,64},{4,196},{64,128},{68,4},{128,192},{132,68},{192,0},{196,132... | collective-permute-start | bytes 1572872 | tf_op jit(solution)/shard_map/ppermute | solution.py:221
  17.3 25.2 %all-to-all-start = ((bf16[8,32,1024]{2,1,0:T(8,128)(2,1)}), bf16[8,32,1024]{2,1,0:T(8,128)(2,1)S(1)}, u32[]{:S(2)}, u32[]{:S(2)}) async-start(bf16[8,32,1024]{2,1,0:T(8,128)(2,1)} %spread.1), calls=%async_computation | async-start | bytes 1048576 | tf_op jit(solution)/shard_map/all_to_all | solution.py:316
  25.1 10.5 %collective-permute-start.7 = (bf16[2048,128]{1,0:T(8,128)(2,1)S(1)}, bf16[2048,128]{1,0:T(8,128)(2,1)S(1)}, u32[]{:S(2)}, u32[]{:S(2)}) collective-permute-start(bf16[2048,128]{1,0:T(8,128)(2,1)S(1)} %collective-permute-done.6.w1), channel_id=1, source_target_pairs={{0,64},{4,196},{64,128},{68,4},{128,192},{132,68},{192,0},{196,132... | collective-permute-start | bytes 1572872 | tf_op jit(solution)/shard_map/ppermute | solution.py:221
  28.6 13.9 %collective-permute-start.10 = (bf16[2048,128]{1,0:T(8,128)(2,1)S(1)}, bf16[2048,128]{1,0:T(8,128)(2,1)S(1)}, u32[]{:S(2)}, u32[]{:S(2)}) collective-permute-start(bf16[2048,128]{1,0:T(8,128)(2,1)S(1)} %collective-permute-done.9), channel_id=1, source_target_pairs={{0,4},{4,0},{1,5},{5,1},{2,6},{6,2},{3,7},{7,3},{8,12},{12,8},{9,1... | collective-permute-start | bytes 1572872 | tf_op jit(solution)/shard_map/ppermute | solution.py:221
  42.5 1.9 %collective-permute-start.11 = (bf16[256,1024]{1,0:T(8,128)(2,1)S(1)}, bf16[256,1024]{1,0:T(8,128)(2,1)S(1)}, u32[]{:S(2)}, u32[]{:S(2)}) collective-permute-start(bf16[256,1024]{1,0:T(8,128)(2,1)S(1)} %hold.1.mine_ref), channel_id=1, source_target_pairs={{0,4},{4,0},{1,5},{5,1},{2,6},{6,2},{3,7},{7,3},{8,12},{12,8},{9,1... | collective-permute-start | bytes 1572872 | tf_op jit(solution)/shard_map/ppermute | solution.py:221
  45.2 9.3 %collective-permute-start.12 = (bf16[2,128,128]{2,1,0:T(8,128)(2,1)S(1)}, bf16[2,128,128]{2,1,0:T(8,128)(2,1)S(1)}, u32[]{:S(2)}, u32[]{:S(2)}) collective-permute-start(bf16[2,128,128]{2,1,0:T(8,128)(2,1)S(1)} %get-tuple-element.29), channel_id=1, source_target_pairs={{0,128},{1,192},{2,0},{3,64},{64,129},{65,193},{66,1},{67,65},{128... | collective-permute-start | bytes 196616 | tf_op jit(solution)/shard_map/ppermute | solution.py:221
  46.3 8.2 %collective-permute-start.13 = (bf16[2,128,128]{2,1,0:T(8,128)(2,1)S(1)}, bf16[2,128,128]{2,1,0:T(8,128)(2,1)S(1)}, u32[]{:S(2)}, u32[]{:S(2)}) collective-permute-start(bf16[2,128,128]{2,1,0:T(8,128)(2,1)S(1)} %get-tuple-element.30), channel_id=1, source_target_pairs={{0,64},{1,128},{2,192},{3,0},{64,65},{65,129},{66,193},{67,1},{128... | collective-permute-start | bytes 196616 | tf_op jit(solution)/shard_map/ppermute | solution.py:221
  48.5 7.9 %collective-permute-start.14 = (bf16[2,128,128]{2,1,0:T(8,128)(2,1)S(1)}, bf16[2,128,128]{2,1,0:T(8,128)(2,1)S(1)}, u32[]{:S(2)}, u32[]{:S(2)}) collective-permute-start(bf16[2,128,128]{2,1,0:T(8,128)(2,1)S(1)} %get-tuple-element.31), channel_id=1, source_target_pairs={{0,192},{1,0},{2,64},{3,128},{64,193},{65,1},{66,65},{67,129},{128... | collective-permute-start | bytes 196616 | tf_op jit(solution)/shard_map/ppermute | solution.py:221
  51.7 11.5 %collective-permute-start.15 = (bf16[2,128,128]{2,1,0:T(8,128)(2,1)S(1)}, bf16[2,128,128]{2,1,0:T(8,128)(2,1)S(1)}, u32[]{:S(2)}, u32[]{:S(2)}) collective-permute-start(bf16[2,128,128]{2,1,0:T(8,128)(2,1)S(1)} %get-tuple-element.32), channel_id=1, source_target_pairs={{0,0},{1,64},{2,128},{3,192},{64,1},{65,65},{66,129},{67,193},{128... | collective-permute-start | bytes 196616 | tf_op jit(solution)/shard_map/ppermute | solution.py:221

commit v6 on v5

--- a/solution.py
+++ b/solution.py
@@ -41,14 +41,14 @@
 
 
 def plan_kernel(
-    ancestors, lengths, key_ref, value_ref, w_ref,
-    sort_ref, back_ref, chunk_ref, keys, values, w0,
+    ancestors, lengths, key_ref, value_ref,
+    sort_ref, back_ref, chunk_ref, keys, values,
     anc_ref, len_ref, free, sems,
 ):
     loads = [
         pltpu.make_async_copy(src, dst, sems.at[k])
         for k, (src, dst) in enumerate(
-            ((ancestors, anc_ref), (lengths, len_ref), (key_ref, keys), (value_ref, values), (w_ref, w0))
+            ((ancestors, anc_ref), (lengths, len_ref), (key_ref, keys), (value_ref, values))
         )
     ]
     for load in loads:
@@ -112,7 +112,7 @@
     lane = lax.broadcasted_iota(jnp.int32, (8, 128), 1)
     slot = lax.broadcasted_iota(jnp.int32, (8 * GROUP, 128), 0) & 7
     extra = lax.broadcasted_iota(jnp.int32, (8 * GROUP, 128), 1)
-    ones = jnp.ones((HD, HD), BF16)
+    ones = jnp.ones((2 * HD, HD), BF16)
     last = (((1,), (1,)), ((), ()))
 
     def body(p, carry):
@@ -152,8 +152,8 @@
             mixes.append(jnp.dot(weights[:, :CACHE], values[h, g], preferred_element_type=F32))
             new_w.append(weights[:, CACHE:])
         new_mix = jnp.dot(jnp.concatenate(new_w), new_v, preferred_element_type=F32)
-        mass = jnp.dot(jnp.concatenate(folded), ones, preferred_element_type=F32)
-        mass += jnp.dot(jnp.concatenate(rest), ones, preferred_element_type=F32)
+        halves = jnp.concatenate([jnp.concatenate(folded), jnp.concatenate(rest)], axis=1)
+        mass = jnp.dot(halves, ones, preferred_element_type=F32)
         for w, (h, g, rows, _, _, _, _, _) in enumerate(jobs):
             mine = slice(w * 8 * GROUP, (w + 1) * 8 * GROUP)
             out = (mixes[w] + new_mix[mine]) / mass[mine]
@@ -169,6 +169,12 @@
         both = jnp.dot(turn, feats, preferred_element_type=F32).astype(BF16)
         for zz, out in enumerate(outs):
             out[...] = both[zz * FAMILY : (zz + 1) * FAMILY]
+
+
+def bring_kernel(src, dst, sem):
+    load = pltpu.make_async_copy(src, dst, sem)
+    load.start()
+    load.wait()
 
 
 def spread_kernel(a_ref, b_ref, c_ref, d_ref, out_ref):
@@ -259,7 +265,7 @@
     m0 = jnp.concatenate([queries, new_keys, new_values], axis=-1).reshape(2 * HOLD, WIDE)
     m1 = swap_core(m0)
     m2 = swap_chip(m0)
-    sort, back, chunks, keys, values, w0 = pl.pallas_call(
+    sort, back, chunks, keys, values = pl.pallas_call(
         plan_kernel,
         out_shape=[
             shape(SLOTS + 8, 128, dtype=F32),
@@ -267,20 +273,29 @@
             shape(CHUNKS + 2 + HOLD, dtype=jnp.int32),
             pltpu.VMEM(key_cache.shape, BF16),
             pltpu.VMEM(value_cache.shape, BF16),
-            pltpu.VMEM(out_weight.shape, BF16),
         ],
-        in_specs=[HBM] * 5,
-        out_specs=[VMEM, VMEM, SMEM, VMEM, VMEM, VMEM],
+        in_specs=[HBM] * 4,
+        out_specs=[VMEM, VMEM, SMEM, VMEM, VMEM],
         scratch_shapes=[
             pltpu.SMEM(ancestors.shape, jnp.int32),
             pltpu.SMEM((HOLD,), jnp.int32),
             pltpu.SMEM((HOLD + 1,), jnp.int32),
-            pltpu.SemaphoreType.DMA((5,)),
+            pltpu.SemaphoreType.DMA((4,)),
         ],
         compiler_params=LIMIT,
         cost_estimate=TINY,
         name="plan",
-    )(*(pltpu.with_memory_space_constraint(v, pltpu.HBM) for v in (ancestors, lengths, key_cache, value_cache, out_weight)))
+    )(*(pltpu.with_memory_space_constraint(v, pltpu.HBM) for v in (ancestors, lengths, key_cache, value_cache)))
+    w0 = pl.pallas_call(
+        bring_kernel,
+        out_shape=pltpu.VMEM(out_weight.shape, BF16),
+        in_specs=[HBM],
+        out_specs=VMEM,
+        scratch_shapes=[pltpu.SemaphoreType.DMA],
+        compiler_params=LIMIT,
+        cost_estimate=TINY,
+        name="bring",
+    )(pltpu.with_memory_space_constraint(out_weight, pltpu.HBM))
     def along(v):
         return permute(v, ("y", "c"), lambda y, c: (y + 1 + 2 * c, c))
 
@@ -320,13 +335,13 @@
     mine = pl.pallas_call(
         hold_kernel,
         out_shape=shape(8 * FAMILY, HALF),
-        in_specs=[VMEM] * 3,
+        in_specs=[VMEM] * 4,
         out_specs=VMEM,
         input_output_aliases={0: 0},
         compiler_params=LIMIT,
         cost_estimate=TINY,
         name="hold",
-    )(mine, w_far, w_back)
+    )(mine, w_far, w_back, w0)
     other = swap_core(mine)
     acc = pl.pallas_call(
         own_half_kernel,

time: 63.9 us -> 63.3 us (level)
  waiting for transfers between devices: 27.6 us -> 25.3 us
  starting transfers between devices: 26.2 us -> 27.5 us
    ppermute x16, waiting for transfers between devices: 20.6 us -> 18.4 us  [permute(): return lax.ppermute(value, axes, pairs)]
    ppermute x16, starting transfers between devices: 18.4 us -> 19.6 us  [permute(): return lax.ppermute(value, axes, pairs)]
    pallas_call x0 -> x1, Pallas kernels: none -> 1.05 us  [per_device(): pl.pallas_call(bring_kernel, out_shape=pltpu.VMEM(out_weight.shape, BF16)...]
    pallas_call x1, Pallas kernels: 3.19 us -> 2.16 us  [attend_call(): pl.pallas_call(attend_kernel, out_shape=[shape(FAMILY, HALF)] * 4, in_spe...]
where the time goes in v6:
time: 63.3 us; the launch traced here: 62.9 us
  starting transfers between devices  27.5 us (43%)
  waiting for transfers between devices  25.3 us (40%)
  Pallas kernels  8.33 us (13%)
  other arithmetic  1.55 us (2%)
    ppermute x16, starting transfers between devices, permute(): return lax.ppermute(value, axes, pairs)  19.6 us
    ppermute x16, waiting for transfers between devices, permute(): return lax.ppermute(value, axes, pairs)  18.4 us
    all_to_all x1, starting transfers between devices, per_device(): lax.all_to_all(spread, Z, split_axis=0, concat_axis=0)  7.89 us
    all_to_all x1, waiting for transfers between devices, per_device(): lax.all_to_all(spread, Z, split_axis=0, concat_axis=0)  6.94 us
    pallas_call x1, Pallas kernels, per_device(): pl.pallas_call(plan_kernel, out_shape=[shape(SLOTS + 8, 128, dtype=F32),...  2.85 us
    pallas_call x1, Pallas kernels, attend_call(): pl.pallas_call(attend_kernel, out_shape=[shape(FAMILY, HALF)] * 4, in_spe...  2.16 us
  transfers between devices with their start and end apart: 17, of which 8 were waited for; matrix products, arithmetic and copies ran while one was open for 0% of the time, Pallas kernels for 12%

profile of v6, /device:TPU:6, one launch (start us, length us, event | category | flops | bytes accessed | tf_op | source)
XLA Modules:
  0.0 62.9 jit_solution(11909691275138920997)
XLA Ops:
  0.0 0.9 %maximum_bitcast_fusion.m0 = bf16[16,2560]{1,0:T(8,128)(2,1)S(1)} fusion(bf16[2,8,256]{2,1,0:T(8,128)(2,1)} %param.12, bf16[2,8,256]{2,1,0:T(8,128)(2,1)} %param.11, bf16[2,8,2048]{2,1,0:T(8,128)(2,1)} %param.8), kind=kLoop, calls=%fused_computation.1 | loop fusion | flops 245760 | bytes 163840 | tf_op jit(solution)/shard_map/reshape | solution.py:265
  0.9 2.0 %collective-permute-start.1 = (bf16[16,2560]{1,0:T(8,128)(2,1)S(1)}, bf16[16,2560]{1,0:T(8,128)(2,1)S(1)}, u32[]{:S(2)}, u32[]{:S(2)}) collective-permute-start(bf16[16,2560]{1,0:T(8,128)(2,1)S(1)} %maximum_bitcast_fusion.m0), channel_id=1, source_target_pairs={{0,8},{8,0},{1,9},{9,1},{2,10},{10,2},{3,11},{11,3},{4,12},{12,4},... | collective-permute-start | bytes 245768 | tf_op jit(solution)/shard_map/ppermute | solution.py:227
  2.9 2.9 %plan.1 = (f32[136,128]{1,0:T(8,128)S(1)}, f32[64,128]{1,0:T(8,128)S(1)}, s32[26]{0:T(128)S(1)}, bf16[8,2,512,128]{3,2,1,0:T(8,128)(2,1)S(1)}, bf16[8,2,512,128]{3,2,1,0:T(8,128)(2,1)S(1)}) custom-call(s32[2,512]{1,0:T(2,128)} %ancestors.1, s32[8]{0:T(128)} %lengths.1, bf16[8,2,512,128]{3,2,1,0:T(8,128)(2,1)} %key_ref.1, bf16[8,2,512,128]{3,2,1,0:T(8,128)(2,1)} %value_ref.1), custom_call_target="tpu_custom_call" | custom-call | flops 1000000 | bytes 100000 | tf_op jit(solution)/shard_map/plan/pallas_call | solution.py:268
  5.7 0.0 collective-permute-done.1.refs_0_
  5.8 0.6 collective-permute-start.2
  6.4 0.1 collective-permute-start.8
  6.5 0.8 %collective-permute-done.2.m3 = bf16[16,2560]{1,0:T(8,128)(2,1)S(1)} collective-permute-done((bf16[16,2560]{1,0:T(8,128)(2,1)S(1)}, bf16[16,2560]{1,0:T(8,128)(2,1)S(1)}, u32[]{:S(2)}, u32[]{:S(2)}) %collective-permute-start.2) | collective-permute-done | bytes 81952 | tf_op jit(solution)/shard_map/ppermute | solution.py:227
  7.3 2.2 %attend.1 = (bf16[32,1024]{1,0:T(8,128)(2,1)S(1)}, bf16[32,1024]{1,0:T(8,128)(2,1)S(1)}, bf16[32,1024]{1,0:T(8,128)(2,1)S(1)}, bf16[32,1024]{1,0:T(8,128)(2,1)S(1)}) custom-call(f32[136,128]{1,0:T(8,128)S(1)} %get-tuple-element.18.plan, f32[64,128]{1,0:T(8,128)S(1)} %get-tuple-element.19.refs_1_.back, s32[26]{0:T(128)S(1)} %get-tuple-element.20.chunks, ...), custom_call_target="tpu_custom_call" | custom-call | flops 7000000000 | bytes 1000000 | tf_op jit(solution)/shard_map/attend/pallas_call | solution.py:247
  9.4 2.2 %collective-permute-start.3 = (bf16[32,1024]{1,0:T(8,128)(2,1)S(1)}, bf16[32,1024]{1,0:T(8,128)(2,1)S(1)}, u32[]{:S(2)}, u32[]{:S(2)}) collective-permute-start(bf16[32,1024]{1,0:T(8,128)(2,1)S(1)} %get-tuple-element.24), channel_id=1, source_target_pairs={{0,12},{4,8},{8,4},{12,0},{1,13},{5,9},{9,5},{13,1},{2,14},{6,10},... | collective-permute-start | bytes 196616 | tf_op jit(solution)/shard_map/ppermute | solution.py:227
  11.7 0.9 %collective-permute-start.4 = (bf16[32,1024]{1,0:T(8,128)(2,1)S(1)}, bf16[32,1024]{1,0:T(8,128)(2,1)S(1)}, u32[]{:S(2)}, u32[]{:S(2)}) collective-permute-start(bf16[32,1024]{1,0:T(8,128)(2,1)S(1)} %get-tuple-element.25), channel_id=1, source_target_pairs={{0,8},{8,0},{1,9},{9,1},{2,10},{10,2},{3,11},{11,3},{4,12},{12,4},... | collective-permute-start | bytes 196616 | tf_op jit(solution)/shard_map/ppermute | solution.py:227
  12.6 1.6 %collective-permute-start.6 = (bf16[2048,128]{1,0:T(8,128)(2,1)S(1)}, bf16[2048,128]{1,0:T(8,128)(2,1)S(1)}, u32[]{:S(2)}, u32[]{:S(2)}) collective-permute-start(bf16[2048,128]{1,0:T(8,128)(2,1)S(1)} %copy-done), channel_id=1, source_target_pairs={{0,64},{4,196},{64,128},{68,4},{128,192},{132,68},{192,0},{196,132... | collective-permute-start | bytes 1572872 | tf_op jit(solution)/shard_map/ppermute | solution.py:227
  14.1 0.0 collective-permute-done.8
  14.1 1.6 %collective-permute-start.9 = (bf16[2048,128]{1,0:T(8,128)(2,1)S(1)}, bf16[2048,128]{1,0:T(8,128)(2,1)}, u32[]{:S(2)}, u32[]{:S(2)}) collective-permute-start(bf16[2048,128]{1,0:T(8,128)(2,1)S(1)} %collective-permute-done.8), channel_id=1, source_target_pairs={{0,64},{4,196},{64,128},{68,4},{128,192},{132,68},{192,0},{196,132... | collective-permute-start | bytes 1572872 | tf_op jit(solution)/shard_map/ppermute | solution.py:227
  15.7 0.2 collective-permute-done.4.c_ref
  15.9 0.8 %spread.1 = bf16[8,32,1024]{2,1,0:T(8,128)(2,1)} custom-call(bf16[32,1024]{1,0:T(8,128)(2,1)S(1)} %get-tuple-element.23.a_ref, bf16[32,1024]{1,0:T(8,128)(2,1)S(1)} %collective-permute-done.3.b_ref, bf16[32,1024]{1,0:T(8,128)(2,1)S(1)} %collective-permute-done.4.c_ref, bf16[32,1024]{1,0:T(8,128)(2,1)S(1)} %collective-permute-done.5.d_ref), custom_call_target="tpu_custom_call" | custom-call | flops 12000000000 | bytes 100000 | tf_op jit(solution)/shard_map/spread/pallas_call | solution.py:322
  16.8 7.9 %all-to-all-start = ((bf16[8,32,1024]{2,1,0:T(8,128)(2,1)}), bf16[8,32,1024]{2,1,0:T(8,128)(2,1)S(1)}, u32[]{:S(2)}, u32[]{:S(2)}) async-start(bf16[8,32,1024]{2,1,0:T(8,128)(2,1)} %spread.1), calls=%async_computation | async-start | bytes 1048576 | tf_op jit(solution)/shard_map/all_to_all | solution.py:331
  24.7 1.2 %collective-permute-start.7 = (bf16[2048,128]{1,0:T(8,128)(2,1)S(1)}, bf16[2048,128]{1,0:T(8,128)(2,1)S(1)}, u32[]{:S(2)}, u32[]{:S(2)}) collective-permute-start(bf16[2048,128]{1,0:T(8,128)(2,1)S(1)} %collective-permute-done.6.w1), channel_id=1, source_target_pairs={{0,64},{4,196},{64,128},{68,4},{128,192},{132,68},{192,0},{196,132... | collective-permute-start | bytes 1572872 | tf_op jit(solution)/shard_map/ppermute | solution.py:227
  25.9 2.8 %collective-permute-done.9 = bf16[2048,128]{1,0:T(8,128)(2,1)} collective-permute-done((bf16[2048,128]{1,0:T(8,128)(2,1)S(1)}, bf16[2048,128]{1,0:T(8,128)(2,1)}, u32[]{:S(2)}, u32[]{:S(2)}) %collective-permute-start.9) | collective-permute-done | bytes 524320 | tf_op jit(solution)/shard_map/ppermute | solution.py:227
  28.7 1.1 %bring.1.refs_3_.w0 = bf16[2048,128]{1,0:T(8,128)(2,1)S(1)} custom-call(bf16[2048,128]{1,0:T(8,128)(2,1)} %src.1), custom_call_target="tpu_custom_call" | custom-call | flops 1000000 | bytes 100000 | tf_op jit(solution)/shard_map/bring/pallas_call | solution.py:289
  29.7 5.4 %collective-permute-done.7.refs_1_.w2 = bf16[2048,128]{1,0:T(8,128)(2,1)S(1)} collective-permute-done((bf16[2048,128]{1,0:T(8,128)(2,1)S(1)}, bf16[2048,128]{1,0:T(8,128)(2,1)S(1)}, u32[]{:S(2)}, u32[]{:S(2)}) %collective-permute-start.7) | collective-permute-done | bytes 524320 | tf_op jit(solution)/shard_map/ppermute | solution.py:227
  35.1 6.9 %all-to-all-done = bf16[8,32,1024]{2,1,0:T(8,128)(2,1)S(1)} async-done(((bf16[8,32,1024]{2,1,0:T(8,128)(2,1)}), bf16[8,32,1024]{2,1,0:T(8,128)(2,1)S(1)}, u32[]{:S(2)}, u32[]{:S(2)}) %all-to-all-start) | async-done | bytes 524320 | tf_op jit(solution)/shard_map/all_to_all | solution.py:331
  42.1 0.0 collective-permute-start.11
  42.1 0.7 %own_half.1.acc_ref = f32[4,256,128]{2,1,0:T(8,128)S(1)} custom-call(bf16[256,1024]{1,0:T(8,128)(2,1)S(1)} %hold.1.mine_ref, bf16[2048,128]{1,0:T(8,128)(2,1)S(1)} %bring.1.refs_3_.w0, bf16[2048,128]{1,0:T(8,128)(2,1)S(1)} %collective-permute-done.6.w1, bf16[2048,128]{1,0:T(8,128)(2,1)S(1)} %collective-permute-done.7.refs_1_.w2, ...), custom_call_target="tpu_custom_call" | custom-call | flops 1000000000 | bytes 1000000 | tf_op jit(solution)/shard_map/own_half/pallas_call | solution.py:346
  42.8 1.2 %collective-permute-done.11.other_ref = bf16[256,1024]{1,0:T(8,128)(2,1)S(1)} collective-permute-done((bf16[256,1024]{1,0:T(8,128)(2,1)S(1)}, bf16[256,1024]{1,0:T(8,128)(2,1)S(1)}, u32[]{:S(2)}, u32[]{:S(2)}) %collective-permute-start.11) | collective-permute-done | bytes 524320 | tf_op jit(solution)/shard_map/ppermute | solution.py:227
  44.0 0.7 %other_half.1 = (bf16[2,128,128]{2,1,0:T(8,128)(2,1)S(1)}, bf16[2,128,128]{2,1,0:T(8,128)(2,1)S(1)}, bf16[2,128,128]{2,1,0:T(8,128)(2,1)S(1)}, bf16[2,128,128]{2,1,0:T(8,128)(2,1)S(1)}) custom-call(bf16[256,1024]{1,0:T(8,128)(2,1)S(1)} %collective-permute-done.11.other_ref, f32[4,256,128]{2,1,0:T(8,128)S(1)} %own_half.1.acc_ref, ...), custom_call_target="tpu_custom_call" | custom-call | flops 1000000000 | bytes 1000000 | tf_op jit(solution)/shard_map/other_half/pallas_call | solution.py:355
  44.7 1.2 %collective-permute-start.12 = (bf16[2,128,128]{2,1,0:T(8,128)(2,1)S(1)}, bf16[2,128,128]{2,1,0:T(8,128)(2,1)S(1)}, u32[]{:S(2)}, u32[]{:S(2)}) collective-permute-start(bf16[2,128,128]{2,1,0:T(8,128)(2,1)S(1)} %get-tuple-element.27), channel_id=1, source_target_pairs={{0,128},{1,192},{2,0},{3,64},{64,129},{65,193},{66,1},{67,65},{128... | collective-permute-start | bytes 196616 | tf_op jit(solution)/shard_map/ppermute | solution.py:227
  46.0 2.1 %collective-permute-start.13 = (bf16[2,128,128]{2,1,0:T(8,128)(2,1)S(1)}, bf16[2,128,128]{2,1,0:T(8,128)(2,1)S(1)}, u32[]{:S(2)}, u32[]{:S(2)}) collective-permute-start(bf16[2,128,128]{2,1,0:T(8,128)(2,1)S(1)} %get-tuple-element.28), channel_id=1, source_target_pairs={{0,64},{1,128},{2,192},{3,0},{64,65},{65,129},{66,193},{67,1},{128... | collective-permute-start | bytes 196616 | tf_op jit(solution)/shard_map/ppermute | solution.py:227
  48.1 3.2 %collective-permute-start.14 = (bf16[2,128,128]{2,1,0:T(8,128)(2,1)S(1)}, bf16[2,128,128]{2,1,0:T(8,128)(2,1)S(1)}, u32[]{:S(2)}, u32[]{:S(2)}) collective-permute-start(bf16[2,128,128]{2,1,0:T(8,128)(2,1)S(1)} %get-tuple-element.29), channel_id=1, source_target_pairs={{0,192},{1,0},{2,64},{3,128},{64,193},{65,1},{66,65},{67,129},{128... | collective-permute-start | bytes 196616 | tf_op jit(solution)/shard_map/ppermute | solution.py:227
  51.3 2.9 %collective-permute-start.15 = (bf16[2,128,128]{2,1,0:T(8,128)(2,1)S(1)}, bf16[2,128,128]{2,1,0:T(8,128)(2,1)S(1)}, u32[]{:S(2)}, u32[]{:S(2)}) collective-permute-start(bf16[2,128,128]{2,1,0:T(8,128)(2,1)S(1)} %get-tuple-element.30), channel_id=1, source_target_pairs={{0,0},{1,64},{2,128},{3,192},{64,1},{65,65},{66,129},{67,193},{128... | collective-permute-start | bytes 196616 | tf_op jit(solution)/shard_map/ppermute | solution.py:227
  54.2 1.8 %collective-permute-done.14 = bf16[2,128,128]{2,1,0:T(8,128)(2,1)S(1)} collective-permute-done((bf16[2,128,128]{2,1,0:T(8,128)(2,1)S(1)}, bf16[2,128,128]{2,1,0:T(8,128)(2,1)S(1)}, u32[]{:S(2)}, u32[]{:S(2)}) %collective-permute-start.14) | collective-permute-done | bytes 65568 | tf_op jit(solution)/shard_map/ppermute | solution.py:227
  55.9 6.2 %collective-permute-done.15 = bf16[2,128,128]{2,1,0:T(8,128)(2,1)S(1)} collective-permute-done((bf16[2,128,128]{2,1,0:T(8,128)(2,1)S(1)}, bf16[2,128,128]{2,1,0:T(8,128)(2,1)S(1)}, u32[]{:S(2)}, u32[]{:S(2)}) %collective-permute-start.15) | collective-permute-done | bytes 65568 | tf_op jit(solution)/shard_map/ppermute | solution.py:227
  62.2 0.7 %add_convert_fusion = bf16[2,128,128]{2,1,0:T(8,128)(2,1)} fusion(bf16[2,128,128]{2,1,0:T(8,128)(2,1)S(1)} %collective-permute-done.15, bf16[2,128,128]{2,1,0:T(8,128)(2,1)S(1)} %collective-permute-done.14, bf16[2,128,128]{2,1,0:T(8,128)(2,1)S(1)} %collective-permute-done.13, bf16[2,128,128]{2,1,0:T(8,128)(2,1)S(1)} %collective-permute-done.12), kind=kLoop, calls=%fused_computation | loop fusion | flops 262144 | bytes 327680 | tf_op jit(solution)/shard_map/convert_element_type | solution.py:368
  (14 shorter events, 0.0 us)
Async XLA Ops:
  0.9 5.5 %copy-start = (bf16[2048,128]{1,0:T(8,128)(2,1)S(1)}, bf16[2048,128]{1,0:T(8,128)(2,1)}, u32[]{:S(2)}) copy-start(bf16[2048,128]{1,0:T(8,128)(2,1)} %src.1) | copy-start | bytes 1572868
  0.9 4.9 %collective-permute-start.1 = (bf16[16,2560]{1,0:T(8,128)(2,1)S(1)}, bf16[16,2560]{1,0:T(8,128)(2,1)S(1)}, u32[]{:S(2)}, u32[]{:S(2)}) collective-permute-start(bf16[16,2560]{1,0:T(8,128)(2,1)S(1)} %maximum_bitcast_fusion.m0), channel_id=1, source_target_pairs={{0,8},{8,0},{1,9},{9,1},{2,10},{10,2},{3,11},{11,3},{4,12},{12,4},... | collective-permute-start | bytes 245768 | tf_op jit(solution)/shard_map/ppermute | solution.py:227
  2.9 3.6 %collective-permute-start = (bf16[16,2560]{1,0:T(8,128)(2,1)S(1)}, bf16[16,2560]{1,0:T(8,128)(2,1)S(1)}, u32[]{:S(2)}, u32[]{:S(2)}) collective-permute-start(bf16[16,2560]{1,0:T(8,128)(2,1)S(1)} %maximum_bitcast_fusion.m0), channel_id=1, source_target_pairs={{0,4},{4,0},{1,5},{5,1},{2,6},{6,2},{3,7},{7,3},{8,12},{12,8},{9,1... | collective-permute-start | bytes 245768 | tf_op jit(solution)/shard_map/ppermute | solution.py:227
  5.8 1.5 %collective-permute-start.2 = (bf16[16,2560]{1,0:T(8,128)(2,1)S(1)}, bf16[16,2560]{1,0:T(8,128)(2,1)S(1)}, u32[]{:S(2)}, u32[]{:S(2)}) collective-permute-start(bf16[16,2560]{1,0:T(8,128)(2,1)S(1)} %relay.1.m2), channel_id=1, source_target_pairs={{0,4},{4,0},{1,5},{5,1},{2,6},{6,2},{3,7},{7,3},{8,12},{12,8},{9,1... | collective-permute-start | bytes 245768 | tf_op jit(solution)/shard_map/ppermute | solution.py:227
  6.4 7.8 %collective-permute-start.8 = (bf16[2048,128]{1,0:T(8,128)(2,1)S(1)}, bf16[2048,128]{1,0:T(8,128)(2,1)S(1)}, u32[]{:S(2)}, u32[]{:S(2)}) collective-permute-start(bf16[2048,128]{1,0:T(8,128)(2,1)S(1)} %copy-done), channel_id=1, source_target_pairs={{0,4},{4,0},{1,5},{5,1},{2,6},{6,2},{3,7},{7,3},{8,12},{12,8},{9,1... | collective-permute-start | bytes 1572872 | tf_op jit(solution)/shard_map/ppermute | solution.py:227
  9.4 6.3 %collective-permute-start.3 = (bf16[32,1024]{1,0:T(8,128)(2,1)S(1)}, bf16[32,1024]{1,0:T(8,128)(2,1)S(1)}, u32[]{:S(2)}, u32[]{:S(2)}) collective-permute-start(bf16[32,1024]{1,0:T(8,128)(2,1)S(1)} %get-tuple-element.24), channel_id=1, source_target_pairs={{0,12},{4,8},{8,4},{12,0},{1,13},{5,9},{9,5},{13,1},{2,14},{6,10},... | collective-permute-start | bytes 196616 | tf_op jit(solution)/shard_map/ppermute | solution.py:227
  11.7 4.3 %collective-permute-start.4 = (bf16[32,1024]{1,0:T(8,128)(2,1)S(1)}, bf16[32,1024]{1,0:T(8,128)(2,1)S(1)}, u32[]{:S(2)}, u32[]{:S(2)}) collective-permute-start(bf16[32,1024]{1,0:T(8,128)(2,1)S(1)} %get-tuple-element.25), channel_id=1, source_target_pairs={{0,8},{8,0},{1,9},{9,1},{2,10},{10,2},{3,11},{11,3},{4,12},{12,4},... | collective-permute-start | bytes 196616 | tf_op jit(solution)/shard_map/ppermute | solution.py:227
  12.6 3.4 %collective-permute-start.5 = (bf16[32,1024]{1,0:T(8,128)(2,1)S(1)}, bf16[32,1024]{1,0:T(8,128)(2,1)S(1)}, u32[]{:S(2)}, u32[]{:S(2)}) collective-permute-start(bf16[32,1024]{1,0:T(8,128)(2,1)S(1)} %get-tuple-element.26), channel_id=1, source_target_pairs={{0,4},{4,0},{1,5},{5,1},{2,6},{6,2},{3,7},{7,3},{8,12},{12,8},{9,1... | collective-permute-start | bytes 196616 | tf_op jit(solution)/shard_map/ppermute | solution.py:227
  12.6 12.1 %collective-permute-start.6 = (bf16[2048,128]{1,0:T(8,128)(2,1)S(1)}, bf16[2048,128]{1,0:T(8,128)(2,1)S(1)}, u32[]{:S(2)}, u32[]{:S(2)}) collective-permute-start(bf16[2048,128]{1,0:T(8,128)(2,1)S(1)} %copy-done), channel_id=1, source_target_pairs={{0,64},{4,196},{64,128},{68,4},{128,192},{132,68},{192,0},{196,132... | collective-permute-start | bytes 1572872 | tf_op jit(solution)/shard_map/ppermute | solution.py:227
  14.1 14.5 %collective-permute-start.9 = (bf16[2048,128]{1,0:T(8,128)(2,1)S(1)}, bf16[2048,128]{1,0:T(8,128)(2,1)}, u32[]{:S(2)}, u32[]{:S(2)}) collective-permute-start(bf16[2048,128]{1,0:T(8,128)(2,1)S(1)} %collective-permute-done.8), channel_id=1, source_target_pairs={{0,64},{4,196},{64,128},{68,4},{128,192},{132,68},{192,0},{196,132... | collective-permute-start | bytes 1572872 | tf_op jit(solution)/shard_map/ppermute | solution.py:227
  16.8 25.3 %all-to-all-start = ((bf16[8,32,1024]{2,1,0:T(8,128)(2,1)}), bf16[8,32,1024]{2,1,0:T(8,128)(2,1)S(1)}, u32[]{:S(2)}, u32[]{:S(2)}) async-start(bf16[8,32,1024]{2,1,0:T(8,128)(2,1)} %spread.1), calls=%async_computation | async-start | bytes 1048576 | tf_op jit(solution)/shard_map/all_to_all | solution.py:331
  24.7 10.5 %collective-permute-start.7 = (bf16[2048,128]{1,0:T(8,128)(2,1)S(1)}, bf16[2048,128]{1,0:T(8,128)(2,1)S(1)}, u32[]{:S(2)}, u32[]{:S(2)}) collective-permute-start(bf16[2048,128]{1,0:T(8,128)(2,1)S(1)} %collective-permute-done.6.w1), channel_id=1, source_target_pairs={{0,64},{4,196},{64,128},{68,4},{128,192},{132,68},{192,0},{196,132... | collective-permute-start | bytes 1572872 | tf_op jit(solution)/shard_map/ppermute | solution.py:227
  28.7 13.4 %collective-permute-start.10 = (bf16[2048,128]{1,0:T(8,128)(2,1)}, bf16[2048,128]{1,0:T(8,128)(2,1)S(1)}, u32[]{:S(2)}, u32[]{:S(2)}) collective-permute-start(bf16[2048,128]{1,0:T(8,128)(2,1)} %collective-permute-done.9), channel_id=1, source_target_pairs={{0,4},{4,0},{1,5},{5,1},{2,6},{6,2},{3,7},{7,3},{8,12},{12,8},{9,1... | collective-permute-start | bytes 1572872 | tf_op jit(solution)/shard_map/ppermute | solution.py:227
  42.1 1.9 %collective-permute-start.11 = (bf16[256,1024]{1,0:T(8,128)(2,1)S(1)}, bf16[256,1024]{1,0:T(8,128)(2,1)S(1)}, u32[]{:S(2)}, u32[]{:S(2)}) collective-permute-start(bf16[256,1024]{1,0:T(8,128)(2,1)S(1)} %hold.1.mine_ref), channel_id=1, source_target_pairs={{0,4},{4,0},{1,5},{5,1},{2,6},{6,2},{3,7},{7,3},{8,12},{12,8},{9,1... | collective-permute-start | bytes 1572872 | tf_op jit(solution)/shard_map/ppermute | solution.py:227
  44.7 9.4 %collective-permute-start.12 = (bf16[2,128,128]{2,1,0:T(8,128)(2,1)S(1)}, bf16[2,128,128]{2,1,0:T(8,128)(2,1)S(1)}, u32[]{:S(2)}, u32[]{:S(2)}) collective-permute-start(bf16[2,128,128]{2,1,0:T(8,128)(2,1)S(1)} %get-tuple-element.27), channel_id=1, source_target_pairs={{0,128},{1,192},{2,0},{3,64},{64,129},{65,193},{66,1},{67,65},{128... | collective-permute-start | bytes 196616 | tf_op jit(solution)/shard_map/ppermute | solution.py:227
  46.0 8.2 %collective-permute-start.13 = (bf16[2,128,128]{2,1,0:T(8,128)(2,1)S(1)}, bf16[2,128,128]{2,1,0:T(8,128)(2,1)S(1)}, u32[]{:S(2)}, u32[]{:S(2)}) collective-permute-start(bf16[2,128,128]{2,1,0:T(8,128)(2,1)S(1)} %get-tuple-element.28), channel_id=1, source_target_pairs={{0,64},{1,128},{2,192},{3,0},{64,65},{65,129},{66,193},{67,1},{128... | collective-permute-start | bytes 196616 | tf_op jit(solution)/shard_map/ppermute | solution.py:227
  48.1 7.9 %collective-permute-start.14 = (bf16[2,128,128]{2,1,0:T(8,128)(2,1)S(1)}, bf16[2,128,128]{2,1,0:T(8,128)(2,1)S(1)}, u32[]{:S(2)}, u32[]{:S(2)}) collective-permute-start(bf16[2,128,128]{2,1,0:T(8,128)(2,1)S(1)} %get-tuple-element.29), channel_id=1, source_target_pairs={{0,192},{1,0},{2,64},{3,128},{64,193},{65,1},{66,65},{67,129},{128... | collective-permute-start | bytes 196616 | tf_op jit(solution)/shard_map/ppermute | solution.py:227
  51.3 10.9 %collective-permute-start.15 = (bf16[2,128,128]{2,1,0:T(8,128)(2,1)S(1)}, bf16[2,128,128]{2,1,0:T(8,128)(2,1)S(1)}, u32[]{:S(2)}, u32[]{:S(2)}) collective-permute-start(bf16[2,128,128]{2,1,0:T(8,128)(2,1)S(1)} %get-tuple-element.30), channel_id=1, source_target_pairs={{0,0},{1,64},{2,128},{3,192},{64,1},{65,65},{66,129},{67,193},{128... | collective-permute-start | bytes 196616 | tf_op jit(solution)/shard_map/ppermute | solution.py:227

commit v7 on v5

--- a/solution.py
+++ b/solution.py
@@ -112,7 +112,7 @@
     lane = lax.broadcasted_iota(jnp.int32, (8, 128), 1)
     slot = lax.broadcasted_iota(jnp.int32, (8 * GROUP, 128), 0) & 7
     extra = lax.broadcasted_iota(jnp.int32, (8 * GROUP, 128), 1)
-    ones = jnp.ones((HD, HD), BF16)
+    ones = jnp.ones((2 * HD, HD), BF16)
     last = (((1,), (1,)), ((), ()))
 
     def body(p, carry):
@@ -152,8 +152,8 @@
             mixes.append(jnp.dot(weights[:, :CACHE], values[h, g], preferred_element_type=F32))
             new_w.append(weights[:, CACHE:])
         new_mix = jnp.dot(jnp.concatenate(new_w), new_v, preferred_element_type=F32)
-        mass = jnp.dot(jnp.concatenate(folded), ones, preferred_element_type=F32)
-        mass += jnp.dot(jnp.concatenate(rest), ones, preferred_element_type=F32)
+        halves = jnp.concatenate([jnp.concatenate(folded), jnp.concatenate(rest)], axis=1)
+        mass = jnp.dot(halves, ones, preferred_element_type=F32)
         for w, (h, g, rows, _, _, _, _, _) in enumerate(jobs):
             mine = slice(w * 8 * GROUP, (w + 1) * 8 * GROUP)
             out = (mixes[w] + new_mix[mine]) / mass[mine]

time: 63.9 us -> 63.2 us (0.989)
  waiting for transfers between devices: 27.6 us -> 25.5 us
  starting transfers between devices: 26.2 us -> 27.1 us
    ppermute x16, waiting for transfers between devices: 20.6 us -> 18.6 us  [permute(): return lax.ppermute(value, axes, pairs)]
    ppermute x16, starting transfers between devices: 18.4 us -> 19.3 us  [permute(): return lax.ppermute(value, axes, pairs)]
where the time goes in v7:
time: 63.2 us; the launch traced here: 62.7 us
  starting transfers between devices  27.1 us (43%)
  waiting for transfers between devices  25.5 us (40%)
  Pallas kernels  8.44 us (13%)
  other arithmetic  1.55 us (2%)
    ppermute x16, starting transfers between devices, permute(): return lax.ppermute(value, axes, pairs)  19.3 us
    ppermute x16, waiting for transfers between devices, permute(): return lax.ppermute(value, axes, pairs)  18.6 us
    all_to_all x1, starting transfers between devices, per_device(): lax.all_to_all(spread, Z, split_axis=0, concat_axis=0)  7.78 us
    all_to_all x1, waiting for transfers between devices, per_device(): lax.all_to_all(spread, Z, split_axis=0, concat_axis=0)  6.96 us
    pallas_call x1, Pallas kernels, attend_call(): pl.pallas_call(attend_kernel, out_shape=[shape(FAMILY, HALF)] * 4, in_spe...  3.2 us
    pallas_call x1, Pallas kernels, per_device(): pl.pallas_call(plan_kernel, out_shape=[shape(SLOTS + 8, 128, dtype=F32),...  2.94 us
  transfers between devices with their start and end apart: 17, of which 8 were waited for; matrix products, arithmetic and copies ran while one was open for 0% of the time, Pallas kernels for 12%

profile of v7, /device:TPU:6, one launch (start us, length us, event | category | flops | bytes accessed | tf_op | source)
XLA Modules:
  0.0 62.7 jit_solution(15924035512535631655)
XLA Ops:
  0.0 0.9 %maximum_bitcast_fusion.m0 = bf16[16,2560]{1,0:T(8,128)(2,1)S(1)} fusion(bf16[2,8,256]{2,1,0:T(8,128)(2,1)} %param.12, bf16[2,8,256]{2,1,0:T(8,128)(2,1)} %param.11, bf16[2,8,2048]{2,1,0:T(8,128)(2,1)} %param.8), kind=kLoop, calls=%fused_computation.1 | loop fusion | flops 245760 | bytes 163840 | tf_op jit(solution)/shard_map/reshape | solution.py:259
  0.9 2.0 %collective-permute-start.1 = (bf16[16,2560]{1,0:T(8,128)(2,1)S(1)}, bf16[16,2560]{1,0:T(8,128)(2,1)S(1)}, u32[]{:S(2)}, u32[]{:S(2)}) collective-permute-start(bf16[16,2560]{1,0:T(8,128)(2,1)S(1)} %maximum_bitcast_fusion.m0), channel_id=1, source_target_pairs={{0,8},{8,0},{1,9},{9,1},{2,10},{10,2},{3,11},{11,3},{4,12},{12,4},... | collective-permute-start | bytes 245768 | tf_op jit(solution)/shard_map/ppermute | solution.py:221
  2.9 2.9 %plan.1 = (f32[136,128]{1,0:T(8,128)S(1)}, f32[64,128]{1,0:T(8,128)S(1)}, s32[26]{0:T(128)S(1)}, bf16[8,2,512,128]{3,2,1,0:T(8,128)(2,1)S(1)}, bf16[8,2,512,128]...) custom-call(s32[2,512]{1,0:T(2,128)} %ancestors.1, s32[8]{0:T(128)} %lengths.1, bf16[8,2,512,128]{3,2,1,0:T(8,128)(2,1)} %key_ref.1, ...), custom_call_target="tpu_custom_call" | custom-call | flops 1000000 | bytes 100000 | tf_op jit(solution)/shard_map/plan/pallas_call | solution.py:262
  5.8 0.0 collective-permute-done.1.refs_0_
  5.9 0.6 collective-permute-start.2
  6.5 0.1 collective-permute-start.8
  6.6 0.8 %collective-permute-done.2.m3 = bf16[16,2560]{1,0:T(8,128)(2,1)S(1)} collective-permute-done((bf16[16,2560]{1,0:T(8,128)(2,1)S(1)}, bf16[16,2560]{1,0:T(8,128)(2,1)S(1)}, u32[]{:S(2)}, u32[]{:S(2)}) %collective-permute-start.2) | collective-permute-done | bytes 81952 | tf_op jit(solution)/shard_map/ppermute | solution.py:221
  7.4 3.2 %attend.1 = (bf16[32,1024]{1,0:T(8,128)(2,1)S(1)}, bf16[32,1024]{1,0:T(8,128)(2,1)S(1)}, bf16[32,1024]{1,0:T(8,128)(2,1)S(1)}, bf16[32,1024]{1,0:T(8,128)(2,1)S(1)}) custom-call(f32[136,128]{1,0:T(8,128)S(1)} %get-tuple-element.19.plan, f32[64,128]{1,0:T(8,128)S(1)} %get-tuple-element.20.refs_1_.back, s32[26]{0:T(128)S(1)} %get-tuple-element.21.chunks, ...), custom_call_target="tpu_custom_call" | custom-call | flops 7000000000 | bytes 1000000 | tf_op jit(solution)/shard_map/attend/pallas_call | solution.py:241
  10.6 0.1 collective-permute-start.3
  10.7 2.0 %collective-permute-start.4 = (bf16[32,1024]{1,0:T(8,128)(2,1)S(1)}, bf16[32,1024]{1,0:T(8,128)(2,1)S(1)}, u32[]{:S(2)}, u32[]{:S(2)}) collective-permute-start(bf16[32,1024]{1,0:T(8,128)(2,1)S(1)} %get-tuple-element.26), channel_id=1, source_target_pairs={{0,8},{8,0},{1,9},{9,1},{2,10},{10,2},{3,11},{11,3},{4,12},{12,4},... | collective-permute-start | bytes 196616 | tf_op jit(solution)/shard_map/ppermute | solution.py:221
  12.6 0.0 collective-permute-start.5
  12.7 1.6 %collective-permute-start.6 = (bf16[2048,128]{1,0:T(8,128)(2,1)S(1)}, bf16[2048,128]{1,0:T(8,128)(2,1)S(1)}, u32[]{:S(2)}, u32[]{:S(2)}) collective-permute-start(bf16[2048,128]{1,0:T(8,128)(2,1)S(1)} %copy-done), channel_id=1, source_target_pairs={{0,64},{4,196},{64,128},{68,4},{128,192},{132,68},{192,0},{196,132... | collective-permute-start | bytes 1572872 | tf_op jit(solution)/shard_map/ppermute | solution.py:221
  14.2 1.6 %collective-permute-start.9 = (bf16[2048,128]{1,0:T(8,128)(2,1)S(1)}, bf16[2048,128]{1,0:T(8,128)(2,1)S(1)}, u32[]{:S(2)}, u32[]{:S(2)}) collective-permute-start(bf16[2048,128]{1,0:T(8,128)(2,1)S(1)} %collective-permute-done.8), channel_id=1, source_target_pairs={{0,64},{4,196},{64,128},{68,4},{128,192},{132,68},{192,0},{196,132... | collective-permute-start | bytes 1572872 | tf_op jit(solution)/shard_map/ppermute | solution.py:221
  15.8 0.7 %collective-permute-done.4.c_ref = bf16[32,1024]{1,0:T(8,128)(2,1)S(1)} collective-permute-done((bf16[32,1024]{1,0:T(8,128)(2,1)S(1)}, bf16[32,1024]{1,0:T(8,128)(2,1)S(1)}, u32[]{:S(2)}, u32[]{:S(2)}) %collective-permute-start.4) | collective-permute-done | bytes 65568 | tf_op jit(solution)/shard_map/ppermute | solution.py:221
  16.5 0.0 collective-permute-done.5.d_ref
  16.5 0.8 %spread.1 = bf16[8,32,1024]{2,1,0:T(8,128)(2,1)} custom-call(bf16[32,1024]{1,0:T(8,128)(2,1)S(1)} %get-tuple-element.24.a_ref, bf16[32,1024]{1,0:T(8,128)(2,1)S(1)} %collective-permute-done.3.b_ref, bf16[32,1024]{1,0:T(8,128)(2,1)S(1)} %collective-permute-done.4.c_ref, bf16[32,1024]{1,0:T(8,128)(2,1)S(1)} %collective-permute-done.5.d_ref), custom_call_target="tpu_custom_call" | custom-call | flops 12000000000 | bytes 100000 | tf_op jit(solution)/shard_map/spread/pallas_call | solution.py:307
  17.3 7.8 %all-to-all-start = ((bf16[8,32,1024]{2,1,0:T(8,128)(2,1)}), bf16[8,32,1024]{2,1,0:T(8,128)(2,1)S(1)}, u32[]{:S(2)}, u32[]{:S(2)}) async-start(bf16[8,32,1024]{2,1,0:T(8,128)(2,1)} %spread.1), calls=%async_computation | async-start | bytes 1048576 | tf_op jit(solution)/shard_map/all_to_all | solution.py:316
  25.1 1.7 %collective-permute-start.7 = (bf16[2048,128]{1,0:T(8,128)(2,1)S(1)}, bf16[2048,128]{1,0:T(8,128)(2,1)S(1)}, u32[]{:S(2)}, u32[]{:S(2)}) collective-permute-start(bf16[2048,128]{1,0:T(8,128)(2,1)S(1)} %collective-permute-done.6.w1), channel_id=1, source_target_pairs={{0,64},{4,196},{64,128},{68,4},{128,192},{132,68},{192,0},{196,132... | collective-permute-start | bytes 1572872 | tf_op jit(solution)/shard_map/ppermute | solution.py:221
  26.8 1.9 %collective-permute-done.9 = bf16[2048,128]{1,0:T(8,128)(2,1)S(1)} collective-permute-done((bf16[2048,128]{1,0:T(8,128)(2,1)S(1)}, bf16[2048,128]{1,0:T(8,128)(2,1)S(1)}, u32[]{:S(2)}, u32[]{:S(2)}) %collective-permute-start.9) | collective-permute-done | bytes 524320 | tf_op jit(solution)/shard_map/ppermute | solution.py:221
  28.7 6.9 %collective-permute-done.7.refs_1_.w2 = bf16[2048,128]{1,0:T(8,128)(2,1)S(1)} collective-permute-done((bf16[2048,128]{1,0:T(8,128)(2,1)S(1)}, bf16[2048,128]{1,0:T(8,128)(2,1)S(1)}, u32[]{:S(2)}, u32[]{:S(2)}) %collective-permute-start.7) | collective-permute-done | bytes 524320 | tf_op jit(solution)/shard_map/ppermute | solution.py:221
  35.6 7.0 %all-to-all-done = bf16[8,32,1024]{2,1,0:T(8,128)(2,1)S(1)} async-done(((bf16[8,32,1024]{2,1,0:T(8,128)(2,1)}), bf16[8,32,1024]{2,1,0:T(8,128)(2,1)S(1)}, u32[]{:S(2)}, u32[]{:S(2)}) %all-to-all-start) | async-done | bytes 524320 | tf_op jit(solution)/shard_map/all_to_all | solution.py:316
  42.5 0.0 collective-permute-start.11
  42.6 0.7 %own_half.1.acc_ref = f32[4,256,128]{2,1,0:T(8,128)S(1)} custom-call(bf16[256,1024]{1,0:T(8,128)(2,1)S(1)} %hold.1.mine_ref, bf16[2048,128]{1,0:T(8,128)(2,1)S(1)} %get-tuple-element.28.w0, bf16[2048,128]{1,0:T(8,128)(2,1)S(1)} %collective-permute-done.6.w1, bf16[2048,128]{1,0:T(8,128)(2,1)S(1)} %collective-permute-done.7.refs_1_.w2, ...), custom_call_target="tpu_custom_call" | custom-call | flops 1000000000 | bytes 1000000 | tf_op jit(solution)/shard_map/own_half/pallas_call | solution.py:331
  43.3 1.2 %collective-permute-done.11.other_ref = bf16[256,1024]{1,0:T(8,128)(2,1)S(1)} collective-permute-done((bf16[256,1024]{1,0:T(8,128)(2,1)S(1)}, bf16[256,1024]{1,0:T(8,128)(2,1)S(1)}, u32[]{:S(2)}, u32[]{:S(2)}) %collective-permute-start.11) | collective-permute-done | bytes 524320 | tf_op jit(solution)/shard_map/ppermute | solution.py:221
  44.4 0.7 %other_half.1 = (bf16[2,128,128]{2,1,0:T(8,128)(2,1)S(1)}, bf16[2,128,128]{2,1,0:T(8,128)(2,1)S(1)}, bf16[2,128,128]{2,1,0:T(8,128)(2,1)S(1)}, bf16[2,128,128]{2,1,0:T(8,128)(2,1)S(1)}) custom-call(bf16[256,1024]{1,0:T(8,128)(2,1)S(1)} %collective-permute-done.11.other_ref, f32[4,256,128]{2,1,0:T(8,128)S(1)} %own_half.1.acc_ref, ...), custom_call_target="tpu_custom_call" | custom-call | flops 1000000000 | bytes 1000000 | tf_op jit(solution)/shard_map/other_half/pallas_call | solution.py:340
  45.2 1.6 %collective-permute-start.12 = (bf16[2,128,128]{2,1,0:T(8,128)(2,1)S(1)}, bf16[2,128,128]{2,1,0:T(8,128)(2,1)S(1)}, u32[]{:S(2)}, u32[]{:S(2)}) collective-permute-start(bf16[2,128,128]{2,1,0:T(8,128)(2,1)S(1)} %get-tuple-element.29), channel_id=1, source_target_pairs={{0,128},{1,192},{2,0},{3,64},{64,129},{65,193},{66,1},{67,65},{128... | collective-permute-start | bytes 196616 | tf_op jit(solution)/shard_map/ppermute | solution.py:221
  46.8 2.2 %collective-permute-start.13 = (bf16[2,128,128]{2,1,0:T(8,128)(2,1)S(1)}, bf16[2,128,128]{2,1,0:T(8,128)(2,1)S(1)}, u32[]{:S(2)}, u32[]{:S(2)}) collective-permute-start(bf16[2,128,128]{2,1,0:T(8,128)(2,1)S(1)} %get-tuple-element.30), channel_id=1, source_target_pairs={{0,64},{1,128},{2,192},{3,0},{64,65},{65,129},{66,193},{67,1},{128... | collective-permute-start | bytes 196616 | tf_op jit(solution)/shard_map/ppermute | solution.py:221
  48.9 2.8 %collective-permute-start.14 = (bf16[2,128,128]{2,1,0:T(8,128)(2,1)S(1)}, bf16[2,128,128]{2,1,0:T(8,128)(2,1)S(1)}, u32[]{:S(2)}, u32[]{:S(2)}) collective-permute-start(bf16[2,128,128]{2,1,0:T(8,128)(2,1)S(1)} %get-tuple-element.31), channel_id=1, source_target_pairs={{0,192},{1,0},{2,64},{3,128},{64,193},{65,1},{66,65},{67,129},{128... | collective-permute-start | bytes 196616 | tf_op jit(solution)/shard_map/ppermute | solution.py:221
  51.7 3.2 %collective-permute-start.15 = (bf16[2,128,128]{2,1,0:T(8,128)(2,1)S(1)}, bf16[2,128,128]{2,1,0:T(8,128)(2,1)S(1)}, u32[]{:S(2)}, u32[]{:S(2)}) collective-permute-start(bf16[2,128,128]{2,1,0:T(8,128)(2,1)S(1)} %get-tuple-element.32), channel_id=1, source_target_pairs={{0,0},{1,64},{2,128},{3,192},{64,1},{65,65},{66,129},{67,193},{128... | collective-permute-start | bytes 196616 | tf_op jit(solution)/shard_map/ppermute | solution.py:221
  55.0 1.9 %collective-permute-done.14 = bf16[2,128,128]{2,1,0:T(8,128)(2,1)S(1)} collective-permute-done((bf16[2,128,128]{2,1,0:T(8,128)(2,1)S(1)}, bf16[2,128,128]{2,1,0:T(8,128)(2,1)S(1)}, u32[]{:S(2)}, u32[]{:S(2)}) %collective-permute-start.14) | collective-permute-done | bytes 65568 | tf_op jit(solution)/shard_map/ppermute | solution.py:221
  56.8 5.2 %collective-permute-done.15 = bf16[2,128,128]{2,1,0:T(8,128)(2,1)S(1)} collective-permute-done((bf16[2,128,128]{2,1,0:T(8,128)(2,1)S(1)}, bf16[2,128,128]{2,1,0:T(8,128)(2,1)S(1)}, u32[]{:S(2)}, u32[]{:S(2)}) %collective-permute-start.15) | collective-permute-done | bytes 65568 | tf_op jit(solution)/shard_map/ppermute | solution.py:221
  62.1 0.7 %add_convert_fusion = bf16[2,128,128]{2,1,0:T(8,128)(2,1)} fusion(bf16[2,128,128]{2,1,0:T(8,128)(2,1)S(1)} %collective-permute-done.15, bf16[2,128,128]{2,1,0:T(8,128)(2,1)S(1)} %collective-permute-done.14, bf16[2,128,128]{2,1,0:T(8,128)(2,1)S(1)} %collective-permute-done.13, bf16[2,128,128]{2,1,0:T(8,128)(2,1)S(1)} %collective-permute-done.12), kind=kLoop, calls=%fused_computation | loop fusion | flops 262144 | bytes 327680 | tf_op jit(solution)/shard_map/convert_element_type | solution.py:353
  (13 shorter events, 0.0 us)
Async XLA Ops:
  0.9 5.6 %copy-start = (bf16[2048,128]{1,0:T(8,128)(2,1)S(1)}, bf16[2048,128]{1,0:T(8,128)(2,1)}, u32[]{:S(2)}) copy-start(bf16[2048,128]{1,0:T(8,128)(2,1)} %w_ref.1) | copy-start | bytes 1572868
  0.9 5.0 %collective-permute-start.1 = (bf16[16,2560]{1,0:T(8,128)(2,1)S(1)}, bf16[16,2560]{1,0:T(8,128)(2,1)S(1)}, u32[]{:S(2)}, u32[]{:S(2)}) collective-permute-start(bf16[16,2560]{1,0:T(8,128)(2,1)S(1)} %maximum_bitcast_fusion.m0), channel_id=1, source_target_pairs={{0,8},{8,0},{1,9},{9,1},{2,10},{10,2},{3,11},{11,3},{4,12},{12,4},... | collective-permute-start | bytes 245768 | tf_op jit(solution)/shard_map/ppermute | solution.py:221
  2.9 3.7 %collective-permute-start = (bf16[16,2560]{1,0:T(8,128)(2,1)S(1)}, bf16[16,2560]{1,0:T(8,128)(2,1)S(1)}, u32[]{:S(2)}, u32[]{:S(2)}) collective-permute-start(bf16[16,2560]{1,0:T(8,128)(2,1)S(1)} %maximum_bitcast_fusion.m0), channel_id=1, source_target_pairs={{0,4},{4,0},{1,5},{5,1},{2,6},{6,2},{3,7},{7,3},{8,12},{12,8},{9,1... | collective-permute-start | bytes 245768 | tf_op jit(solution)/shard_map/ppermute | solution.py:221
  5.9 1.5 %collective-permute-start.2 = (bf16[16,2560]{1,0:T(8,128)(2,1)S(1)}, bf16[16,2560]{1,0:T(8,128)(2,1)S(1)}, u32[]{:S(2)}, u32[]{:S(2)}) collective-permute-start(bf16[16,2560]{1,0:T(8,128)(2,1)S(1)} %relay.1.m2), channel_id=1, source_target_pairs={{0,4},{4,0},{1,5},{5,1},{2,6},{6,2},{3,7},{7,3},{8,12},{12,8},{9,1... | collective-permute-start | bytes 245768 | tf_op jit(solution)/shard_map/ppermute | solution.py:221
  6.5 7.8 %collective-permute-start.8 = (bf16[2048,128]{1,0:T(8,128)(2,1)S(1)}, bf16[2048,128]{1,0:T(8,128)(2,1)S(1)}, u32[]{:S(2)}, u32[]{:S(2)}) collective-permute-start(bf16[2048,128]{1,0:T(8,128)(2,1)S(1)} %copy-done), channel_id=1, source_target_pairs={{0,4},{4,0},{1,5},{5,1},{2,6},{6,2},{3,7},{7,3},{8,12},{12,8},{9,1... | collective-permute-start | bytes 1572872 | tf_op jit(solution)/shard_map/ppermute | solution.py:221
  10.6 5.2 %collective-permute-start.3 = (bf16[32,1024]{1,0:T(8,128)(2,1)S(1)}, bf16[32,1024]{1,0:T(8,128)(2,1)S(1)}, u32[]{:S(2)}, u32[]{:S(2)}) collective-permute-start(bf16[32,1024]{1,0:T(8,128)(2,1)S(1)} %get-tuple-element.25), channel_id=1, source_target_pairs={{0,12},{4,8},{8,4},{12,0},{1,13},{5,9},{9,5},{13,1},{2,14},{6,10},... | collective-permute-start | bytes 196616 | tf_op jit(solution)/shard_map/ppermute | solution.py:221
  10.7 5.8 %collective-permute-start.4 = (bf16[32,1024]{1,0:T(8,128)(2,1)S(1)}, bf16[32,1024]{1,0:T(8,128)(2,1)S(1)}, u32[]{:S(2)}, u32[]{:S(2)}) collective-permute-start(bf16[32,1024]{1,0:T(8,128)(2,1)S(1)} %get-tuple-element.26), channel_id=1, source_target_pairs={{0,8},{8,0},{1,9},{9,1},{2,10},{10,2},{3,11},{11,3},{4,12},{12,4},... | collective-permute-start | bytes 196616 | tf_op jit(solution)/shard_map/ppermute | solution.py:221
  12.6 3.8 %collective-permute-start.5 = (bf16[32,1024]{1,0:T(8,128)(2,1)S(1)}, bf16[32,1024]{1,0:T(8,128)(2,1)S(1)}, u32[]{:S(2)}, u32[]{:S(2)}) collective-permute-start(bf16[32,1024]{1,0:T(8,128)(2,1)S(1)} %get-tuple-element.27), channel_id=1, source_target_pairs={{0,4},{4,0},{1,5},{5,1},{2,6},{6,2},{3,7},{7,3},{8,12},{12,8},{9,1... | collective-permute-start | bytes 196616 | tf_op jit(solution)/shard_map/ppermute | solution.py:221
  12.7 12.4 %collective-permute-start.6 = (bf16[2048,128]{1,0:T(8,128)(2,1)S(1)}, bf16[2048,128]{1,0:T(8,128)(2,1)S(1)}, u32[]{:S(2)}, u32[]{:S(2)}) collective-permute-start(bf16[2048,128]{1,0:T(8,128)(2,1)S(1)} %copy-done), channel_id=1, source_target_pairs={{0,64},{4,196},{64,128},{68,4},{128,192},{132,68},{192,0},{196,132... | collective-permute-start | bytes 1572872 | tf_op jit(solution)/shard_map/ppermute | solution.py:221
  14.2 14.4 %collective-permute-start.9 = (bf16[2048,128]{1,0:T(8,128)(2,1)S(1)}, bf16[2048,128]{1,0:T(8,128)(2,1)S(1)}, u32[]{:S(2)}, u32[]{:S(2)}) collective-permute-start(bf16[2048,128]{1,0:T(8,128)(2,1)S(1)} %collective-permute-done.8), channel_id=1, source_target_pairs={{0,64},{4,196},{64,128},{68,4},{128,192},{132,68},{192,0},{196,132... | collective-permute-start | bytes 1572872 | tf_op jit(solution)/shard_map/ppermute | solution.py:221
  17.3 25.2 %all-to-all-start = ((bf16[8,32,1024]{2,1,0:T(8,128)(2,1)}), bf16[8,32,1024]{2,1,0:T(8,128)(2,1)S(1)}, u32[]{:S(2)}, u32[]{:S(2)}) async-start(bf16[8,32,1024]{2,1,0:T(8,128)(2,1)} %spread.1), calls=%async_computation | async-start | bytes 1048576 | tf_op jit(solution)/shard_map/all_to_all | solution.py:316
  25.1 10.5 %collective-permute-start.7 = (bf16[2048,128]{1,0:T(8,128)(2,1)S(1)}, bf16[2048,128]{1,0:T(8,128)(2,1)S(1)}, u32[]{:S(2)}, u32[]{:S(2)}) collective-permute-start(bf16[2048,128]{1,0:T(8,128)(2,1)S(1)} %collective-permute-done.6.w1), channel_id=1, source_target_pairs={{0,64},{4,196},{64,128},{68,4},{128,192},{132,68},{192,0},{196,132... | collective-permute-start | bytes 1572872 | tf_op jit(solution)/shard_map/ppermute | solution.py:221
  28.7 13.9 %collective-permute-start.10 = (bf16[2048,128]{1,0:T(8,128)(2,1)S(1)}, bf16[2048,128]{1,0:T(8,128)(2,1)S(1)}, u32[]{:S(2)}, u32[]{:S(2)}) collective-permute-start(bf16[2048,128]{1,0:T(8,128)(2,1)S(1)} %collective-permute-done.9), channel_id=1, source_target_pairs={{0,4},{4,0},{1,5},{5,1},{2,6},{6,2},{3,7},{7,3},{8,12},{12,8},{9,1... | collective-permute-start | bytes 1572872 | tf_op jit(solution)/shard_map/ppermute | solution.py:221
  42.5 1.9 %collective-permute-start.11 = (bf16[256,1024]{1,0:T(8,128)(2,1)S(1)}, bf16[256,1024]{1,0:T(8,128)(2,1)S(1)}, u32[]{:S(2)}, u32[]{:S(2)}) collective-permute-start(bf16[256,1024]{1,0:T(8,128)(2,1)S(1)} %hold.1.mine_ref), channel_id=1, source_target_pairs={{0,4},{4,0},{1,5},{5,1},{2,6},{6,2},{3,7},{7,3},{8,12},{12,8},{9,1... | collective-permute-start | bytes 1572872 | tf_op jit(solution)/shard_map/ppermute | solution.py:221
  45.2 9.8 %collective-permute-start.12 = (bf16[2,128,128]{2,1,0:T(8,128)(2,1)S(1)}, bf16[2,128,128]{2,1,0:T(8,128)(2,1)S(1)}, u32[]{:S(2)}, u32[]{:S(2)}) collective-permute-start(bf16[2,128,128]{2,1,0:T(8,128)(2,1)S(1)} %get-tuple-element.29), channel_id=1, source_target_pairs={{0,128},{1,192},{2,0},{3,64},{64,129},{65,193},{66,1},{67,65},{128... | collective-permute-start | bytes 196616 | tf_op jit(solution)/shard_map/ppermute | solution.py:221
  46.8 8.2 %collective-permute-start.13 = (bf16[2,128,128]{2,1,0:T(8,128)(2,1)S(1)}, bf16[2,128,128]{2,1,0:T(8,128)(2,1)S(1)}, u32[]{:S(2)}, u32[]{:S(2)}) collective-permute-start(bf16[2,128,128]{2,1,0:T(8,128)(2,1)S(1)} %get-tuple-element.30), channel_id=1, source_target_pairs={{0,64},{1,128},{2,192},{3,0},{64,65},{65,129},{66,193},{67,1},{128... | collective-permute-start | bytes 196616 | tf_op jit(solution)/shard_map/ppermute | solution.py:221
  48.9 7.9 %collective-permute-start.14 = (bf16[2,128,128]{2,1,0:T(8,128)(2,1)S(1)}, bf16[2,128,128]{2,1,0:T(8,128)(2,1)S(1)}, u32[]{:S(2)}, u32[]{:S(2)}) collective-permute-start(bf16[2,128,128]{2,1,0:T(8,128)(2,1)S(1)} %get-tuple-element.31), channel_id=1, source_target_pairs={{0,192},{1,0},{2,64},{3,128},{64,193},{65,1},{66,65},{67,129},{128... | collective-permute-start | bytes 196616 | tf_op jit(solution)/shard_map/ppermute | solution.py:221
  51.7 10.3 %collective-permute-start.15 = (bf16[2,128,128]{2,1,0:T(8,128)(2,1)S(1)}, bf16[2,128,128]{2,1,0:T(8,128)(2,1)S(1)}, u32[]{:S(2)}, u32[]{:S(2)}) collective-permute-start(bf16[2,128,128]{2,1,0:T(8,128)(2,1)S(1)} %get-tuple-element.32), channel_id=1, source_target_pairs={{0,0},{1,64},{2,128},{3,192},{64,1},{65,65},{66,129},{67,193},{128... | collective-permute-start | bytes 196616 | tf_op jit(solution)/shard_map/ppermute | solution.py:221
